TPU v7x, 32 devices: a whole 2x2x4 slice. The times are simulated.
32 devices in a mesh: seq: 8 (over z, y), head: 4 (over x, core).
Axes of the slice: x: 2, y: 2, z: 4, core: 2. Of those that a mesh axis runs over, the one named last changes fastest.
Arguments:
- queries: bfloat16 [4096, 2048], P('seq', 'head'), may hold values from -5 to 5
- keys: bfloat16 [4096, 2048], P('seq', 'head'), may hold values from -5 to 5
- values: bfloat16 [4096, 2048], P('seq', 'head'), may hold values from -5 to 5
- out_weight: bfloat16 [2048, 2048], P('head'), may hold values from -0.125 to 0.125
- out_grad: bfloat16 [4096, 2048], P('seq'), may hold values from -5 to 5
- global_pos: int32 [256], replicated, may hold values from 0 to 511, as said below
- block_mask: int32 [32, 4], P('seq'), may hold values 0 or 1
Outputs:
- layer_out: bfloat16 [4096, 2048], P('seq', 'head')
- grad_queries: bfloat16 [4096, 2048], P('seq', 'head')
- grad_keys: bfloat16 [4096, 2048], P('seq', 'head')
- grad_values: bfloat16 [4096, 2048], P('seq', 'head')
Inputs may be any that keep to these rules, and one draw needn't show every extreme that they name: `global_pos`: 256 distinct positions among the first 512 tokens.
All inputs are finite; a program needn't handle non-finite values. No bound on the sum of `block_mask` on one device may be relied on, other than what follows from the above.
Results may differ from a plain program's by a relative error of at most 0.012.
Values may be sent and summed in bfloat16 or wider, within the bound.
No kernel may reach another device: no remote copies, remote signals or barrier semaphores. Data moves between devices by JAX's collectives and lax.ppermute only.
A program may use at most 192 MiB of HBM per device.

v0:
```python
import math

import jax
import jax.numpy as jnp
from jax import lax
from jax.experimental import pallas as pl
from jax.experimental.pallas import tpu as pltpu
from jax.sharding import PartitionSpec as P

HEAD_DIM = 128
BLOCK = 128
WBLK = 4
RIM = (WBLK - 1) * BLOCK
QROWS = 2 * BLOCK
SCALE = 1.0 / math.sqrt(HEAD_DIM)
SCALE2 = SCALE * math.log2(math.e)
BF = jnp.bfloat16
F32 = jnp.float32
NEG = float("-inf")


def nn(a, b):
    return lax.dot_general(a, b, (((1,), (0,)), ((), ())), preferred_element_type=F32)


def nt(a, b):
    return lax.dot_general(a, b, (((1,), (1,)), ((), ())), preferred_element_type=F32)


def tn(a, b):
    return lax.dot_general(a, b, (((0,), (0,)), ((), ())), preferred_element_type=F32)


def rows(slot, count):
    return pl.ds(pl.multiple_of(slot * count, count), count)


def local_call(name, body, ids, arrays, outs, scratch=(), flops=0):
    moved = sum(a.size * a.dtype.itemsize for a in arrays)
    moved += sum(math.prod(s) * jnp.dtype(t).itemsize for s, t in outs)
    return pl.pallas_call(
        body,
        name=name,
        out_shape=tuple(jax.ShapeDtypeStruct(s, t) for s, t in outs),
        in_specs=[pl.BlockSpec(memory_space=pltpu.SMEM)]
        + [pl.BlockSpec(memory_space=pltpu.VMEM)] * len(arrays),
        out_specs=tuple(pl.BlockSpec(memory_space=pltpu.VMEM) for _ in outs),
        scratch_shapes=list(scratch),
        compiler_params=pltpu.CompilerParams(vmem_limit_bytes=40 * 2**20),
        cost_estimate=pl.CostEstimate(flops=flops, bytes_accessed=moved, transcendentals=0),
    )(ids, *arrays)


def pack_kv_body(ids, k, v, mask, *outs):
    tok = k.shape[0]
    for i, out in enumerate(outs):
        col = rows(ids[0] ^ i, HEAD_DIM)
        out[0:tok, :] = k[:, col]
        out[tok : 2 * tok, :] = v[:, col]
        out[2 * tok :, :] = mask[...]


def pack_qo_body(ids, q, out_grad, out_weight, *refs):
    outs, d_attn = refs[:-1], refs[-1]
    tok = q.shape[0]
    d_attn[...] = nt(out_grad[...], out_weight[...]).astype(BF)
    for i, out in enumerate(outs):
        col = rows(ids[0] ^ i, HEAD_DIM)
        out[0:tok, :] = q[:, col]
        out[tok:, :] = d_attn[:, col]


def pick_rows(pos_col, tok):
    hits = pos_col == lax.broadcasted_iota(jnp.int32, (pos_col.shape[0], tok), 1)
    return hits.astype(BF)


def place_rows(pos_row, tok):
    return lax.broadcasted_iota(jnp.int32, (tok, pos_row.shape[1]), 0) == pos_row


def join_kv_body(ids, pos_col, *refs):
    pieces, (k, v, bias, picked, rim) = refs[:-5], refs[-5:]
    tok = k.shape[0] // len(pieces)
    n_rows = bias.shape[0] // len(pieces)
    for i, piece in enumerate(pieces):
        slot = ids[0] ^ i
        k[rows(slot, tok), :] = piece[0:tok, :]
        v[rows(slot, tok), :] = piece[tok : 2 * tok, :]
        open_ = piece[2 * tok :, :].astype(F32)
        entry = lax.broadcasted_iota(jnp.int32, open_.shape, 0) + slot * n_rows
        inside = (ids[1] > 0) | (entry // WBLK >= entry % WBLK)
        bias[rows(slot, n_rows), :] = jnp.where((open_ > 0.5) & inside, 0.0, NEG)
    picks = pick_rows(pos_col[...], tok)
    n = pos_col.shape[0]
    picked[0:n, :] = nn(picks, k[0:tok, :]).astype(BF)
    picked[n:, :] = nn(picks, v[0:tok, :]).astype(BF)
    rim[0:RIM, :] = k[k.shape[0] - RIM :, :]
    rim[RIM:, :] = v[k.shape[0] - RIM :, :]


def join_qo_body(ids, pos_col, pos_row, *refs):
    pieces, (q, d_attn, picked) = refs[:-3], refs[-3:]
    tok = q.shape[0] // len(pieces)
    for i, piece in enumerate(pieces):
        slot = ids[0] ^ i
        q[rows(slot, tok), :] = piece[0:tok, :]
        d_attn[rows(slot, tok), :] = piece[tok:, :]
    picks = pick_rows(pos_col[...], tok)
    n = pos_col.shape[0]
    picked[0:n, :] = nn(picks, q[0:tok, :]).astype(BF)
    picked[n:, :] = nn(picks, d_attn[0:tok, :]).astype(BF)

    @pl.when(ids[1] == 0)
    def _():
        hit = place_rows(pos_row[...], tok).astype(F32)
        is_row = jnp.max(hit, axis=1, keepdims=True) > 0.5
        kept = jnp.where(is_row, 0.0, d_attn[0:tok, :].astype(F32))
        d_attn[0:tok, :] = kept.astype(BF)


def row_forward_body(ids, qo, k, v, attn_t, stats, scores):
    n = qo.shape[0] // 2
    step = 512
    query, d_out = qo[0:n, :], qo[n:, :]
    peak = None
    for c in range(0, k.shape[0], step):
        s = nt(k[c : c + step, :], query) * SCALE2
        scores[c : c + step, :] = s
        top = jnp.max(s, axis=0, keepdims=True)
        peak = top if peak is None else jnp.maximum(peak, top)
    mass = jnp.zeros((1, n), F32)
    dot = jnp.zeros((1, n), F32)
    numer = jnp.zeros((HEAD_DIM, n), F32)
    for c in range(0, k.shape[0], step):
        e = jnp.exp2(scores[c : c + step, :] - peak)
        vals = v[c : c + step, :]
        mass = mass + jnp.sum(e, axis=0, keepdims=True)
        dot = dot + jnp.sum(e * nt(vals, d_out), axis=0, keepdims=True)
        numer = numer + tn(vals, e.astype(BF))
    attn_t[...] = (numer / mass).astype(BF)
    stats[...] = jnp.concatenate([peak, mass, dot, jnp.zeros((5, n), F32)], axis=0)


def merged(mine, other):
    peak = jnp.maximum(mine[0:1, :], other[0:1, :])
    wa = jnp.exp2(mine[0:1, :] - peak)
    wb = jnp.exp2(other[0:1, :] - peak)
    mass = mine[1:2, :] * wa + other[1:2, :] * wb
    dot = mine[2:3, :] * wa + other[2:3, :] * wb
    return peak, mass, dot, mine[1:2, :] * wa / mass, other[1:2, :] * wb / mass


def window_body(ids, pos_row, q, d_out, k, v, rim, kv_glob, bias, *refs):
    attn, dq, dk, dv, rim_back, dk_glob, dv_glob, kx, vx, kt, vt, key_bias = refs
    n = kv_glob.shape[0] // 2
    total = k.shape[0]
    tok = total // 4
    kx[0:RIM, :] = rim[0:RIM, :]
    kx[RIM:, :] = k[...]
    vx[0:RIM, :] = rim[RIM:, :]
    vx[RIM:, :] = v[...]
    kt[...] = kx[...].T
    vt[...] = vx[...].T
    dk[...] = jnp.zeros_like(dk)
    dv[...] = jnp.zeros_like(dv)
    dk_glob[...] = jnp.zeros_like(dk_glob)
    dv_glob[...] = jnp.zeros_like(dv_glob)
    key_bias[...] = jnp.zeros_like(key_bias)

    @pl.when(ids[1] == 0)
    def _():
        hit = place_rows(pos_row[...], tok).astype(F32)
        is_row = jnp.max(hit, axis=1, keepdims=True) > 0.5
        key_bias[RIM : RIM + tok, :] = jnp.where(is_row, NEG, jnp.zeros((tok, QROWS), F32))

    kg, vg = kv_glob[0:n, :], kv_glob[n:, :]
    kgt, vgt = kg.T, vg.T
    key_in = lax.broadcasted_iota(jnp.int32, (BLOCK, QROWS), 0)
    query_in = lax.broadcasted_iota(jnp.int32, (BLOCK, QROWS), 1)
    n_keys = RIM + QROWS
    shut = jnp.full((1, BLOCK), NEG, F32)

    def step(sb, carry):
        here = rows(sb, QROWS)
        span = pl.ds(pl.multiple_of(sb * QROWS, QROWS), n_keys)
        qb, dob = q[here, :], d_out[here, :]
        kw, vw = kx[span, :], vx[span, :]
        raw = nt(kw, qb)
        parts = []
        for kb in range(n_keys // BLOCK):
            halves = []
            for half in range(QROWS // BLOCK):
                r = half + WBLK - 1 - kb
                if 0 <= r < WBLK:
                    at = (sb * (QROWS // BLOCK) + half) * WBLK + r
                    halves.append(bias[pl.ds(at, 1), :])
                else:
                    halves.append(shut)
            part = (
                raw[kb * BLOCK : (kb + 1) * BLOCK, :] * SCALE2
                + key_bias[pl.ds(pl.multiple_of(sb * QROWS + kb * BLOCK, BLOCK), BLOCK), :]
                + jnp.concatenate(halves, axis=1)
            )
            own = kb - (WBLK - 1)
            if own >= 0:
                part = jnp.where(query_in - key_in >= own * BLOCK, part, NEG) if own else jnp.where(
                    key_in <= query_in, part, NEG
                )
            parts.append(part)
        tw = jnp.concatenate(parts, axis=0)
        tg = nt(kg, qb) * SCALE2
        peak = jnp.maximum(
            jnp.max(tw, axis=0, keepdims=True), jnp.max(tg, axis=0, keepdims=True)
        )
        ew, eg = jnp.exp2(tw - peak), jnp.exp2(tg - peak)
        mass = jnp.sum(ew, axis=0, keepdims=True) + jnp.sum(eg, axis=0, keepdims=True)
        inv = 1.0 / mass
        pw, pg = ew * inv, eg * inv
        ww, wg = pw.astype(BF), pg.astype(BF)
        out_t = (nn(vt[:, span], ww) + nn(vgt, wg)).astype(BF).astype(F32)
        attn[here, :] = out_t.T.astype(BF)
        delta = jnp.sum(out_t * dob.astype(F32).T, axis=0, keepdims=True)
        dw = (pw * (nt(vw, dob) - delta)).astype(BF)
        dg = (pg * (nt(vg, dob) - delta)).astype(BF)
        dq_t = nn(kt[:, span], dw) + nn(kgt, dg)
        dq[here, :] = (dq_t.T * SCALE).astype(BF)
        dk[span, :] += nn(dw, qb)
        dv[span, :] += nn(ww, dob)
        dk_glob[...] += nn(dg, qb)
        dv_glob[...] += nn(wg, dob)
        return carry

    lax.fori_loop(0, total // QROWS, step, 0)
    rim_back[0:RIM, :] = dk[0:RIM, :].astype(BF)
    rim_back[RIM:, :] = dv[0:RIM, :].astype(BF)


def row_backward_body(ids, qo, k, v, stats, other, dkw, dvw, dkg, dvg, dk, dv, sums):
    n = qo.shape[0] // 2
    step = 512
    query, d_out = qo[0:n, :], qo[n:, :]
    peak, mass, dot, _, _ = merged(stats[...], other[...])
    lse = peak + jnp.log2(mass)
    delta = dot / mass
    dq_t = jnp.zeros((HEAD_DIM, n), F32)
    for c in range(0, k.shape[0], step):
        keys, vals = k[c : c + step, :], v[c : c + step, :]
        prob = jnp.exp2(nt(keys, query) * SCALE2 - lse)
        ds = (prob * (nt(vals, d_out) - delta)).astype(BF)
        dk[c : c + step, :] = dkw[RIM + c : RIM + c + step, :] + nn(ds, query)
        dv[c : c + step, :] = dvw[RIM + c : RIM + c + step, :] + nn(prob.astype(BF), d_out)
        dq_t = dq_t + tn(keys, ds)
    sums[0:n, :] = dq_t.T.astype(BF)
    sums[n : 2 * n, :] = dkg[...].astype(BF)
    sums[2 * n :, :] = dvg[...].astype(BF)


def pack_attn_body(ids, pos_row, attn, mine_t, other_t, stats, other, *refs):
    outs, full = refs[:-1], refs[-1]
    tok = attn.shape[0] // len(outs)
    full[...] = attn[...]

    @pl.when(ids[1] == 0)
    def _():
        _, _, _, wa, wb = merged(stats[...], other[...])
        both_t = (mine_t[...].astype(F32) * wa + other_t[...].astype(F32) * wb).astype(BF)
        hit = place_rows(pos_row[...], tok)
        is_row = jnp.max(hit.astype(F32), axis=1, keepdims=True) > 0.5
        placed = nt(hit.astype(BF), both_t)
        full[0:tok, :] = jnp.where(is_row, placed, attn[0:tok, :].astype(F32)).astype(BF)

    for i, out in enumerate(outs):
        out[...] = full[rows(ids[0] ^ i, tok), :]


def project_body(ids, w, *refs):
    pieces, (keep, send, attn) = refs[:-3], refs[-3:]
    for i, piece in enumerate(pieces):
        attn[:, rows(ids[0] ^ i, HEAD_DIM)] = piece[...]
    cols = keep.shape[2]
    a = attn[...]
    me = ids[2]
    for i, group in enumerate((me, me ^ 2)):
        keep[i] = nn(a, w[:, rows(group, cols)]).astype(BF)
    for i, group in enumerate((me ^ 1, me ^ 3)):
        send[i] = nn(a, w[:, rows(group, cols)]).astype(BF)


def pack_grads_body(ids, pos_row, dq, dk, dv, rim_back, sums, other, *refs):
    outs, (dqf, dkf, dvf) = refs[:-3], refs[-3:]
    total = dq.shape[0]
    tok = total // len(outs)
    n = sums.shape[0] // 3
    dqf[...] = dq[...]
    dkf[...] = dk[...]
    dvf[...] = dv[...]
    dkf[total - RIM :, :] += rim_back[0:RIM, :].astype(F32)
    dvf[total - RIM :, :] += rim_back[RIM:, :].astype(F32)

    @pl.when(ids[1] == 0)
    def _():
        both = sums[...].astype(F32) + other[...].astype(F32)
        hit = place_rows(pos_row[...], tok).astype(BF)
        dq_add = nn(hit, (both[0:n, :] * SCALE).astype(BF))
        dqf[0:tok, :] = (dqf[0:tok, :].astype(F32) + dq_add).astype(BF)
        dkf[0:tok, :] += nn(hit, both[n : 2 * n, :].astype(BF))
        dvf[0:tok, :] += nn(hit, both[2 * n :, :].astype(BF))

    for i, out in enumerate(outs):
        here = rows(ids[0] ^ i, tok)
        out[0:tok, :] = dqf[here, :]
        out[tok : 2 * tok, :] = (dkf[here, :] * SCALE).astype(BF)
        out[2 * tok :, :] = dvf[here, :].astype(BF)


def join_grads_body(ids, *refs):
    pieces, outs = refs[:-3], refs[-3:]
    tok = outs[0].shape[0]
    for i, piece in enumerate(pieces):
        col = rows(ids[0] ^ i, HEAD_DIM)
        for at, out in enumerate(outs):
            out[:, col] = piece[at * tok : (at + 1) * tok, :]


def on_device(queries, keys, values, out_weight, out_grad, global_pos, block_mask):
    tok, cols = queries.shape
    heads = cols // HEAD_DIM
    n_seq = lax.axis_size("seq")
    n_groups = n_seq // heads
    total = heads * tok
    n_glob = global_pos.shape[0]
    seq_index = lax.axis_index("seq")
    group = seq_index // heads
    ids = jnp.stack([seq_index % heads, group, lax.axis_index("head")]).astype(jnp.int32)
    pos_col = global_pos.reshape(n_glob, 1)
    pos_row = global_pos.reshape(1, n_glob)

    def swap_in_group(pieces):
        moved = [
            lax.ppermute(piece, "seq", [(s, s ^ i) for s in range(n_seq)])
            for i, piece in enumerate(pieces)
            if i
        ]
        return [pieces[0]] + moved

    def from_first(x):
        d = 1
        while d < n_groups:
            route = [
                (g * heads + j, (g + d) * heads + j)
                for g in range(d)
                for j in range(heads)
                if g + d < n_groups
            ]
            x = jnp.where((group >= d) & (group < 2 * d), lax.ppermute(x, "seq", route), x)
            d *= 2
        return x

    def to_next_group(x, step):
        route = [(s, s + step * heads) for s in range(n_seq) if 0 <= s + step * heads < n_seq]
        return lax.ppermute(x, "seq", route)

    def with_group(x, d):
        return lax.ppermute(x, "seq", [(s, s ^ (d * heads)) for s in range(n_seq)])

    mask_rows = jnp.broadcast_to(
        block_mask.reshape(-1, 1).astype(BF), (block_mask.size, HEAD_DIM)
    )
    kv_rows = 2 * tok + block_mask.size
    kv = swap_in_group(
        local_call(
            "pack_kv", pack_kv_body, ids, (keys, values, mask_rows), [((kv_rows, HEAD_DIM), BF)] * heads
        )
    )
    qo = swap_in_group(
        local_call(
            "pack_qo",
            pack_qo_body,
            ids,
            (queries, out_grad, out_weight),
            [((2 * tok, HEAD_DIM), BF)] * heads,
            [pltpu.VMEM((tok, cols), BF)],
            flops=2 * tok * cols * out_weight.shape[1],
        )
    )
    k, v, bias, kv_pick, rim_out = local_call(
        "join_kv",
        join_kv_body,
        ids,
        (pos_col, *kv),
        [
            ((total, HEAD_DIM), BF),
            ((total, HEAD_DIM), BF),
            ((heads * block_mask.size, HEAD_DIM), F32),
            ((2 * n_glob, HEAD_DIM), BF),
            ((2 * RIM, HEAD_DIM), BF),
        ],
    )
    rim = to_next_group(rim_out, 1)
    kv_glob = from_first(kv_pick)
    q, d_attn, qo_pick = local_call(
        "join_qo",
        join_qo_body,
        ids,
        (pos_col, pos_row, *qo),
        [
            ((total, HEAD_DIM), BF),
            ((total, HEAD_DIM), BF),
            ((2 * n_glob, HEAD_DIM), BF),
        ],
    )
    qo_glob = from_first(qo_pick)
    row_flops = 2 * n_glob * total * HEAD_DIM
    attn_t, stats = local_call(
        "row_forward",
        row_forward_body,
        ids,
        (qo_glob, k, v),
        [((HEAD_DIM, n_glob), BF), ((8, n_glob), F32)],
        [pltpu.VMEM((total, n_glob), F32)],
        flops=3 * row_flops,
    )
    d = 1
    while 2 * d < n_groups:
        other_t, other = with_group(attn_t, d), with_group(stats, d)
        peak, mass, dot, wa, wb = merged(stats, other)
        attn_t = (attn_t.astype(F32) * wa + other_t.astype(F32) * wb).astype(BF)
        stats = jnp.concatenate([peak, mass, dot, jnp.zeros((5, n_glob), F32)], axis=0)
        d *= 2
    other_t, other = with_group(attn_t, d), with_group(stats, d)
    wide = RIM + total
    attn, dq, dkw, dvw, rim_sum, dkg, dvg = local_call(
        "window",
        window_body,
        ids,
        (pos_row, q, d_attn, k, v, rim, kv_glob, bias),
        [
            ((total, HEAD_DIM), BF),
            ((total, HEAD_DIM), BF),
            ((wide, HEAD_DIM), F32),
            ((wide, HEAD_DIM), F32),
            ((2 * RIM, HEAD_DIM), BF),
            ((n_glob, HEAD_DIM), F32),
            ((n_glob, HEAD_DIM), F32),
        ],
        [
            pltpu.VMEM((wide, HEAD_DIM), BF),
            pltpu.VMEM((wide, HEAD_DIM), BF),
            pltpu.VMEM((HEAD_DIM, wide), BF),
            pltpu.VMEM((HEAD_DIM, wide), BF),
            pltpu.VMEM((wide, QROWS), F32),
        ],
        flops=12 * total * (RIM + QROWS + n_glob) * HEAD_DIM,
    )
    rim_back = to_next_group(rim_sum, -1)
    attn_parts = swap_in_group(
        local_call(
            "pack_attn",
            pack_attn_body,
            ids,
            (pos_row, attn, attn_t, other_t, stats, other),
            [((tok, HEAD_DIM), BF)] * heads,
            [pltpu.VMEM((total, HEAD_DIM), BF)],
        )
    )
    dk, dv, sums = local_call(
        "row_backward",
        row_backward_body,
        ids,
        (qo_glob, k, v, stats, other, dkw, dvw, dkg, dvg),
        [
            ((total, HEAD_DIM), F32),
            ((total, HEAD_DIM), F32),
            ((3 * n_glob, HEAD_DIM), BF),
        ],
        flops=5 * row_flops,
    )

    def to_lower(x, d):
        route = [
            (g * heads + j, (g - d) * heads + j)
            for g in range(d, min(2 * d, n_groups))
            for j in range(heads)
        ]
        return lax.ppermute(x, "seq", route)

    d = n_groups // 2
    while d > 1:
        sums = (sums.astype(F32) + to_lower(sums, d).astype(F32)).astype(BF)
        d //= 2
    other_sums = to_lower(sums, 1)
    n_head = lax.axis_size("head")
    out_cols = out_weight.shape[1] // n_head
    keep, send = local_call(
        "project",
        project_body,
        ids,
        (out_weight, *attn_parts),
        [((2, tok, out_cols), BF)] * 2,
        [pltpu.VMEM((tok, cols), BF)],
        flops=2 * tok * cols * out_weight.shape[1],
    )
    half = lax.ppermute(send, "head", [(h, h ^ 1) for h in range(n_head)])
    summed = keep.astype(F32) + half.astype(F32)
    far = lax.ppermute(summed[1].astype(BF), "head", [(h, h ^ 2) for h in range(n_head)])
    layer_out = (summed[0] + far.astype(F32)).astype(BF)
    grads = swap_in_group(
        local_call(
            "pack_grads",
            pack_grads_body,
            ids,
            (pos_row, dq, dk, dv, rim_back, sums, other_sums),
            [((3 * tok, HEAD_DIM), BF)] * heads,
            [
                pltpu.VMEM((total, HEAD_DIM), BF),
                pltpu.VMEM((total, HEAD_DIM), F32),
                pltpu.VMEM((total, HEAD_DIM), F32),
            ],
        )
    )
    grad_queries, grad_keys, grad_values = local_call(
        "join_grads", join_grads_body, ids, tuple(grads), [((tok, cols), BF)] * 3
    )
    return (layer_out, grad_queries, grad_keys, grad_values)


def solution(mesh):
    return jax.shard_map(
        on_device,
        mesh=mesh,
        in_specs=(
            P("seq", "head"),
            P("seq", "head"),
            P("seq", "head"),
            P("head", None),
            P("seq", None),
            P(),
            P("seq", None),
        ),
        out_specs=(P("seq", "head"), P("seq", "head"), P("seq", "head"), P("seq", "head")),
        check_vma=False,
    )
```

profile of v0, /device:TPU:0, one launch (start us, length us, event | category | flops | bytes accessed | tf_op | source)
XLA Modules:
  0.0 130.4 jit_solution(4353300732960055442)
XLA Ops:
  0.7 1.6 %copy-done = bf16[512,2048]{1,0:T(8,128)(2,1)S(1)} copy-done((bf16[512,2048]{1,0:T(8,128)(2,1)S(1)}, bf16[512,2048]{1,0:T(8,128)(2,1)}, u32[]{:S(2)}) %copy-start) | copy-done | bytes 2097176
  2.3 1.6 %copy-done.1 = bf16[512,2048]{1,0:T(8,128)(2,1)S(1)} copy-done((bf16[512,2048]{1,0:T(8,128)(2,1)S(1)}, bf16[512,2048]{1,0:T(8,128)(2,1)}, u32[]{:S(2)}) %copy-start.1) | copy-done | bytes 2097176
  5.0 2.0 %pack_qo.1 = (bf16[1024,128]{1,0:T(8,128)(2,1)S(1)}, bf16[1024,128]{1,0:T(8,128)(2,1)S(1)}, bf16[1024,128]{1,0:T(8,128)(2,1)S(1)}, bf16[1024,128]{1,0:T(8,128)(2,1)S(1)}) custom-call(s32[3]{0:T(128)S(1)} %pad_add_fusion.ids, bf16[512,512]{1,0:T(8,128)(2,1)S(1)} %copy-done.3, bf16[512,2048]{1,0:T(8,128)(2,1)S(1)} %copy-done, bf16[512,2048]{1,0:T(8,128)(2,1)S(1)} %copy-done.1), custom_call_target="tpu_custom_call" | custom-call | flops 1073741824 | bytes 5767168 | tf_op jit(solution)/shard_map/pack_qo/pallas_call | solution.py:41
  6.9 3.0 %collective-permute-start = (bf16[1024,128]{1,0:T(8,128)(2,1)S(1)}, bf16[1024,128]{1,0:T(8,128)(2,1)S(1)}, u32[]{:S(2)}, u32[]{:S(2)}) collective-permute-start(bf16[1024,128]{1,0:T(8,128)(2,1)S(1)} %get-tuple-element.46), channel_id=1, source_target_pairs={{0,4},{4,0},{8,12},{12,8},{16,20},{20,16},{24,28},{28,24},{1,5},{5... | collective-permute-start | bytes 786440 | tf_op jit(solution)/shard_map/ppermute | solution.py:341
  13.3 1.9 %collective-permute-start.3 = (bf16[1040,128]{1,0:T(8,128)(2,1)}, bf16[1040,128]{1,0:T(8,128)(2,1)S(1)}, u32[]{:S(2)}, u32[]{:S(2)}) collective-permute-start(bf16[1040,128]{1,0:T(8,128)(2,1)} %get-tuple-element.52), channel_id=1, source_target_pairs={{0,4},{4,0},{8,12},{12,8},{16,20},{20,16},{24,28},{28,24},{1,5},{5... | collective-permute-start | bytes 798728 | tf_op jit(solution)/shard_map/ppermute | solution.py:341
  17.8 3.4 %collective-permute-start.5 = (bf16[1040,128]{1,0:T(8,128)(2,1)}, bf16[1040,128]{1,0:T(8,128)(2,1)S(1)}, u32[]{:S(2)}, u32[]{:S(2)}) collective-permute-start(bf16[1040,128]{1,0:T(8,128)(2,1)} %get-tuple-element.54), channel_id=1, source_target_pairs={{0,12},{4,8},{8,4},{12,0},{16,28},{20,24},{24,20},{28,16},{1,13},{... | collective-permute-start | bytes 798728 | tf_op jit(solution)/shard_map/ppermute | solution.py:341
  21.4 3.0 %collective-permute-done.2.refs_3_ = bf16[1024,128]{1,0:T(8,128)(2,1)S(1)} collective-permute-done((bf16[1024,128]{1,0:T(8,128)(2,1)S(1)}, bf16[1024,128]{1,0:T(8,128)(2,1)S(1)}, u32[]{:S(2)}, u32[]{:S(2)}) %collective-permute-start.2) | collective-permute-done | bytes 262176 | tf_op jit(solution)/shard_map/ppermute | solution.py:341
  25.4 4.8 %collective-permute-start.8 = (bf16[512,128]{1,0:T(8,128)(2,1)S(1)}, bf16[512,128]{1,0:T(8,128)(2,1)S(1)}, u32[]{:S(2)}, u32[]{:S(2)}) collective-permute-start(bf16[512,128]{1,0:T(8,128)(2,1)S(1)} %get-tuple-element.61), channel_id=1, source_target_pairs={{0,16},{4,20},{8,24},{12,28},{1,17},{5,21},{9,25},{13,29},{2,18},{... | collective-permute-start | bytes 393224 | tf_op jit(solution)/shard_map/ppermute | solution.py:356
  30.6 4.8 %collective-permute-done.5.refs_3_ = bf16[1040,128]{1,0:T(8,128)(2,1)S(1)} collective-permute-done((bf16[1040,128]{1,0:T(8,128)(2,1)}, bf16[1040,128]{1,0:T(8,128)(2,1)S(1)}, u32[]{:S(2)}, u32[]{:S(2)}) %collective-permute-start.5) | collective-permute-done | bytes 266272 | tf_op jit(solution)/shard_map/ppermute | solution.py:341
  36.3 5.9 %collective-permute-start.7 = (bf16[512,128]{1,0:T(8,128)(2,1)S(1)}, bf16[512,128]{1,0:T(8,128)(2,1)S(1)}, u32[]{:S(2)}, u32[]{:S(2)}) collective-permute-start(bf16[512,128]{1,0:T(8,128)(2,1)S(1)} %get-tuple-element.58), channel_id=1, source_target_pairs={{0,16},{4,20},{8,24},{12,28},{1,17},{5,21},{9,25},{13,29},{2,18},{... | collective-permute-start | bytes 393224 | tf_op jit(solution)/shard_map/ppermute | solution.py:356
  43.6 1.7 %row_forward.1 = (bf16[128,256]{1,0:T(8,128)(2,1)S(1)}, f32[8,256]{1,0:T(8,128)S(1)}) custom-call(s32[3]{0:T(128)S(1)} %pad_add_fusion.ids, bf16[512,128]{1,0:T(8,128)(2,1)S(1)} %broadcast_select_fusion.qo, bf16[2048,128]{1,0:T(8,128)(2,1)S(1)} %get-tuple-element.55.k, bf16[2048,128]{1,0:T(8,128)(2,1)S(1)} %get-tuple-element.56.v), custom_call_target="tpu_custom_call" | custom-call | flops 402653184 | bytes 1253376 | tf_op jit(solution)/shard_map/row_forward/pallas_call | solution.py:41
  45.4 2.9 %collective-permute-start.9 = (bf16[128,256]{1,0:T(8,128)(2,1)S(1)}, bf16[128,256]{1,0:T(8,128)(2,1)S(1)}, u32[]{:S(2)}, u32[]{:S(2)}) collective-permute-start(bf16[128,256]{1,0:T(8,128)(2,1)S(1)} %get-tuple-element.62.mine_t), channel_id=1, source_target_pairs={{0,16},{4,20},{8,24},{12,28},{16,0},{20,4},{24,8},{28,12},{1,17},{... | collective-permute-start | bytes 196616 | tf_op jit(solution)/shard_map/ppermute | solution.py:365
  48.8 12.3 %window.1 = (bf16[2048,128]{1,0:T(8,128)(2,1)S(1)}, bf16[2048,128]{1,0:T(8,128)(2,1)S(1)}, f32[2432,128]{1,0:T(8,128)S(1)}, f32[2432,128]{1,0:T(8,128)S(1)}, bf1...) custom-call(s32[3]{0:T(128)S(1)} %pad_add_fusion.ids, s32[1,256]{1,0:T(1,128)S(1)} %bitcast.15, ...), custom_call_target="tpu_custom_call" | custom-call | flops 2818572288 | bytes 6456320 | tf_op jit(solution)/shard_map/window/pallas_call | solution.py:41
  62.4 9.3 %collective-permute-start.12 = (bf16[512,128]{1,0:T(8,128)(2,1)S(1)}, bf16[512,128]{1,0:T(8,128)(2,1)S(1)}, u32[]{:S(2)}, u32[]{:S(2)}) collective-permute-start(bf16[512,128]{1,0:T(8,128)(2,1)S(1)} %get-tuple-element.66), channel_id=1, source_target_pairs={{0,8},{4,12},{8,0},{12,4},{16,24},{20,28},{24,16},{28,20},{1,9},{5... | collective-permute-start | bytes 393224 | tf_op jit(solution)/shard_map/ppermute | solution.py:341
  72.9 2.7 %collective-permute-done.12.refs_2_ = bf16[512,128]{1,0:T(8,128)(2,1)S(1)} collective-permute-done((bf16[512,128]{1,0:T(8,128)(2,1)S(1)}, bf16[512,128]{1,0:T(8,128)(2,1)S(1)}, u32[]{:S(2)}, u32[]{:S(2)}) %collective-permute-start.12) | collective-permute-done | bytes 131104 | tf_op jit(solution)/shard_map/ppermute | solution.py:341
  75.6 3.3 %collective-permute-done.13.refs_3_ = bf16[512,128]{1,0:T(8,128)(2,1)S(1)} collective-permute-done((bf16[512,128]{1,0:T(8,128)(2,1)S(1)}, bf16[512,128]{1,0:T(8,128)(2,1)S(1)}, u32[]{:S(2)}, u32[]{:S(2)}) %collective-permute-start.13) | collective-permute-done | bytes 131104 | tf_op jit(solution)/shard_map/ppermute | solution.py:341
  79.0 1.9 %project.1 = (bf16[2,512,512]{2,1,0:T(8,128)(2,1)S(1)}, bf16[2,512,512]{2,1,0:T(8,128)(2,1)S(1)}) custom-call(s32[3]{0:T(128)S(1)} %pad_add_fusion.ids, bf16[512,2048]{1,0:T(8,128)(2,1)S(1)} %copy-done.2, bf16[512,128]{1,0:T(8,128)(2,1)S(1)} %get-tuple-element.64.refs_0_, bf16[512,128]{1,0:T(8,128)(2,1)S(1)} %collective-permute-done.11.refs_1_, ...), custom_call_target="tpu_custom_call" | custom-call | flops 1073741824 | bytes 4718592 | tf_op jit(solution)/shard_map/project/pallas_call | solution.py:41
  80.9 2.2 %row_backward.1 = (f32[2048,128]{1,0:T(8,128)S(1)}, f32[2048,128]{1,0:T(8,128)S(1)}, bf16[768,128]{1,0:T(8,128)(2,1)S(1)}) custom-call(s32[3]{0:T(128)S(1)} %pad_add_fusion.ids, bf16[512,128]{1,0:T(8,128)(2,1)S(1)} %broadcast_select_fusion.qo, bf16[2048,128]{1,0:T(8,128)(2,1)S(1)} %get-tuple-element.55.k, bf16[2048,128]{1,0:T(8,128)(2,1)S(1)} %get-tuple-element.56.v, ...), custom_call_target="tpu_custom_call" | custom-call | flops 671088640 | bytes 6242304 | tf_op jit(solution)/shard_map/row_backward/pallas_call | solution.py:41
  87.7 14.4 %collective-permute-done.17.other = bf16[768,128]{1,0:T(8,128)(2,1)S(1)} collective-permute-done((bf16[768,128]{1,0:T(8,128)(2,1)S(1)}, bf16[768,128]{1,0:T(8,128)(2,1)S(1)}, u32[]{:S(2)}, u32[]{:S(2)}) %collective-permute-start.17) | collective-permute-done | bytes 196640 | tf_op jit(solution)/shard_map/ppermute | solution.py:486
  102.0 3.8 %collective-permute-done.16.rim_back = bf16[768,128]{1,0:T(8,128)(2,1)S(1)} collective-permute-done((bf16[768,128]{1,0:T(8,128)(2,1)S(1)}, bf16[768,128]{1,0:T(8,128)(2,1)S(1)}, u32[]{:S(2)}, u32[]{:S(2)}) %collective-permute-start.16) | collective-permute-done | bytes 196640 | tf_op jit(solution)/shard_map/ppermute | solution.py:362
  107.5 3.1 %collective-permute-start.20 = (bf16[1536,128]{1,0:T(8,128)(2,1)S(1)}, bf16[1536,128]{1,0:T(8,128)(2,1)S(1)}, u32[]{:S(2)}, u32[]{:S(2)}) collective-permute-start(bf16[1536,128]{1,0:T(8,128)(2,1)S(1)} %get-tuple-element.82), channel_id=1, source_target_pairs={{0,12},{4,8},{8,4},{12,0},{16,28},{20,24},{24,20},{28,16},{1,13},{... | collective-permute-start | bytes 1179656 | tf_op jit(solution)/shard_map/ppermute | solution.py:341
  110.7 7.7 %collective-permute-done.18.refs_1_ = bf16[1536,128]{1,0:T(8,128)(2,1)S(1)} collective-permute-done((bf16[1536,128]{1,0:T(8,128)(2,1)S(1)}, bf16[1536,128]{1,0:T(8,128)(2,1)S(1)}, u32[]{:S(2)}, u32[]{:S(2)}) %collective-permute-start.18) | collective-permute-done | bytes 393248 | tf_op jit(solution)/shard_map/ppermute | solution.py:341
  119.6 7.9 %collective-permute-done.20.refs_3_ = bf16[1536,128]{1,0:T(8,128)(2,1)S(1)} collective-permute-done((bf16[1536,128]{1,0:T(8,128)(2,1)S(1)}, bf16[1536,128]{1,0:T(8,128)(2,1)S(1)}, u32[]{:S(2)}, u32[]{:S(2)}) %collective-permute-start.20) | collective-permute-done | bytes 393248 | tf_op jit(solution)/shard_map/ppermute | solution.py:341
  127.5 1.9 %join_grads.1 = (bf16[512,512]{1,0:T(8,128)(2,1)}, bf16[512,512]{1,0:T(8,128)(2,1)}, bf16[512,512]{1,0:T(8,128)(2,1)}) custom-call(s32[3]{0:T(128)S(1)} %pad_add_fusion.ids, bf16[1536,128]{1,0:T(8,128)(2,1)S(1)} %get-tuple-element.79.refs_0_, bf16[1536,128]{1,0:T(8,128)(2,1)S(1)} %collective-permute-done.18.refs_1_, ...), custom_call_target="tpu_custom_call" | custom-call | bytes 3145728 | tf_op jit(solution)/shard_map/join_grads/pallas_call | solution.py:41
  (55 shorter events, 22.3 us)
Async XLA Ops:
  5.0 6.8 %copy-start.5 = (bf16[512,512]{1,0:T(8,128)(2,1)S(1)}, bf16[512,512]{1,0:T(8,128)(2,1)}, u32[]{:S(2)}) copy-start(bf16[512,512]{1,0:T(8,128)(2,1)} %v.1) | copy-start | bytes 1572868
  5.0 16.2 %copy-start.6 = (s32[256]{0:T(256)S(1)}, s32[256]{0:T(256)}, u32[]{:S(2)}) copy-start(s32[256]{0:T(256)} %param.12) | copy-start | bytes 3076
  6.9 10.9 %collective-permute-start = (bf16[1024,128]{1,0:T(8,128)(2,1)S(1)}, bf16[1024,128]{1,0:T(8,128)(2,1)S(1)}, u32[]{:S(2)}, u32[]{:S(2)}) collective-permute-start(bf16[1024,128]{1,0:T(8,128)(2,1)S(1)} %get-tuple-element.46), channel_id=1, source_target_pairs={{0,4},{4,0},{8,12},{12,8},{16,20},{20,16},{24,28},{28,24},{1,5},{5... | collective-permute-start | bytes 786440 | tf_op jit(solution)/shard_map/ppermute | solution.py:341
  10.0 11.4 %collective-permute-start.1 = (bf16[1024,128]{1,0:T(8,128)(2,1)S(1)}, bf16[1024,128]{1,0:T(8,128)(2,1)S(1)}, u32[]{:S(2)}, u32[]{:S(2)}) collective-permute-start(bf16[1024,128]{1,0:T(8,128)(2,1)S(1)} %get-tuple-element.47), channel_id=1, source_target_pairs={{0,8},{4,12},{8,0},{12,4},{16,24},{20,28},{24,16},{28,20},{1,9},{5... | collective-permute-start | bytes 786440 | tf_op jit(solution)/shard_map/ppermute | solution.py:341
  11.6 12.8 %collective-permute-start.2 = (bf16[1024,128]{1,0:T(8,128)(2,1)S(1)}, bf16[1024,128]{1,0:T(8,128)(2,1)S(1)}, u32[]{:S(2)}, u32[]{:S(2)}) collective-permute-start(bf16[1024,128]{1,0:T(8,128)(2,1)S(1)} %get-tuple-element.48), channel_id=1, source_target_pairs={{0,12},{4,8},{8,4},{12,0},{16,28},{20,24},{24,20},{28,16},{1,13},{... | collective-permute-start | bytes 786440 | tf_op jit(solution)/shard_map/ppermute | solution.py:341
  13.3 16.9 %collective-permute-start.3 = (bf16[1040,128]{1,0:T(8,128)(2,1)}, bf16[1040,128]{1,0:T(8,128)(2,1)S(1)}, u32[]{:S(2)}, u32[]{:S(2)}) collective-permute-start(bf16[1040,128]{1,0:T(8,128)(2,1)} %get-tuple-element.52), channel_id=1, source_target_pairs={{0,4},{4,0},{8,12},{12,8},{16,20},{20,16},{24,28},{28,24},{1,5},{5... | collective-permute-start | bytes 798728 | tf_op jit(solution)/shard_map/ppermute | solution.py:341
  15.2 15.4 %collective-permute-start.4 = (bf16[1040,128]{1,0:T(8,128)(2,1)}, bf16[1040,128]{1,0:T(8,128)(2,1)S(1)}, u32[]{:S(2)}, u32[]{:S(2)}) collective-permute-start(bf16[1040,128]{1,0:T(8,128)(2,1)} %get-tuple-element.53), channel_id=1, source_target_pairs={{0,8},{4,12},{8,0},{12,4},{16,24},{20,28},{24,16},{28,20},{1,9},{5... | collective-permute-start | bytes 798728 | tf_op jit(solution)/shard_map/ppermute | solution.py:341
  17.8 17.6 %collective-permute-start.5 = (bf16[1040,128]{1,0:T(8,128)(2,1)}, bf16[1040,128]{1,0:T(8,128)(2,1)S(1)}, u32[]{:S(2)}, u32[]{:S(2)}) collective-permute-start(bf16[1040,128]{1,0:T(8,128)(2,1)} %get-tuple-element.54), channel_id=1, source_target_pairs={{0,12},{4,8},{8,4},{12,0},{16,28},{20,24},{24,20},{28,16},{1,13},{... | collective-permute-start | bytes 798728 | tf_op jit(solution)/shard_map/ppermute | solution.py:341
  25.4 18.2 %collective-permute-start.8 = (bf16[512,128]{1,0:T(8,128)(2,1)S(1)}, bf16[512,128]{1,0:T(8,128)(2,1)S(1)}, u32[]{:S(2)}, u32[]{:S(2)}) collective-permute-start(bf16[512,128]{1,0:T(8,128)(2,1)S(1)} %get-tuple-element.61), channel_id=1, source_target_pairs={{0,16},{4,20},{8,24},{12,28},{1,17},{5,21},{9,25},{13,29},{2,18},{... | collective-permute-start | bytes 393224 | tf_op jit(solution)/shard_map/ppermute | solution.py:356
  36.3 12.0 %collective-permute-start.7 = (bf16[512,128]{1,0:T(8,128)(2,1)S(1)}, bf16[512,128]{1,0:T(8,128)(2,1)S(1)}, u32[]{:S(2)}, u32[]{:S(2)}) collective-permute-start(bf16[512,128]{1,0:T(8,128)(2,1)S(1)} %get-tuple-element.58), channel_id=1, source_target_pairs={{0,16},{4,20},{8,24},{12,28},{1,17},{5,21},{9,25},{13,29},{2,18},{... | collective-permute-start | bytes 393224 | tf_op jit(solution)/shard_map/ppermute | solution.py:356
  42.2 6.6 %collective-permute-start.6 = (bf16[768,128]{1,0:T(8,128)(2,1)S(1)}, bf16[768,128]{1,0:T(8,128)(2,1)S(1)}, u32[]{:S(2)}, u32[]{:S(2)}) collective-permute-start(bf16[768,128]{1,0:T(8,128)(2,1)S(1)} %get-tuple-element.57), channel_id=1, source_target_pairs={{0,16},{4,20},{8,24},{12,28},{1,17},{5,21},{9,25},{13,29},{2,18},{... | collective-permute-start | bytes 589832 | tf_op jit(solution)/shard_map/ppermute | solution.py:362
  45.3 15.8 %collective-permute-start.10 = (f32[8,256]{1,0:T(8,128)S(1)}, f32[8,256]{1,0:T(8,128)S(1)}, u32[]{:S(2)}, u32[]{:S(2)}) collective-permute-start(f32[8,256]{1,0:T(8,128)S(1)} %get-tuple-element.63.stats), channel_id=1, source_target_pairs={{0,16},{4,20},{8,24},{12,28},{16,0},{20,4},{24,8},{28,12},{1,17},{... | collective-permute-start | bytes 24584 | tf_op jit(solution)/shard_map/ppermute | solution.py:365
  45.4 15.7 %collective-permute-start.9 = (bf16[128,256]{1,0:T(8,128)(2,1)S(1)}, bf16[128,256]{1,0:T(8,128)(2,1)S(1)}, u32[]{:S(2)}, u32[]{:S(2)}) collective-permute-start(bf16[128,256]{1,0:T(8,128)(2,1)S(1)} %get-tuple-element.62.mine_t), channel_id=1, source_target_pairs={{0,16},{4,20},{8,24},{12,28},{16,0},{20,4},{24,8},{28,12},{1,17},{... | collective-permute-start | bytes 196616 | tf_op jit(solution)/shard_map/ppermute | solution.py:365
  48.8 30.1 %copy-start.2 = (bf16[512,2048]{1,0:T(8,128)(2,1)S(1)}, bf16[512,2048]{1,0:T(8,128)(2,1)}, u32[]{:S(2)}) copy-start(bf16[512,2048]{1,0:T(8,128)(2,1)} %w.1) | copy-start | bytes 6291460
  62.0 10.9 %collective-permute-start.11 = (bf16[512,128]{1,0:T(8,128)(2,1)S(1)}, bf16[512,128]{1,0:T(8,128)(2,1)S(1)}, u32[]{:S(2)}, u32[]{:S(2)}) collective-permute-start(bf16[512,128]{1,0:T(8,128)(2,1)S(1)} %get-tuple-element.65), channel_id=1, source_target_pairs={{0,4},{4,0},{8,12},{12,8},{16,20},{20,16},{24,28},{28,24},{1,5},{5... | collective-permute-start | bytes 393224 | tf_op jit(solution)/shard_map/ppermute | solution.py:341
  62.4 13.3 %collective-permute-start.12 = (bf16[512,128]{1,0:T(8,128)(2,1)S(1)}, bf16[512,128]{1,0:T(8,128)(2,1)S(1)}, u32[]{:S(2)}, u32[]{:S(2)}) collective-permute-start(bf16[512,128]{1,0:T(8,128)(2,1)S(1)} %get-tuple-element.66), channel_id=1, source_target_pairs={{0,8},{4,12},{8,0},{12,4},{16,24},{20,28},{24,16},{28,20},{1,9},{5... | collective-permute-start | bytes 393224 | tf_op jit(solution)/shard_map/ppermute | solution.py:341
  71.7 7.2 %collective-permute-start.13 = (bf16[512,128]{1,0:T(8,128)(2,1)S(1)}, bf16[512,128]{1,0:T(8,128)(2,1)S(1)}, u32[]{:S(2)}, u32[]{:S(2)}) collective-permute-start(bf16[512,128]{1,0:T(8,128)(2,1)S(1)} %get-tuple-element.67), channel_id=1, source_target_pairs={{0,12},{4,8},{8,4},{12,0},{16,28},{20,24},{24,20},{28,16},{1,13},{... | collective-permute-start | bytes 393224 | tf_op jit(solution)/shard_map/ppermute | solution.py:341
  80.8 4.9 %collective-permute-start.14 = (bf16[2,512,512]{2,1,0:T(8,128)(2,1)S(1)}, bf16[2,512,512]{2,1,0:T(8,128)(2,1)S(1)}, u32[]{:S(2)}, u32[]{:S(2)}) collective-permute-start(bf16[2,512,512]{2,1,0:T(8,128)(2,1)S(1)} %get-tuple-element.69), channel_id=1, source_target_pairs={{0,1},{1,0},{2,3},{3,2},{4,5},{5,4},{6,7},{7,6},{8,9},{9,8},{10,11... | collective-permute-start | bytes 3145736 | tf_op jit(solution)/shard_map/ppermute | solution.py:504
  83.1 18.9 %collective-permute-start.17 = (bf16[768,128]{1,0:T(8,128)(2,1)S(1)}, bf16[768,128]{1,0:T(8,128)(2,1)S(1)}, u32[]{:S(2)}, u32[]{:S(2)}) collective-permute-start(bf16[768,128]{1,0:T(8,128)(2,1)S(1)} %get-tuple-element.78.sums), channel_id=1, source_target_pairs={{16,0},{20,4},{24,8},{28,12},{17,1},{21,5},{25,9},{29,13},{18,2},{... | collective-permute-start | bytes 589832 | tf_op jit(solution)/shard_map/ppermute | solution.py:486
  84.4 21.4 %collective-permute-start.16 = (bf16[768,128]{1,0:T(8,128)(2,1)S(1)}, bf16[768,128]{1,0:T(8,128)(2,1)S(1)}, u32[]{:S(2)}, u32[]{:S(2)}) collective-permute-start(bf16[768,128]{1,0:T(8,128)(2,1)S(1)} %get-tuple-element.77), channel_id=1, source_target_pairs={{16,0},{20,4},{24,8},{28,12},{17,1},{21,5},{25,9},{29,13},{18,2},{... | collective-permute-start | bytes 589832 | tf_op jit(solution)/shard_map/ppermute | solution.py:362
  86.1 43.4 %collective-permute-start.15 = (bf16[512,512]{1,0:T(8,128)(2,1)S(1)}, bf16[512,512]{1,0:T(8,128)(2,1)S(1)}, u32[]{:S(2)}, u32[]{:S(2)}) collective-permute-start(bf16[512,512]{1,0:T(8,128)(2,1)S(1)} %fusion.2), channel_id=1, source_target_pairs={{0,2},{1,3},{2,0},{3,1},{4,6},{5,7},{6,4},{7,5},{8,10},{9,11},{10,... | collective-permute-start | bytes 1572872 | tf_op jit(solution)/shard_map/ppermute | solution.py:506
  107.1 11.2 %collective-permute-start.18 = (bf16[1536,128]{1,0:T(8,128)(2,1)S(1)}, bf16[1536,128]{1,0:T(8,128)(2,1)S(1)}, u32[]{:S(2)}, u32[]{:S(2)}) collective-permute-start(bf16[1536,128]{1,0:T(8,128)(2,1)S(1)} %get-tuple-element.80), channel_id=1, source_target_pairs={{0,4},{4,0},{8,12},{12,8},{16,20},{20,16},{24,28},{28,24},{1,5},{5... | collective-permute-start | bytes 1179656 | tf_op jit(solution)/shard_map/ppermute | solution.py:341
  107.5 12.1 %collective-permute-start.19 = (bf16[1536,128]{1,0:T(8,128)(2,1)S(1)}, bf16[1536,128]{1,0:T(8,128)(2,1)S(1)}, u32[]{:S(2)}, u32[]{:S(2)}) collective-permute-start(bf16[1536,128]{1,0:T(8,128)(2,1)S(1)} %get-tuple-element.81), channel_id=1, source_target_pairs={{0,8},{4,12},{8,0},{12,4},{16,24},{20,28},{24,16},{28,20},{1,9},{5... | collective-permute-start | bytes 1179656 | tf_op jit(solution)/shard_map/ppermute | solution.py:341
  107.5 20.0 %collective-permute-start.20 = (bf16[1536,128]{1,0:T(8,128)(2,1)S(1)}, bf16[1536,128]{1,0:T(8,128)(2,1)S(1)}, u32[]{:S(2)}, u32[]{:S(2)}) collective-permute-start(bf16[1536,128]{1,0:T(8,128)(2,1)S(1)} %get-tuple-element.82), channel_id=1, source_target_pairs={{0,12},{4,8},{8,4},{12,0},{16,28},{20,24},{24,20},{28,16},{1,13},{... | collective-permute-start | bytes 1179656 | tf_op jit(solution)/shard_map/ppermute | solution.py:341
  (5 other events, 17.6 us)
where the time goes:
time: 131 us; the launch traced here: 130 us
  waiting for transfers between devices  50.8 us (39%)
  starting transfers between devices  45.1 us (34%)
  Pallas kernels  27.6 us (21%)
  local copies, waits for them, and re-layouts  4.6 us (4%)
  other arithmetic  1.38 us (1%)
    ppermute x12, waiting for transfers between devices, swap_in_group(): lax.ppermute(piece, 'seq', [(s, s ^ i) for s in range(n_seq)])  32.1 us
    pallas_call x11, Pallas kernels, local_call(): pl.pallas_call(body, name=name, out_shape=tuple((jax.ShapeDtypeStruct(s,...  27.6 us
    ppermute x12, starting transfers between devices, swap_in_group(): lax.ppermute(piece, 'seq', [(s, s ^ i) for s in range(n_seq)])  25.9 us
    ppermute x1, waiting for transfers between devices, to_lower(): return lax.ppermute(x, 'seq', route)  14.4 us
    ppermute x2, starting transfers between devices, from_first(): lax.ppermute(x, 'seq', route)  10.7 us
    ppermute x2, waiting for transfers between devices, to_next_group(): return lax.ppermute(x, 'seq', route)  4.3 us
    unnamed x16, local copies, waits for them, and re-layouts  4.24 us
    ppermute x2, starting transfers between devices, with_group(): return lax.ppermute(x, 'seq', [(s, s ^ d * heads) for s in range(n_seq)])  2.98 us
  transfers between devices with their start and end apart: 21, of which 12 were waited for; matrix products, arithmetic and copies ran while one was open for 1% of the time, Pallas kernels for 18%

commit v1 on v0

v1 whole, which is shorter than its diff:
```python
import functools
import math

import jax
import jax.numpy as jnp
from jax import lax
from jax.experimental import pallas as pl
from jax.experimental.pallas import tpu as pltpu
from jax.sharding import PartitionSpec as P

HEAD_DIM = 128
BLOCK = 128
WBLK = 4
RIM = (WBLK - 1) * BLOCK
QROWS = 2 * BLOCK
SCALE = 1.0 / math.sqrt(HEAD_DIM)
SCALE2 = SCALE * math.log2(math.e)
BF = jnp.bfloat16
F32 = jnp.float32
NEG = float("-inf")
JOIN_US = 12.0
PACK_MIB = 14


def nn(a, b):
    return lax.dot_general(a, b, (((1,), (0,)), ((), ())), preferred_element_type=F32)


def nt(a, b):
    return lax.dot_general(a, b, (((1,), (1,)), ((), ())), preferred_element_type=F32)


def tn(a, b):
    return lax.dot_general(a, b, (((0,), (0,)), ((), ())), preferred_element_type=F32)


def rows(slot, count):
    return pl.ds(pl.multiple_of(slot * count, count), count)


def local_call(name, body, ids, arrays, outs, scratch=(), after=(), aliases=None, far=(), mib=14, us=0.0, out_space=pltpu.VMEM):
    first = 1 + len(arrays) + len(far)

    def kernel(*refs):
        body(*refs[:first], *refs[first + len(after) :])

    return pl.pallas_call(
        kernel,
        name=name,
        out_shape=tuple(jax.ShapeDtypeStruct(s, t) for s, t in outs),
        in_specs=[pl.BlockSpec(memory_space=pltpu.SMEM)]
        + [pl.BlockSpec(memory_space=pltpu.VMEM)] * len(arrays)
        + [pl.BlockSpec(memory_space=space) for _, space in far]
        + [pl.BlockSpec(memory_space=pl.ANY)] * len(after),
        out_specs=tuple(pl.BlockSpec(memory_space=out_space) for _ in outs),
        scratch_shapes=list(scratch),
        compiler_params=pltpu.CompilerParams(vmem_limit_bytes=mib * 2**20),
        input_output_aliases=aliases or {},
        cost_estimate=pl.CostEstimate(
            flops=1000 + int(us * 1.15e9), bytes_accessed=1000, transcendentals=0
        ),
    )(ids, *arrays, *[array for array, _ in far], *after)


def pack_kv_body(ids, k, v, *refs):
    outs, sems = refs[:-1], refs[-1]
    tok = k.shape[0]
    copies = []
    for i, out in enumerate(outs):
        col = rows(ids[0] ^ i, HEAD_DIM)
        copies += [
            pltpu.make_async_copy(k.at[:, col], out.at[0:tok, :], sems.at[2 * i]),
            pltpu.make_async_copy(v.at[:, col], out.at[tok:, :], sems.at[2 * i + 1]),
        ]
    for copy in copies:
        copy.start()
    for copy in copies:
        copy.wait()


def pack_qo_body(ids, q, out_grad, out_weight, block_mask, *refs):
    outs, d_attn = refs[:-1], refs[-1]
    tok = q.shape[0]
    entries = outs[0].shape[0] - 2 * tok
    at = lax.broadcasted_iota(jnp.int32, (entries, HEAD_DIM), 0)
    mask = jnp.zeros((entries, HEAD_DIM), jnp.int32)
    for e in range(entries):
        mask = jnp.where(at == e, block_mask[e // WBLK, e % WBLK], mask)
    mask = mask.astype(F32).astype(BF)
    d_attn[...] = nt(out_grad[...], out_weight[...]).astype(BF)
    for i, out in enumerate(outs):
        col = rows(ids[0] ^ i, HEAD_DIM)
        out[0:tok, :] = q[:, col]
        out[tok : 2 * tok, :] = d_attn[:, col]
        out[2 * tok :, :] = mask


def pick_rows(pos_col, tok):
    hits = pos_col == lax.broadcasted_iota(jnp.int32, (pos_col.shape[0], tok), 1)
    return hits.astype(BF)


def place_rows(pos_row, tok):
    return lax.broadcasted_iota(jnp.int32, (tok, pos_row.shape[1]), 0) == pos_row


def row_column(pos_row, tok):
    hit = place_rows(pos_row, tok).astype(F32)
    return jnp.max(hit, axis=1, keepdims=True) > 0.5


def join_kv_body(ids, pos_col, pos_row, *refs):
    pieces, (k, v, key_bias, picked, rim) = refs[:-5], refs[-5:]
    tok = k.shape[0] // len(pieces)
    for i, piece in enumerate(pieces):
        slot = ids[0] ^ i
        k[rows(slot, tok), :] = piece[0:tok, :]
        v[rows(slot, tok), :] = piece[tok:, :]
    picks = pick_rows(pos_col[...], tok)
    n = pos_col.shape[0]
    picked[0:n, :] = nn(picks, k[0:tok, :]).astype(BF)
    picked[n:, :] = nn(picks, v[0:tok, :]).astype(BF)
    rim[0:RIM, :] = k[k.shape[0] - RIM :, :]
    rim[RIM:, :] = v[k.shape[0] - RIM :, :]
    hidden = jnp.logical_and(row_column(pos_row[...], tok), ids[1] == 0)
    key_bias[...] = jnp.where(hidden, NEG, jnp.zeros(key_bias.shape, F32))


def join_qo_body(ids, pos_col, pos_row, *refs):
    pieces, (q, d_attn, bias, picked) = refs[:-4], refs[-4:]
    tok = q.shape[0] // len(pieces)
    n_rows = bias.shape[0] // len(pieces)
    n = pos_col.shape[0]
    for i, piece in enumerate(pieces):
        slot = ids[0] ^ i
        q[rows(slot, tok), :] = piece[0:tok, :]
        d_attn[rows(slot, tok), :] = piece[tok : 2 * tok, :]
        open_ = piece[2 * tok :, :].astype(F32)
        entry = lax.broadcasted_iota(jnp.int32, open_.shape, 0) + slot * n_rows
        inside = (ids[1] > 0) | (entry // WBLK >= entry % WBLK)
        bias[rows(slot, n_rows), :] = jnp.where((open_ > 0.5) & inside, 0.0, NEG)

    @pl.when(ids[1] == 0)
    def _():
        picks = pick_rows(pos_col[...], tok)
        picked[0:n, :] = nn(picks, q[0:tok, :]).astype(BF)
        picked[n:, :] = nn(picks, d_attn[0:tok, :]).astype(BF)
        is_row = row_column(pos_row[...], tok)
        kept = jnp.where(is_row, 0.0, d_attn[0:tok, :].astype(F32))
        d_attn[0:tok, :] = kept.astype(BF)

    @pl.when(ids[1] > 0)
    def _():
        picked[...] = jnp.zeros_like(picked)


def row_forward_body(ids, picked, k, v, mine, scores):
    n = picked.shape[0] // 2
    step = 512
    query, d_out = picked[0:n, :], picked[n:, :]
    peak = None
    for c in range(0, k.shape[0], step):
        s = nt(k[c : c + step, :], query) * SCALE2
        scores[c : c + step, :] = s
        top = jnp.max(s, axis=0, keepdims=True)
        peak = top if peak is None else jnp.maximum(peak, top)
    mass = jnp.zeros((1, n), F32)
    dot = jnp.zeros((1, n), F32)
    numer = jnp.zeros((HEAD_DIM, n), F32)
    for c in range(0, k.shape[0], step):
        e = jnp.exp2(scores[c : c + step, :] - peak)
        vals = v[c : c + step, :]
        mass = mass + jnp.sum(e, axis=0, keepdims=True)
        dot = dot + jnp.sum(e * nt(vals, d_out), axis=0, keepdims=True)
        numer = numer + tn(vals, e.astype(BF))
    mine[0:HEAD_DIM, :] = (numer / mass).astype(BF)
    mine[HEAD_DIM:, :] = in_thirds((peak, mass, dot))


def in_thirds(values):
    parts = []
    for value in values:
        for _ in range(3):
            part = value.astype(BF).astype(F32)
            parts.append(part)
            value = value - part
    empty = jnp.zeros((16 - len(parts), parts[0].shape[1]), F32)
    return jnp.concatenate(parts + [empty], axis=0).astype(BF)


def merged(mine, other):
    thirds = [ref[HEAD_DIM:, :].astype(F32) for ref in (mine, other)]
    (pa, ma, da), (pb, mb, db) = [
        [t[3 * i : 3 * i + 1] + t[3 * i + 1 : 3 * i + 2] + t[3 * i + 2 : 3 * i + 3] for i in range(3)]
        for t in thirds
    ]
    peak = jnp.maximum(pa, pb)
    wa, wb = jnp.exp2(pa - peak), jnp.exp2(pb - peak)
    mass = ma * wa + mb * wb
    return peak, mass, da * wa + db * wb, ma * wa / mass, mb * wb / mass


def merged_attn(mine, other, wa, wb):
    both = mine[0:HEAD_DIM, :].astype(F32) * wa + other[0:HEAD_DIM, :].astype(F32) * wb
    return both.astype(BF)


def merge_body(ids, mine, other, out):
    peak, mass, dot, wa, wb = merged(mine, other)
    out[0:HEAD_DIM, :] = merged_attn(mine, other, wa, wb)
    out[HEAD_DIM:, :] = in_thirds((peak, mass, dot))


N_KEYS = RIM + QROWS


def window_keys(sb, k, v, rim):
    first = sb * QROWS - RIM
    cut = max(0, -first)
    inner = slice(first + cut, (sb + 1) * QROWS)
    kw, vw = k[inner, :], v[inner, :]
    if cut:
        kw = jnp.concatenate([rim[RIM - cut : RIM, :], kw], axis=0)
        vw = jnp.concatenate([rim[2 * RIM - cut :, :], vw], axis=0)
    return first, cut, inner, kw, vw


def window_forward_body(steps, with_rim, ids, *refs):
    q, d_out, k, v, picked, bias, key_bias = refs[:7]
    rim = refs[7] if with_rim else None
    attn, weights, delta = refs[-3:]
    n = picked.shape[0] // 2
    kg, vg = picked[0:n, :], picked[n:, :]
    key_in = lax.broadcasted_iota(jnp.int32, (BLOCK, QROWS), 0)
    query_in = lax.broadcasted_iota(jnp.int32, (BLOCK, QROWS), 1)
    shut = jnp.full((1, BLOCK), NEG, F32)
    for sb in steps:
        here = slice(sb * QROWS, (sb + 1) * QROWS)
        first, _, _, kw, vw = window_keys(sb, k, v, rim)
        qb = q[here, :]
        raw = nt(kw, qb)
        parts = []
        for kb in range(N_KEYS // BLOCK):
            halves = []
            for half in range(QROWS // BLOCK):
                r = half + WBLK - 1 - kb
                at = (sb * (QROWS // BLOCK) + half) * WBLK + r
                halves.append(bias[at : at + 1, :] if 0 <= r < WBLK else shut)
            part = raw[kb * BLOCK : (kb + 1) * BLOCK, :] * SCALE2 + jnp.concatenate(halves, axis=1)
            at = first + kb * BLOCK
            if 0 <= at < key_bias.shape[0]:
                col = key_bias[at : at + BLOCK, :]
                part = part + jnp.concatenate([col] * (QROWS // BLOCK), axis=1)
            own = kb - (WBLK - 1)
            if own >= 0:
                part = jnp.where(query_in - key_in >= own * BLOCK, part, NEG)
            parts.append(part)
        parts.append(nt(kg, qb) * SCALE2)
        peak = parts[0].max(axis=0, keepdims=True)
        for part in parts[1:]:
            peak = jnp.maximum(peak, part.max(axis=0, keepdims=True))
        grown = [jnp.exp2(part - peak) for part in parts]
        mass = sum(e.sum(axis=0, keepdims=True) for e in grown)
        inv = 1.0 / mass
        ww = jnp.concatenate([(e * inv).astype(BF) for e in grown], axis=0)
        weights[sb * (N_KEYS + n) : (sb + 1) * (N_KEYS + n), :] = ww
        out_t = tn(vw, ww[0:N_KEYS, :]) + tn(vg, ww[N_KEYS:, :])
        out = out_t.T.astype(BF)
        attn[here, :] = out
        dot = out_t.astype(BF).astype(F32) * d_out[here, :].astype(F32).T
        delta[sb : sb + 1, :] = jnp.sum(dot, axis=0, keepdims=True)


def glob_backward_body(ids, q, d_out, picked, weights, delta, dq_part, dk_glob, dv_glob):
    n = picked.shape[0] // 2
    n_steps = delta.shape[0]
    kg, vg = picked[0:n, :], picked[n:, :]
    dk_glob[...] = jnp.zeros_like(dk_glob)
    dv_glob[...] = jnp.zeros_like(dv_glob)
    for sb in range(n_steps):
        here = slice(sb * QROWS, (sb + 1) * QROWS)
        qb, dob = q[here, :], d_out[here, :]
        wg = weights[sb * (N_KEYS + n) + N_KEYS : (sb + 1) * (N_KEYS + n), :]
        dg = (wg.astype(F32) * (nt(vg, dob) - delta[sb : sb + 1, :])).astype(BF)
        dq_part[sb * HEAD_DIM : (sb + 1) * HEAD_DIM, :] = tn(kg, dg)
        dk_glob[...] += nn(dg, qb)
        dv_glob[...] += nn(wg, dob)


def window_backward_body(steps, n, with_rim, ids, *refs):
    q, d_out, k, v, weights, delta = refs[:6]
    if with_rim:
        rim = refs[6]
        dq_rim, dk, dv, rim_back, dk_rim, dv_rim = refs[-6:]
        for ref in (dk, dv, dk_rim, dv_rim):
            ref[...] = jnp.zeros_like(ref)
    else:
        rim = None
        dq_part, dq_rim = refs[6:8]
        dk, dv, dq = refs[-3:]
        for sb in range(dq_rim.shape[0] // HEAD_DIM):
            here = slice(sb * HEAD_DIM, (sb + 1) * HEAD_DIM)
            dq_t = dq_rim[here, :] + dq_part[here, :]
            dq[sb * QROWS : (sb + 1) * QROWS, :] = (dq_t.T * SCALE).astype(BF)
    for sb in steps:
        here = slice(sb * QROWS, (sb + 1) * QROWS)
        _, cut, inner, kw, vw = window_keys(sb, k, v, rim)
        qb, dob = q[here, :], d_out[here, :]
        at = sb * (N_KEYS + n)
        ww = weights[at : at + N_KEYS, :]
        dw = (ww.astype(F32) * (nt(vw, dob) - delta[sb : sb + 1, :])).astype(BF)
        part = slice(sb * HEAD_DIM, (sb + 1) * HEAD_DIM)
        if with_rim:
            dq_rim[part, :] = tn(kw, dw)
        else:
            dq_t = tn(kw, dw) + dq_part[part, :]
            dq[here, :] = (dq_t.T * SCALE).astype(BF)
        dkw, dvw = nn(dw, qb), nn(ww, dob)
        if cut:
            dk_rim[RIM - cut :, :] += dkw[0:cut, :]
            dv_rim[RIM - cut :, :] += dvw[0:cut, :]
        dk[inner, :] += dkw[cut:, :]
        dv[inner, :] += dvw[cut:, :]
    if with_rim:
        rim_back[0:RIM, :] = dk_rim[...].astype(BF)
        rim_back[RIM:, :] = dv_rim[...].astype(BF)


def row_backward_body(ids, picked, k, v, mine, other, dkg, dvg, dk, dv, sums):
    n = picked.shape[0] // 2
    step = 512
    query, d_out = picked[0:n, :], picked[n:, :]
    peak, mass, dot, _, _ = merged(mine, other)
    lse = peak + jnp.log2(mass)
    delta = dot / mass
    dq_t = jnp.zeros((HEAD_DIM, n), F32)
    for c in range(0, k.shape[0], step):
        keys, vals = k[c : c + step, :], v[c : c + step, :]
        prob = jnp.exp2(nt(keys, query) * SCALE2 - lse)
        ds = (prob * (nt(vals, d_out) - delta)).astype(BF)
        dk[c : c + step, :] = nn(ds, query)
        dv[c : c + step, :] = nn(prob.astype(BF), d_out)
        dq_t = dq_t + tn(keys, ds)
    sums[0:n, :] = (dq_t.T * SCALE).astype(BF)
    sums[n : 2 * n, :] = dkg[...].astype(BF)
    sums[2 * n :, :] = dvg[...].astype(BF)


def pack_rows_body(ids, pos_row, attn, mine, other, *refs):
    outs, attn_f = refs[:-1], refs[-1]
    tok = attn.shape[0] // len(outs)
    attn_f[...] = attn[...]

    @pl.when(ids[1] == 0)
    def _():
        _, _, _, wa, wb = merged(mine, other)
        both_t = merged_attn(mine, other, wa, wb)
        hit = place_rows(pos_row[...], tok)
        is_row = jnp.max(hit.astype(F32), axis=1, keepdims=True) > 0.5
        placed = nt(hit.astype(BF), both_t)
        attn_f[0:tok, :] = jnp.where(is_row, placed, attn[0:tok, :].astype(F32)).astype(BF)

    for i, out in enumerate(outs):
        out[...] = attn_f[rows(ids[0] ^ i, tok), :]


def project_body(ids, w, *refs):
    pieces, (keep, send, attn) = refs[:-3], refs[-3:]
    for i, piece in enumerate(pieces):
        attn[:, rows(ids[0] ^ i, HEAD_DIM)] = piece[...]
    cols = keep.shape[2]
    a = attn[...]
    me = ids[2]
    for i, group in enumerate((me, me ^ 2)):
        keep[i] = nn(a, w[:, rows(group, cols)]).astype(BF)
    for i, group in enumerate((me ^ 1, me ^ 3)):
        send[i] = nn(a, w[:, rows(group, cols)]).astype(BF)


def pack_grads_body(ids, pos_row, dq, dk, dv, rk, rv, rim_back, sums, other, *refs):
    outs, (dqf, dkf, dvf) = refs[:-3], refs[-3:]
    total = dk.shape[0]
    tok = total // len(outs)
    n = sums.shape[0] // 3
    dqf[...] = dq[...]
    dkf[...] = dk[...] + rk[...]
    dvf[...] = dv[...] + rv[...]
    dkf[total - RIM :, :] += rim_back[0:RIM, :].astype(F32)
    dvf[total - RIM :, :] += rim_back[RIM:, :].astype(F32)

    @pl.when(ids[1] == 0)
    def _():
        both = (sums[...].astype(F32) + other[...].astype(F32)).astype(BF)
        hit = place_rows(pos_row[...], tok).astype(BF)
        dqf[0:tok, :] = (dqf[0:tok, :].astype(F32) + nn(hit, both[0:n, :])).astype(BF)
        dkf[0:tok, :] += nn(hit, both[n : 2 * n, :])
        dvf[0:tok, :] += nn(hit, both[2 * n :, :])

    for i, out in enumerate(outs):
        here = rows(ids[0] ^ i, tok)
        out[0:tok, :] = dqf[here, :]
        out[tok : 2 * tok, :] = (dkf[here, :] * SCALE).astype(BF)
        out[2 * tok :, :] = dvf[here, :].astype(BF)


def join_grads_body(ids, *refs):
    pieces, outs = refs[:-3], refs[-3:]
    tok = outs[0].shape[0]
    for i, piece in enumerate(pieces):
        col = rows(ids[0] ^ i, HEAD_DIM)
        for at, out in enumerate(outs):
            out[:, col] = piece[at * tok : (at + 1) * tok, :]


def on_device(queries, keys, values, out_weight, out_grad, global_pos, block_mask):
    tok, cols = queries.shape
    heads = cols // HEAD_DIM
    n_seq = lax.axis_size("seq")
    n_groups = n_seq // heads
    total = heads * tok
    n_glob = global_pos.shape[0]
    seq_index = lax.axis_index("seq")
    group = seq_index // heads
    ids = jnp.stack([seq_index % heads, group, lax.axis_index("head")]).astype(jnp.int32)
    pos_col = global_pos.reshape(n_glob, 1)
    pos_row = global_pos.reshape(1, n_glob)

    def swap_in_group(pieces):
        moved = [
            lax.ppermute(piece, "seq", [(s, s ^ i) for s in range(n_seq)])
            for i, piece in enumerate(pieces)
            if i
        ]
        return [pieces[0]] + moved

    def from_first(x):
        d = 1
        while d < n_groups:
            route = [
                (g * heads + j, (g + d) * heads + j)
                for g in range(d)
                for j in range(heads)
                if g + d < n_groups
            ]
            x = jnp.where((group >= d) & (group < 2 * d), lax.ppermute(x, "seq", route), x)
            d *= 2
        return x

    def to_next_group(x, step):
        route = [(s, s + step * heads) for s in range(n_seq) if 0 <= s + step * heads < n_seq]
        return lax.ppermute(x, "seq", route)

    def with_group(x, d):
        return lax.ppermute(x, "seq", [(s, s ^ (d * heads)) for s in range(n_seq)])

    kv_packed = local_call(
        "pack_kv",
        pack_kv_body,
        ids,
        (),
        [((2 * tok, HEAD_DIM), BF)] * heads,
        [pltpu.SemaphoreType.DMA((2 * heads,))],
        far=((keys, pltpu.HBM), (values, pltpu.HBM)),
        mib=PACK_MIB,
        out_space=pltpu.VMEM,
    )
    kv = swap_in_group(kv_packed)
    qo = swap_in_group(
        local_call(
            "pack_qo",
            pack_qo_body,
            ids,
            (queries, out_grad, out_weight),
            [((2 * tok + block_mask.size, HEAD_DIM), BF)] * heads,
            [pltpu.VMEM((tok, cols), BF)],
            far=((block_mask, pltpu.SMEM),),
            after=(kv_packed[0],),
        )
    )
    head_rows = ((total, HEAD_DIM), BF)
    head_sums = ((total, HEAD_DIM), F32)
    glob_sums = ((n_glob, HEAD_DIM), F32)
    k, v, key_bias, picked, rim_out = local_call(
        "join_kv",
        join_kv_body,
        ids,
        (pos_col, pos_row, *kv),
        [
            head_rows,
            head_rows,
            ((tok, HEAD_DIM), F32),
            ((2 * n_glob, HEAD_DIM), BF),
            ((2 * RIM, HEAD_DIM), BF),
        ],
    )
    kv_glob = from_first(picked)
    rim = to_next_group(rim_out, 1)
    q, d_attn, bias, qo_pick = local_call(
        "join_qo",
        join_qo_body,
        ids,
        (pos_col, pos_row, *qo),
        [
            head_rows,
            head_rows,
            ((heads * block_mask.size, HEAD_DIM), F32),
            ((2 * n_glob, HEAD_DIM), BF),
        ],
        after=(picked,),
    )
    qo_glob = from_first(qo_pick)
    n_steps = total // QROWS
    base = (q, d_attn, k, v, kv_glob)
    forward_types = [
        head_rows,
        ((n_steps * (N_KEYS + n_glob), QROWS), BF),
        ((n_steps, QROWS), F32),
    ]
    backward_types = [head_rows, head_sums, head_sums, glob_sums, glob_sums]
    rim_type = [((2 * RIM, HEAD_DIM), BF)]

    def window(name, body, args, state, outs, scratch=(), after=()):
        at = 1 + len(args)
        return local_call(
            name,
            body,
            ids,
            tuple(args) + tuple(state),
            outs,
            scratch,
            after=after,
            aliases={at + i: i for i in range(len(state))},
            mib=20,
        )

    seen = window(
        "forward_inner",
        functools.partial(window_forward_body, range(2, n_steps), False),
        base + (bias, key_bias),
        (),
        forward_types,
    )
    attn, weights, delta = window(
        "forward_rim",
        functools.partial(window_forward_body, range(0, 2), True),
        base + (bias, key_bias, rim),
        seen,
        forward_types,
    )
    backward = (q, d_attn, k, v, weights, delta)
    dq_rim, *state, rim_sum = window(
        "backward_rim",
        functools.partial(window_backward_body, range(0, 2), n_glob, True),
        backward + (rim,),
        (),
        [((2 * HEAD_DIM, QROWS), F32), head_sums, head_sums, ((2 * RIM, HEAD_DIM), BF)],
        [pltpu.VMEM((RIM, HEAD_DIM), F32)] * 2,
    )
    rim_back = to_next_group(rim_sum, -1)
    packed_rows = ((HEAD_DIM + 16, n_glob), BF)
    mine = local_call(
        "row_forward",
        row_forward_body,
        ids,
        (qo_glob, k, v),
        [packed_rows],
        [pltpu.VMEM((total, n_glob), F32)],
        after=(rim_sum,),
    )[0]
    d = 1
    while 2 * d < n_groups:
        mine = local_call("merge", merge_body, ids, (mine, with_group(mine, d)), [packed_rows])[0]
        d *= 2
    other = with_group(mine, d)
    dq_part, dkg, dvg = local_call(
        "glob_backward",
        glob_backward_body,
        ids,
        (q, d_attn, kv_glob, weights, delta),
        [((n_steps * HEAD_DIM, QROWS), F32), glob_sums, glob_sums],
        after=(mine,),
    )
    rk, rv, sums = local_call(
        "row_backward",
        row_backward_body,
        ids,
        (qo_glob, k, v, mine, other, dkg, dvg),
        [head_sums, head_sums, ((3 * n_glob, HEAD_DIM), BF)],
    )
    attn_parts = swap_in_group(
        local_call(
            "pack_rows",
            pack_rows_body,
            ids,
            (pos_row, attn, mine, other),
            [((tok, HEAD_DIM), BF)] * heads,
            [pltpu.VMEM((total, HEAD_DIM), BF)],
            after=(sums,),
        )
    )
    dk, dv, dq = window(
        "backward_inner",
        functools.partial(window_backward_body, range(2, n_steps), n_glob, False),
        backward + (dq_part, dq_rim),
        state,
        [head_sums, head_sums, head_rows],
        after=(attn_parts[0],),
    )

    def to_lower(x, d):
        route = [
            (g * heads + j, (g - d) * heads + j)
            for g in range(d, min(2 * d, n_groups))
            for j in range(heads)
        ]
        return lax.ppermute(x, "seq", route)

    d = n_groups // 2
    while d > 1:
        sums = (sums.astype(F32) + to_lower(sums, d).astype(F32)).astype(BF)
        d //= 2
    other_sums = to_lower(sums, 1)
    grads = swap_in_group(
        local_call(
            "pack_grads",
            pack_grads_body,
            ids,
            (pos_row, dq, dk, dv, rk, rv, rim_back, sums, other_sums),
            [((3 * tok, HEAD_DIM), BF)] * heads,
            [
                pltpu.VMEM((total, HEAD_DIM), BF),
                pltpu.VMEM((total, HEAD_DIM), F32),
                pltpu.VMEM((total, HEAD_DIM), F32),
            ],
        )
    )
    n_head = lax.axis_size("head")
    out_cols = out_weight.shape[1] // n_head
    keep, send = local_call(
        "project",
        project_body,
        ids,
        (out_weight, *attn_parts),
        [((2, tok, out_cols), BF)] * 2,
        [pltpu.VMEM((tok, cols), BF)],
        after=(grads[0],),
    )
    half = lax.ppermute(send, "head", [(h, h ^ 1) for h in range(n_head)])
    summed = keep.astype(F32) + half.astype(F32)
    far = lax.ppermute(summed[1].astype(BF), "head", [(h, h ^ 2) for h in range(n_head)])
    layer_out = (summed[0] + far.astype(F32)).astype(BF)
    grad_queries, grad_keys, grad_values = local_call(
        "join_grads", join_grads_body, ids, tuple(grads), [((tok, cols), BF)] * 3, us=JOIN_US
    )
    return (layer_out, grad_queries, grad_keys, grad_values)


def solution(mesh):
    return jax.shard_map(
        on_device,
        mesh=mesh,
        in_specs=(
            P("seq", "head"),
            P("seq", "head"),
            P("seq", "head"),
            P("head", None),
            P("seq", None),
            P(),
            P("seq", None),
        ),
        out_specs=(P("seq", "head"), P("seq", "head"), P("seq", "head"), P("seq", "head")),
        check_vma=False,
    )
```

time: 131 us -> 103 us (0.79)
  waiting for transfers between devices: 50.8 us -> 23.4 us
  starting transfers between devices: 45.1 us -> 37.4 us
  local copies, waits for them, and re-layouts: 4.6 us -> 9.71 us
  Pallas kernels: 27.6 us -> 30 us
    ppermute x12, waiting for transfers between devices: 32.1 us -> 19.1 us  [swap_in_group(): lax.ppermute(piece, 'seq', [(s, s ^ i) for s in range(n_seq)])]
    ppermute x1, waiting for transfers between devices: 14.4 us -> 3.07 us  [to_lower(): return lax.ppermute(x, 'seq', route)]
    ppermute x12, starting transfers between devices: 25.9 us -> 18.7 us  [swap_in_group(): lax.ppermute(piece, 'seq', [(s, s ^ i) for s in range(n_seq)])]
    unnamed x16 -> x22, local copies, waits for them, and re-layouts: 4.24 us -> 9.51 us
    ppermute x2, waiting for transfers between devices: 4.3 us -> 1.23 us  [to_next_group(): return lax.ppermute(x, 'seq', route)]
    pallas_call x11 -> x15, Pallas kernels: 27.6 us -> 30 us  [local_call(): pl.pallas_call(kernel, name=name, out_shape=tuple((jax.ShapeDtypeStruct(s...]
    ppermute x2 -> x1, starting transfers between devices: 2.98 us -> 1.84 us  [with_group(): return lax.ppermute(x, 'seq', [(s, s ^ d * heads) for s in range(n_seq)])]
  transfers between devices with their start and end apart: 21 -> 20, of which waited for: 12 -> 7; matrix products, arithmetic and copies ran while one was open for 1% -> 1% of each run, Pallas kernels for 18% -> 21%
where the time goes in v1:
time: 103 us
  starting transfers between devices  37.4 us (36%)
  Pallas kernels  30 us (29%)
  waiting for transfers between devices  23.4 us (23%)
  local copies, waits for them, and re-layouts  9.71 us (9%)
  other arithmetic  1.41 us (1%)
    pallas_call x15, Pallas kernels, local_call(): pl.pallas_call(kernel, name=name, out_shape=tuple((jax.ShapeDtypeStruct(s...  30 us
    ppermute x12, waiting for transfers between devices, swap_in_group(): lax.ppermute(piece, 'seq', [(s, s ^ i) for s in range(n_seq)])  19.1 us
    ppermute x12, starting transfers between devices, swap_in_group(): lax.ppermute(piece, 'seq', [(s, s ^ i) for s in range(n_seq)])  18.7 us
    ppermute x2, starting transfers between devices, from_first(): lax.ppermute(x, 'seq', route)  11.2 us
    unnamed x22, local copies, waits for them, and re-layouts  9.51 us
    ppermute x1, waiting for transfers between devices, to_lower(): return lax.ppermute(x, 'seq', route)  3.07 us
    ppermute x2, starting transfers between devices, to_next_group(): return lax.ppermute(x, 'seq', route)  2.77 us
  transfers between devices with their start and end apart: 20, of which 7 were waited for; matrix products, arithmetic and copies ran while one was open for 1% of the time, Pallas kernels for 21%

profile of v1, /device:TPU:0, one launch (start us, length us, event | category | flops | bytes accessed | tf_op | source)
XLA Modules:
  0.0 102.9 jit_solution(2091636174613369720)
XLA Ops:
  3.6 3.0 %collective-permute-start.3 = (bf16[1024,128]{1,0:T(8,128)(2,1)S(1)}, bf16[1024,128]{1,0:T(8,128)(2,1)S(1)}, u32[]{:S(2)}, u32[]{:S(2)}) collective-permute-start(bf16[1024,128]{1,0:T(8,128)(2,1)S(1)} %get-tuple-element.58), channel_id=1, source_target_pairs={{0,4},{4,0},{8,12},{12,8},{16,20},{20,16},{24,28},{28,24},{1,5},{5... | collective-permute-start | bytes 786440 | tf_op jit(solution)/shard_map/ppermute | solution.py:430
  8.3 1.6 %copy-done = bf16[512,2048]{1,0:T(8,128)(2,1)S(1)} copy-done((bf16[512,2048]{1,0:T(8,128)(2,1)S(1)}, bf16[512,2048]{1,0:T(8,128)(2,1)}, u32[]{:S(2)}) %copy-start) | copy-done | bytes 2097176
  9.9 1.6 %copy-done.2 = bf16[512,2048]{1,0:T(8,128)(2,1)S(1)} copy-done((bf16[512,2048]{1,0:T(8,128)(2,1)S(1)}, bf16[512,2048]{1,0:T(8,128)(2,1)}, u32[]{:S(2)}) %copy-start.2) | copy-done | bytes 2097176
  13.2 2.8 %pack_qo.1 = (bf16[1040,128]{1,0:T(8,128)(2,1)S(1)}, bf16[1040,128]{1,0:T(8,128)(2,1)}, bf16[1040,128]{1,0:T(8,128)(2,1)}, bf16[1040,128]{1,0:T(8,128)(2,1)}) custom-call(s32[3]{0:T(128)S(1)} %pad_add_fusion.refs_0_, bf16[512,512]{1,0:T(8,128)(2,1)S(1)} %copy-done.3, bf16[512,2048]{1,0:T(8,128)(2,1)S(1)} %copy-done.2, bf16[512,2048]{1,0:T(8,128)(2,1)S(1)} %copy-done, ...), custom_call_target="tpu_custom_call" | custom-call | flops 1000 | bytes 1000 | tf_op jit(solution)/shard_map/pack_qo/pallas_call | solution.py:47
  15.9 1.9 %collective-permute-start = (bf16[1040,128]{1,0:T(8,128)(2,1)}, bf16[1040,128]{1,0:T(8,128)(2,1)S(1)}, u32[]{:S(2)}, u32[]{:S(2)}) collective-permute-start(bf16[1040,128]{1,0:T(8,128)(2,1)} %get-tuple-element.55), channel_id=1, source_target_pairs={{0,4},{4,0},{8,12},{12,8},{16,20},{20,16},{24,28},{28,24},{1,5},{5... | collective-permute-start | bytes 798728 | tf_op jit(solution)/shard_map/ppermute | solution.py:430
  17.9 1.6 %collective-permute-start.1 = (bf16[1040,128]{1,0:T(8,128)(2,1)}, bf16[1040,128]{1,0:T(8,128)(2,1)S(1)}, u32[]{:S(2)}, u32[]{:S(2)}) collective-permute-start(bf16[1040,128]{1,0:T(8,128)(2,1)} %get-tuple-element.56), channel_id=1, source_target_pairs={{0,8},{4,12},{8,0},{12,4},{16,24},{20,28},{24,16},{28,20},{1,9},{5... | collective-permute-start | bytes 798728 | tf_op jit(solution)/shard_map/ppermute | solution.py:430
  23.7 4.7 %collective-permute-start.6 = (bf16[512,128]{1,0:T(8,128)(2,1)S(1)}, bf16[512,128]{1,0:T(8,128)(2,1)S(1)}, u32[]{:S(2)}, u32[]{:S(2)}) collective-permute-start(bf16[512,128]{1,0:T(8,128)(2,1)S(1)} %get-tuple-element.61.refs_7_), channel_id=1, source_target_pairs={{0,16},{4,20},{8,24},{12,28},{1,17},{5,21},{9,25},{13,29},{2,18},{... | collective-permute-start | bytes 393224 | tf_op jit(solution)/shard_map/ppermute | solution.py:445
  29.7 2.6 %collective-permute-done.2.refs_6_ = bf16[1040,128]{1,0:T(8,128)(2,1)S(1)} collective-permute-done((bf16[1040,128]{1,0:T(8,128)(2,1)}, bf16[1040,128]{1,0:T(8,128)(2,1)S(1)}, u32[]{:S(2)}, u32[]{:S(2)}) %collective-permute-start.2) | collective-permute-done | bytes 266272 | tf_op jit(solution)/shard_map/ppermute | solution.py:430
  33.3 6.5 %collective-permute-start.8 = (bf16[512,128]{1,0:T(8,128)(2,1)S(1)}, bf16[512,128]{1,0:T(8,128)(2,1)S(1)}, u32[]{:S(2)}, u32[]{:S(2)}) collective-permute-start(bf16[512,128]{1,0:T(8,128)(2,1)S(1)} %get-tuple-element.73), channel_id=1, source_target_pairs={{0,16},{4,20},{8,24},{12,28},{1,17},{5,21},{9,25},{13,29},{2,18},{... | collective-permute-start | bytes 393224 | tf_op jit(solution)/shard_map/ppermute | solution.py:445
  39.8 4.1 %forward_inner.1 = (bf16[2048,128]{1,0:T(8,128)(2,1)S(1)}, bf16[7168,256]{1,0:T(8,128)(2,1)S(1)}, f32[8,256]{1,0:T(8,128)S(1)}) custom-call(s32[3]{0:T(128)S(1)} %pad_add_fusion.refs_0_, bf16[2048,128]{1,0:T(8,128)(2,1)S(1)} %get-tuple-element.62.refs_1_, bf16[2048,128]{1,0:T(8,128)(2,1)S(1)} %get-tuple-element.63.refs_2_, ...), custom_call_target="tpu_custom_call" | custom-call | flops 1000 | bytes 1000 | tf_op jit(solution)/shard_map/forward_inner/pallas_call | solution.py:47
  44.0 2.0 %forward_rim.1 = (bf16[2048,128]{1,0:T(8,128)(2,1)S(1)}, bf16[7168,256]{1,0:T(8,128)(2,1)S(1)}, f32[8,256]{1,0:T(8,128)S(1)}) custom-call(s32[3]{0:T(128)S(1)} %pad_add_fusion.refs_0_, bf16[2048,128]{1,0:T(8,128)(2,1)S(1)} %get-tuple-element.62.refs_1_, ...), custom_call_target="tpu_custom_call", output_to_operand_aliasing={{0}: (9, {}), {1}: (10, {}), {2}: (11, {})} | custom-call | flops 1000 | bytes 1000 | tf_op jit(solution)/shard_map/forward_rim/pallas_call | solution.py:47
  46.0 1.8 %backward_rim.1 = (f32[256,256]{1,0:T(8,128)S(1)}, f32[2048,128]{1,0:T(8,128)S(1)}, f32[2048,128]{1,0:T(8,128)S(1)}, bf16[768,128]{1,0:T(8,128)(2,1)S(1)}) custom-call(s32[3]{0:T(128)S(1)} %pad_add_fusion.refs_0_, bf16[2048,128]{1,0:T(8,128)(2,1)S(1)} %get-tuple-element.62.refs_1_, bf16[2048,128]{1,0:T(8,128)(2,1)S(1)} %get-tuple-element.63.refs_2_, ...), custom_call_target="tpu_custom_call" | custom-call | flops 1000 | bytes 1000 | tf_op jit(solution)/shard_map/backward_rim/pallas_call | solution.py:47
  47.8 1.7 %row_forward.1.refs_6_.refs_4_.refs_3_ = bf16[144,256]{1,0:T(8,128)(2,1)S(1)} custom-call(s32[3]{0:T(128)S(1)} %pad_add_fusion.refs_0_, bf16[512,128]{1,0:T(8,128)(2,1)S(1)} %broadcast_select_fusion.refs_1_, bf16[2048,128]{1,0:T(8,128)(2,1)S(1)} %get-tuple-element.64.refs_3_.refs_2_, bf16[2048,128]{1,0:T(8,128)(2,1)S(1)} %get-tuple-element.65.refs_4_.refs_3_, ...), custom_call_target="tpu_custom_call" | custom-call | flops 1000 | bytes 1000 | tf_op jit(solution)/shard_map/row_forward/pallas_call | solution.py:47
  49.5 1.8 %collective-permute-start.9 = (bf16[144,256]{1,0:T(8,128)(2,1)S(1)}, bf16[144,256]{1,0:T(8,128)(2,1)S(1)}, u32[]{:S(2)}, u32[]{:S(2)}) collective-permute-start(bf16[144,256]{1,0:T(8,128)(2,1)S(1)} %row_forward.1.refs_6_.refs_4_.refs_3_), channel_id=1, source_target_pairs={{0,16},{4,20},{8,24},{12,28},{16,0},{20,4},{24,8},{28,12},{1,17},{... | collective-permute-start | bytes 221192 | tf_op jit(solution)/shard_map/ppermute | solution.py:454
  51.3 3.0 %glob_backward.1 = (f32[1024,256]{1,0:T(8,128)S(1)}, f32[256,128]{1,0:T(8,128)S(1)}, f32[256,128]{1,0:T(8,128)S(1)}) custom-call(s32[3]{0:T(128)S(1)} %pad_add_fusion.refs_0_, bf16[2048,128]{1,0:T(8,128)(2,1)S(1)} %get-tuple-element.62.refs_1_, bf16[2048,128]{1,0:T(8,128)(2,1)S(1)} %get-tuple-element.63.refs_2_, ...), custom_call_target="tpu_custom_call" | custom-call | flops 1000 | bytes 1000 | tf_op jit(solution)/shard_map/glob_backward/pallas_call | solution.py:47
  55.8 2.2 %row_backward.1 = (f32[2048,128]{1,0:T(8,128)S(1)}, f32[2048,128]{1,0:T(8,128)S(1)}, bf16[768,128]{1,0:T(8,128)(2,1)S(1)}) custom-call(s32[3]{0:T(128)S(1)} %pad_add_fusion.refs_0_, bf16[512,128]{1,0:T(8,128)(2,1)S(1)} %broadcast_select_fusion.refs_1_, bf16[2048,128]{1,0:T(8,128)(2,1)S(1)} %get-tuple-element.64.refs_3_.refs_2_, ...), custom_call_target="tpu_custom_call" | custom-call | flops 1000 | bytes 1000 | tf_op jit(solution)/shard_map/row_backward/pallas_call | solution.py:47
  60.3 6.9 %collective-permute-start.11 = (bf16[512,128]{1,0:T(8,128)(2,1)S(1)}, bf16[512,128]{1,0:T(8,128)(2,1)S(1)}, u32[]{:S(2)}, u32[]{:S(2)}) collective-permute-start(bf16[512,128]{1,0:T(8,128)(2,1)S(1)} %get-tuple-element.82), channel_id=1, source_target_pairs={{0,8},{4,12},{8,0},{12,4},{16,24},{20,28},{24,16},{28,20},{1,9},{5... | collective-permute-start | bytes 393224 | tf_op jit(solution)/shard_map/ppermute | solution.py:430
  67.3 3.7 %backward_inner.1 = (f32[2048,128]{1,0:T(8,128)S(1)}, f32[2048,128]{1,0:T(8,128)S(1)}, bf16[2048,128]{1,0:T(8,128)(2,1)S(1)}) custom-call(s32[3]{0:T(128)S(1)} %pad_add_fusion.refs_0_, bf16[2048,128]{1,0:T(8,128)(2,1)S(1)} %get-tuple-element.62.refs_1_, ...), custom_call_target="tpu_custom_call", output_to_operand_aliasing={{0}: (9, {}), {1}: (10, {})} | custom-call | flops 1000 | bytes 1000 | tf_op jit(solution)/shard_map/backward_inner/pallas_call | solution.py:47
  72.2 3.1 %collective-permute-done.14.refs_9_ = bf16[768,128]{1,0:T(8,128)(2,1)S(1)} collective-permute-done((bf16[768,128]{1,0:T(8,128)(2,1)S(1)}, bf16[768,128]{1,0:T(8,128)(2,1)S(1)}, u32[]{:S(2)}, u32[]{:S(2)}) %collective-permute-start.14) | collective-permute-done | bytes 196640 | tf_op jit(solution)/shard_map/ppermute | solution.py:616
  76.8 1.9 %project.1 = (bf16[2,512,512]{2,1,0:T(8,128)(2,1)S(1)}, bf16[2,512,512]{2,1,0:T(8,128)(2,1)S(1)}) custom-call(s32[3]{0:T(128)S(1)} %pad_add_fusion.refs_0_, bf16[512,2048]{1,0:T(8,128)(2,1)S(1)} %copy-done.1, bf16[512,128]{1,0:T(8,128)(2,1)S(1)} %get-tuple-element.80.refs_11_.refs_2_, bf16[512,128]{1,0:T(8,128)(2,1)S(1)} %collective-permute-done.10.refs_3_, ...), custom_call_target="tpu_custom_call" | custom-call | flops 1000 | bytes 1000 | tf_op jit(solution)/shard_map/project/pallas_call | solution.py:47
  79.4 2.9 %collective-permute-start.19 = (bf16[1536,128]{1,0:T(8,128)(2,1)S(1)}, bf16[1536,128]{1,0:T(8,128)(2,1)S(1)}, u32[]{:S(2)}, u32[]{:S(2)}) collective-permute-start(bf16[1536,128]{1,0:T(8,128)(2,1)S(1)} %get-tuple-element.98), channel_id=1, source_target_pairs={{0,12},{4,8},{8,4},{12,0},{16,28},{20,24},{24,20},{28,16},{1,13},{... | collective-permute-start | bytes 1179656 | tf_op jit(solution)/shard_map/ppermute | solution.py:430
  84.3 6.0 %collective-permute-done.17.refs_2_ = bf16[1536,128]{1,0:T(8,128)(2,1)S(1)} collective-permute-done((bf16[1536,128]{1,0:T(8,128)(2,1)S(1)}, bf16[1536,128]{1,0:T(8,128)(2,1)S(1)}, u32[]{:S(2)}, u32[]{:S(2)}) %collective-permute-start.17) | collective-permute-done | bytes 393248 | tf_op jit(solution)/shard_map/ppermute | solution.py:430
  90.8 9.1 %collective-permute-done.19.refs_4_ = bf16[1536,128]{1,0:T(8,128)(2,1)S(1)} collective-permute-done((bf16[1536,128]{1,0:T(8,128)(2,1)S(1)}, bf16[1536,128]{1,0:T(8,128)(2,1)S(1)}, u32[]{:S(2)}, u32[]{:S(2)}) %collective-permute-start.19) | collective-permute-done | bytes 393248 | tf_op jit(solution)/shard_map/ppermute | solution.py:430
  99.9 1.9 %join_grads.1 = (bf16[512,512]{1,0:T(8,128)(2,1)}, bf16[512,512]{1,0:T(8,128)(2,1)}, bf16[512,512]{1,0:T(8,128)(2,1)}) custom-call(s32[3]{0:T(128)S(1)} %pad_add_fusion.refs_0_, bf16[1536,128]{1,0:T(8,128)(2,1)S(1)} %get-tuple-element.93.refs_6_.refs_1_, bf16[1536,128]{1,0:T(8,128)(2,1)S(1)} %collective-permute-done.17.refs_2_, ...), custom_call_target="tpu_custom_call" | custom-call | flops 13800000512 | bytes 1000 | tf_op jit(solution)/shard_map/join_grads/pallas_call | solution.py:47
  (60 shorter events, 23.5 us)
Async XLA Ops:
  3.6 15.8 %collective-permute-start.3 = (bf16[1024,128]{1,0:T(8,128)(2,1)S(1)}, bf16[1024,128]{1,0:T(8,128)(2,1)S(1)}, u32[]{:S(2)}, u32[]{:S(2)}) collective-permute-start(bf16[1024,128]{1,0:T(8,128)(2,1)S(1)} %get-tuple-element.58), channel_id=1, source_target_pairs={{0,4},{4,0},{8,12},{12,8},{16,20},{20,16},{24,28},{28,24},{1,5},{5... | collective-permute-start | bytes 786440 | tf_op jit(solution)/shard_map/ppermute | solution.py:430
  6.7 12.9 %collective-permute-start.4 = (bf16[1024,128]{1,0:T(8,128)(2,1)S(1)}, bf16[1024,128]{1,0:T(8,128)(2,1)S(1)}, u32[]{:S(2)}, u32[]{:S(2)}) collective-permute-start(bf16[1024,128]{1,0:T(8,128)(2,1)S(1)} %get-tuple-element.59), channel_id=1, source_target_pairs={{0,8},{4,12},{8,0},{12,4},{16,24},{20,28},{24,16},{28,20},{1,9},{5... | collective-permute-start | bytes 786440 | tf_op jit(solution)/shard_map/ppermute | solution.py:430
  8.3 12.2 %collective-permute-start.5 = (bf16[1024,128]{1,0:T(8,128)(2,1)S(1)}, bf16[1024,128]{1,0:T(8,128)(2,1)S(1)}, u32[]{:S(2)}, u32[]{:S(2)}) collective-permute-start(bf16[1024,128]{1,0:T(8,128)(2,1)S(1)} %get-tuple-element.60), channel_id=1, source_target_pairs={{0,12},{4,8},{8,4},{12,0},{16,28},{20,24},{24,20},{28,16},{1,13},{... | collective-permute-start | bytes 786440 | tf_op jit(solution)/shard_map/ppermute | solution.py:430
  8.3 1.6 %copy-start = (bf16[512,2048]{1,0:T(8,128)(2,1)S(1)}, bf16[512,2048]{1,0:T(8,128)(2,1)}, u32[]{:S(2)}) copy-start(bf16[512,2048]{1,0:T(8,128)(2,1)} %refs_1_.5) | copy-start | bytes 6291460
  9.8 1.6 %copy-start.2 = (bf16[512,2048]{1,0:T(8,128)(2,1)S(1)}, bf16[512,2048]{1,0:T(8,128)(2,1)}, u32[]{:S(2)}) copy-start(bf16[512,2048]{1,0:T(8,128)(2,1)} %refs_2_.3) | copy-start | bytes 6291460
  13.2 6.3 %copy-start.8 = (s32[256]{0:T(256)S(1)}, s32[256]{0:T(256)}, u32[]{:S(2)}) copy-start(s32[256]{0:T(256)} %param.12) | copy-start | bytes 3076
  15.9 13.7 %collective-permute-start = (bf16[1040,128]{1,0:T(8,128)(2,1)}, bf16[1040,128]{1,0:T(8,128)(2,1)S(1)}, u32[]{:S(2)}, u32[]{:S(2)}) collective-permute-start(bf16[1040,128]{1,0:T(8,128)(2,1)} %get-tuple-element.55), channel_id=1, source_target_pairs={{0,4},{4,0},{8,12},{12,8},{16,20},{20,16},{24,28},{28,24},{1,5},{5... | collective-permute-start | bytes 798728 | tf_op jit(solution)/shard_map/ppermute | solution.py:430
  17.9 11.8 %collective-permute-start.1 = (bf16[1040,128]{1,0:T(8,128)(2,1)}, bf16[1040,128]{1,0:T(8,128)(2,1)S(1)}, u32[]{:S(2)}, u32[]{:S(2)}) collective-permute-start(bf16[1040,128]{1,0:T(8,128)(2,1)} %get-tuple-element.56), channel_id=1, source_target_pairs={{0,8},{4,12},{8,0},{12,4},{16,24},{20,28},{24,16},{28,20},{1,9},{5... | collective-permute-start | bytes 798728 | tf_op jit(solution)/shard_map/ppermute | solution.py:430
  19.4 12.9 %collective-permute-start.2 = (bf16[1040,128]{1,0:T(8,128)(2,1)}, bf16[1040,128]{1,0:T(8,128)(2,1)S(1)}, u32[]{:S(2)}, u32[]{:S(2)}) collective-permute-start(bf16[1040,128]{1,0:T(8,128)(2,1)} %get-tuple-element.57), channel_id=1, source_target_pairs={{0,12},{4,8},{8,4},{12,0},{16,28},{20,24},{24,20},{28,16},{1,13},{... | collective-permute-start | bytes 798728 | tf_op jit(solution)/shard_map/ppermute | solution.py:430
  23.7 16.1 %collective-permute-start.6 = (bf16[512,128]{1,0:T(8,128)(2,1)S(1)}, bf16[512,128]{1,0:T(8,128)(2,1)S(1)}, u32[]{:S(2)}, u32[]{:S(2)}) collective-permute-start(bf16[512,128]{1,0:T(8,128)(2,1)S(1)} %get-tuple-element.61.refs_7_), channel_id=1, source_target_pairs={{0,16},{4,20},{8,24},{12,28},{1,17},{5,21},{9,25},{13,29},{2,18},{... | collective-permute-start | bytes 393224 | tf_op jit(solution)/shard_map/ppermute | solution.py:445
  28.4 15.6 %collective-permute-start.7 = (bf16[768,128]{1,0:T(8,128)(2,1)}, bf16[768,128]{1,0:T(8,128)(2,1)S(1)}, u32[]{:S(2)}, u32[]{:S(2)}) collective-permute-start(bf16[768,128]{1,0:T(8,128)(2,1)} %copy-done.10), channel_id=1, source_target_pairs={{0,16},{4,20},{8,24},{12,28},{1,17},{5,21},{9,25},{13,29},{2,18},{... | collective-permute-start | bytes 589832 | tf_op jit(solution)/shard_map/ppermute | solution.py:451
  33.3 10.6 %collective-permute-start.8 = (bf16[512,128]{1,0:T(8,128)(2,1)S(1)}, bf16[512,128]{1,0:T(8,128)(2,1)S(1)}, u32[]{:S(2)}, u32[]{:S(2)}) collective-permute-start(bf16[512,128]{1,0:T(8,128)(2,1)S(1)} %get-tuple-element.73), channel_id=1, source_target_pairs={{0,16},{4,20},{8,24},{12,28},{1,17},{5,21},{9,25},{13,29},{2,18},{... | collective-permute-start | bytes 393224 | tf_op jit(solution)/shard_map/ppermute | solution.py:445
  49.5 6.3 %collective-permute-start.9 = (bf16[144,256]{1,0:T(8,128)(2,1)S(1)}, bf16[144,256]{1,0:T(8,128)(2,1)S(1)}, u32[]{:S(2)}, u32[]{:S(2)}) collective-permute-start(bf16[144,256]{1,0:T(8,128)(2,1)S(1)} %row_forward.1.refs_6_.refs_4_.refs_3_), channel_id=1, source_target_pairs={{0,16},{4,20},{8,24},{12,28},{16,0},{20,4},{24,8},{28,12},{1,17},{... | collective-permute-start | bytes 221192 | tf_op jit(solution)/shard_map/ppermute | solution.py:454
  54.3 17.8 %collective-permute-start.13 = (bf16[768,128]{1,0:T(8,128)(2,1)S(1)}, bf16[768,128]{1,0:T(8,128)(2,1)S(1)}, u32[]{:S(2)}, u32[]{:S(2)}) collective-permute-start(bf16[768,128]{1,0:T(8,128)(2,1)S(1)} %get-tuple-element.76.refs_4_), channel_id=1, source_target_pairs={{16,0},{20,4},{24,8},{28,12},{17,1},{21,5},{25,9},{29,13},{18,2},{... | collective-permute-start | bytes 589832 | tf_op jit(solution)/shard_map/ppermute | solution.py:451
  58.0 17.2 %collective-permute-start.14 = (bf16[768,128]{1,0:T(8,128)(2,1)S(1)}, bf16[768,128]{1,0:T(8,128)(2,1)S(1)}, u32[]{:S(2)}, u32[]{:S(2)}) collective-permute-start(bf16[768,128]{1,0:T(8,128)(2,1)S(1)} %get-tuple-element.79.refs_5_.refs_8_), channel_id=1, source_target_pairs={{16,0},{20,4},{24,8},{28,12},{17,1},{21,5},{25,9},{29,13},{18,2},{... | collective-permute-start | bytes 589832 | tf_op jit(solution)/shard_map/ppermute | solution.py:616
  60.2 16.4 %collective-permute-start.10 = (bf16[512,128]{1,0:T(8,128)(2,1)S(1)}, bf16[512,128]{1,0:T(8,128)(2,1)S(1)}, u32[]{:S(2)}, u32[]{:S(2)}) collective-permute-start(bf16[512,128]{1,0:T(8,128)(2,1)S(1)} %get-tuple-element.81), channel_id=1, source_target_pairs={{0,4},{4,0},{8,12},{12,8},{16,20},{20,16},{24,28},{28,24},{1,5},{5... | collective-permute-start | bytes 393224 | tf_op jit(solution)/shard_map/ppermute | solution.py:430
  60.3 16.3 %collective-permute-start.11 = (bf16[512,128]{1,0:T(8,128)(2,1)S(1)}, bf16[512,128]{1,0:T(8,128)(2,1)S(1)}, u32[]{:S(2)}, u32[]{:S(2)}) collective-permute-start(bf16[512,128]{1,0:T(8,128)(2,1)S(1)} %get-tuple-element.82), channel_id=1, source_target_pairs={{0,8},{4,12},{8,0},{12,4},{16,24},{20,28},{24,16},{28,20},{1,9},{5... | collective-permute-start | bytes 393224 | tf_op jit(solution)/shard_map/ppermute | solution.py:430
  67.2 9.4 %collective-permute-start.12 = (bf16[512,128]{1,0:T(8,128)(2,1)S(1)}, bf16[512,128]{1,0:T(8,128)(2,1)S(1)}, u32[]{:S(2)}, u32[]{:S(2)}) collective-permute-start(bf16[512,128]{1,0:T(8,128)(2,1)S(1)} %get-tuple-element.83), channel_id=1, source_target_pairs={{0,12},{4,8},{8,4},{12,0},{16,28},{20,24},{24,20},{28,16},{1,13},{... | collective-permute-start | bytes 393224 | tf_op jit(solution)/shard_map/ppermute | solution.py:430
  75.2 1.6 %copy-start.1 = (bf16[512,2048]{1,0:T(8,128)(2,1)S(1)}, bf16[512,2048]{1,0:T(8,128)(2,1)}, u32[]{:S(2)}) copy-start(bf16[512,2048]{1,0:T(8,128)(2,1)} %refs_1_.5) | copy-start | bytes 6291460
  78.7 3.6 %collective-permute-start.15 = (bf16[2,512,512]{2,1,0:T(8,128)(2,1)S(1)}, bf16[2,512,512]{2,1,0:T(8,128)(2,1)S(1)}, u32[]{:S(2)}, u32[]{:S(2)}) collective-permute-start(bf16[2,512,512]{2,1,0:T(8,128)(2,1)S(1)} %get-tuple-element.95), channel_id=1, source_target_pairs={{0,1},{1,0},{2,3},{3,2},{4,5},{5,4},{6,7},{7,6},{8,9},{9,8},{10,11... | collective-permute-start | bytes 3145736 | tf_op jit(solution)/shard_map/ppermute | solution.py:648
  78.8 11.5 %collective-permute-start.17 = (bf16[1536,128]{1,0:T(8,128)(2,1)S(1)}, bf16[1536,128]{1,0:T(8,128)(2,1)S(1)}, u32[]{:S(2)}, u32[]{:S(2)}) collective-permute-start(bf16[1536,128]{1,0:T(8,128)(2,1)S(1)} %get-tuple-element.96), channel_id=1, source_target_pairs={{0,4},{4,0},{8,12},{12,8},{16,20},{20,16},{24,28},{28,24},{1,5},{5... | collective-permute-start | bytes 1179656 | tf_op jit(solution)/shard_map/ppermute | solution.py:430
  78.9 12.0 %collective-permute-start.18 = (bf16[1536,128]{1,0:T(8,128)(2,1)S(1)}, bf16[1536,128]{1,0:T(8,128)(2,1)S(1)}, u32[]{:S(2)}, u32[]{:S(2)}) collective-permute-start(bf16[1536,128]{1,0:T(8,128)(2,1)S(1)} %get-tuple-element.97), channel_id=1, source_target_pairs={{0,8},{4,12},{8,0},{12,4},{16,24},{20,28},{24,16},{28,20},{1,9},{5... | collective-permute-start | bytes 1179656 | tf_op jit(solution)/shard_map/ppermute | solution.py:430
  79.4 20.5 %collective-permute-start.19 = (bf16[1536,128]{1,0:T(8,128)(2,1)S(1)}, bf16[1536,128]{1,0:T(8,128)(2,1)S(1)}, u32[]{:S(2)}, u32[]{:S(2)}) collective-permute-start(bf16[1536,128]{1,0:T(8,128)(2,1)S(1)} %get-tuple-element.98), channel_id=1, source_target_pairs={{0,12},{4,8},{8,4},{12,0},{16,28},{20,24},{24,20},{28,16},{1,13},{... | collective-permute-start | bytes 1179656 | tf_op jit(solution)/shard_map/ppermute | solution.py:430
  82.7 19.2 %collective-permute-start.16 = (bf16[512,512]{1,0:T(8,128)(2,1)S(1)}, bf16[512,512]{1,0:T(8,128)(2,1)S(1)}, u32[]{:S(2)}, u32[]{:S(2)}) collective-permute-start(bf16[512,512]{1,0:T(8,128)(2,1)S(1)} %fusion.2), channel_id=1, source_target_pairs={{0,2},{1,3},{2,0},{3,1},{4,6},{5,7},{6,4},{7,5},{8,10},{9,11},{10,... | collective-permute-start | bytes 1572872 | tf_op jit(solution)/shard_map/ppermute | solution.py:650
  (7 other events, 6.1 us)

commit v2 on v1

--- a/solution.py
+++ b/solution.py
@@ -18,6 +18,7 @@
 BF = jnp.bfloat16
 F32 = jnp.float32
 NEG = float("-inf")
+FLOOR = -1e30
 JOIN_US = 12.0
 PACK_MIB = 14
 
@@ -28,10 +29,6 @@
 
 def nt(a, b):
     return lax.dot_general(a, b, (((1,), (1,)), ((), ())), preferred_element_type=F32)
-
-
-def tn(a, b):
-    return lax.dot_general(a, b, (((0,), (0,)), ((), ())), preferred_element_type=F32)
 
 
 def rows(slot, count):
@@ -126,6 +123,11 @@
     key_bias[...] = jnp.where(hidden, NEG, jnp.zeros(key_bias.shape, F32))
 
 
+def turn_body(ids, k, v, kt, vt):
+    kt[...] = k[...].T
+    vt[...] = v[...].T
+
+
 def join_qo_body(ids, pos_col, pos_row, *refs):
     pieces, (q, d_attn, bias, picked) = refs[:-4], refs[-4:]
     tok = q.shape[0] // len(pieces)
@@ -154,7 +156,8 @@
         picked[...] = jnp.zeros_like(picked)
 
 
-def row_forward_body(ids, picked, k, v, mine, scores):
+def row_forward_body(ids, own, sent, k, v, vt, mine, scores):
+    picked = ours(ids, own, sent)
     n = picked.shape[0] // 2
     step = 512
     query, d_out = picked[0:n, :], picked[n:, :]
@@ -172,7 +175,7 @@
         vals = v[c : c + step, :]
         mass = mass + jnp.sum(e, axis=0, keepdims=True)
         dot = dot + jnp.sum(e * nt(vals, d_out), axis=0, keepdims=True)
-        numer = numer + tn(vals, e.astype(BF))
+        numer = numer + nn(vt[:, c : c + step], e.astype(BF))
     mine[0:HEAD_DIM, :] = (numer / mass).astype(BF)
     mine[HEAD_DIM:, :] = in_thirds((peak, mass, dot))
 
@@ -214,31 +217,38 @@
 N_KEYS = RIM + QROWS
 
 
-def window_keys(sb, k, v, rim):
+def window_span(sb):
     first = sb * QROWS - RIM
     cut = max(0, -first)
-    inner = slice(first + cut, (sb + 1) * QROWS)
-    kw, vw = k[inner, :], v[inner, :]
-    if cut:
-        kw = jnp.concatenate([rim[RIM - cut : RIM, :], kw], axis=0)
-        vw = jnp.concatenate([rim[2 * RIM - cut :, :], vw], axis=0)
-    return first, cut, inner, kw, vw
+    return first, cut, slice(first + cut, (sb + 1) * QROWS)
+
+
+def window_rows(sb, own, rim):
+    _, cut, inner = window_span(sb)
+    if not cut:
+        return own[inner, :]
+    return jnp.concatenate([rim[RIM - cut : RIM, :], own[inner, :]], axis=0)
+
+
+def window_cols(sb, own_t, rim):
+    _, cut, inner = window_span(sb)
+    if not cut:
+        return own_t[:, inner]
+    return jnp.concatenate([rim[RIM - cut : RIM, :].T, own_t[:, inner]], axis=1)
 
 
 def window_forward_body(steps, with_rim, ids, *refs):
-    q, d_out, k, v, picked, bias, key_bias = refs[:7]
-    rim = refs[7] if with_rim else None
-    attn, weights, delta = refs[-3:]
-    n = picked.shape[0] // 2
-    kg, vg = picked[0:n, :], picked[n:, :]
+    q, k, vt, bias, key_bias = refs[:5]
+    k_rim, v_rim = (refs[5].at[0:RIM], refs[5].at[RIM:]) if with_rim else (None, None)
+    weights, out_t, peaks, masses = refs[-4:]
     key_in = lax.broadcasted_iota(jnp.int32, (BLOCK, QROWS), 0)
     query_in = lax.broadcasted_iota(jnp.int32, (BLOCK, QROWS), 1)
     shut = jnp.full((1, BLOCK), NEG, F32)
     for sb in steps:
         here = slice(sb * QROWS, (sb + 1) * QROWS)
-        first, _, _, kw, vw = window_keys(sb, k, v, rim)
-        qb = q[here, :]
-        raw = nt(kw, qb)
+        first = window_span(sb)[0]
+        kw, vwt = window_rows(sb, k, k_rim), window_cols(sb, vt, v_rim)
+        raw = nt(kw, q[here, :])
         parts = []
         for kb in range(N_KEYS // BLOCK):
             halves = []
@@ -255,47 +265,78 @@
             if own >= 0:
                 part = jnp.where(query_in - key_in >= own * BLOCK, part, NEG)
             parts.append(part)
-        parts.append(nt(kg, qb) * SCALE2)
-        peak = parts[0].max(axis=0, keepdims=True)
-        for part in parts[1:]:
+        peak = jnp.full((1, QROWS), FLOOR, F32)
+        for part in parts:
             peak = jnp.maximum(peak, part.max(axis=0, keepdims=True))
         grown = [jnp.exp2(part - peak) for part in parts]
-        mass = sum(e.sum(axis=0, keepdims=True) for e in grown)
-        inv = 1.0 / mass
-        ww = jnp.concatenate([(e * inv).astype(BF) for e in grown], axis=0)
-        weights[sb * (N_KEYS + n) : (sb + 1) * (N_KEYS + n), :] = ww
-        out_t = tn(vw, ww[0:N_KEYS, :]) + tn(vg, ww[N_KEYS:, :])
-        out = out_t.T.astype(BF)
-        attn[here, :] = out
-        dot = out_t.astype(BF).astype(F32) * d_out[here, :].astype(F32).T
-        delta[sb : sb + 1, :] = jnp.sum(dot, axis=0, keepdims=True)
+        masses[sb : sb + 1, :] = sum(e.sum(axis=0, keepdims=True) for e in grown)
+        peaks[sb : sb + 1, :] = peak
+        ww = jnp.concatenate([e.astype(BF) for e in grown], axis=0)
+        weights[sb * N_KEYS : (sb + 1) * N_KEYS, :] = ww
+        out_t[sb * HEAD_DIM : (sb + 1) * HEAD_DIM, :] = nn(vwt, ww)
+
+
+def ours(ids, mine, sent):
+    return jnp.where(ids[1] < ids[3], mine[...], sent[...])
+
+
+def glob_forward_body(ids, q, d_out, picked, out_t, peaks, masses, *refs):
+    attn, weights, d_win, d_glob, delta_win, delta_glob = refs
+    n = picked.shape[0] // 2
+    kg, vgt = picked[0:n, :], picked[n:, :].T
+    for sb in range(peaks.shape[0]):
+        here = slice(sb * QROWS, (sb + 1) * QROWS)
+        row = slice(sb, sb + 1)
+        score = nt(kg, q[here, :]) * SCALE2
+        peak = jnp.maximum(peaks[row, :], score.max(axis=0, keepdims=True))
+        grown = jnp.exp2(score - peak)
+        part = jnp.exp2(peaks[row, :] - peak)
+        inv = 1.0 / (masses[row, :] * part + grown.sum(axis=0, keepdims=True))
+        part = part * inv
+        wg = grown.astype(BF)
+        weights[sb * n : (sb + 1) * n, :] = wg
+        both = out_t[sb * HEAD_DIM : (sb + 1) * HEAD_DIM, :] * part + nn(vgt, wg) * inv
+        attn[here, :] = both.T.astype(BF)
+        d_t = d_out[here, :].astype(F32).T
+        delta = jnp.sum(both.astype(BF).astype(F32) * d_t, axis=0, keepdims=True)
+        d_win[here, :] = (d_t * part).T.astype(BF)
+        d_glob[here, :] = (d_t * inv).T.astype(BF)
+        delta_win[row, :] = delta * part
+        delta_glob[row, :] = delta * inv
 
 
 def glob_backward_body(ids, q, d_out, picked, weights, delta, dq_part, dk_glob, dv_glob):
     n = picked.shape[0] // 2
     n_steps = delta.shape[0]
-    kg, vg = picked[0:n, :], picked[n:, :]
-    dk_glob[...] = jnp.zeros_like(dk_glob)
-    dv_glob[...] = jnp.zeros_like(dv_glob)
-    for sb in range(n_steps):
-        here = slice(sb * QROWS, (sb + 1) * QROWS)
+    kt, vg = picked[0:n, :].T, picked[n:, :]
+    wide = 2
+    dkg = jnp.zeros(dk_glob.shape, F32)
+    dvg = jnp.zeros(dv_glob.shape, F32)
+    for c in range(0, n_steps, wide):
+        here = slice(c * QROWS, (c + wide) * QROWS)
         qb, dob = q[here, :], d_out[here, :]
-        wg = weights[sb * (N_KEYS + n) + N_KEYS : (sb + 1) * (N_KEYS + n), :]
-        dg = (wg.astype(F32) * (nt(vg, dob) - delta[sb : sb + 1, :])).astype(BF)
-        dq_part[sb * HEAD_DIM : (sb + 1) * HEAD_DIM, :] = tn(kg, dg)
-        dk_glob[...] += nn(dg, qb)
-        dv_glob[...] += nn(wg, dob)
-
-
-def window_backward_body(steps, n, with_rim, ids, *refs):
-    q, d_out, k, v, weights, delta = refs[:6]
+        wg = jnp.concatenate(
+            [weights[sb * n : (sb + 1) * n, :] for sb in range(c, c + wide)], axis=1
+        )
+        off = jnp.concatenate([delta[sb : sb + 1, :] for sb in range(c, c + wide)], axis=1)
+        dg = (wg.astype(F32) * (nt(vg, dob) - off)).astype(BF)
+        dq_t = nn(kt, dg)
+        for i in range(wide):
+            dq_part[(c + i) * HEAD_DIM : (c + i + 1) * HEAD_DIM, :] = dq_t[:, i * QROWS : (i + 1) * QROWS]
+        dkg = dkg + nn(dg, qb)
+        dvg = dvg + nn(wg, dob)
+    dk_glob[...] = dkg
+    dv_glob[...] = dvg
+
+
+def window_backward_body(steps, with_rim, ids, *refs):
+    q, d_out, kt, v, weights, delta = refs[:6]
+    k_rim, v_rim = (refs[6].at[0:RIM], refs[6].at[RIM:]) if with_rim else (None, None)
     if with_rim:
-        rim = refs[6]
         dq_rim, dk, dv, rim_back, dk_rim, dv_rim = refs[-6:]
         for ref in (dk, dv, dk_rim, dv_rim):
             ref[...] = jnp.zeros_like(ref)
     else:
-        rim = None
         dq_part, dq_rim = refs[6:8]
         dk, dv, dq = refs[-3:]
         for sb in range(dq_rim.shape[0] // HEAD_DIM):
@@ -304,16 +345,16 @@
             dq[sb * QROWS : (sb + 1) * QROWS, :] = (dq_t.T * SCALE).astype(BF)
     for sb in steps:
         here = slice(sb * QROWS, (sb + 1) * QROWS)
-        _, cut, inner, kw, vw = window_keys(sb, k, v, rim)
+        _, cut, inner = window_span(sb)
+        kwt, vw = window_cols(sb, kt, k_rim), window_rows(sb, v, v_rim)
         qb, dob = q[here, :], d_out[here, :]
-        at = sb * (N_KEYS + n)
-        ww = weights[at : at + N_KEYS, :]
+        ww = weights[sb * N_KEYS : (sb + 1) * N_KEYS, :]
         dw = (ww.astype(F32) * (nt(vw, dob) - delta[sb : sb + 1, :])).astype(BF)
         part = slice(sb * HEAD_DIM, (sb + 1) * HEAD_DIM)
         if with_rim:
-            dq_rim[part, :] = tn(kw, dw)
+            dq_rim[part, :] = nn(kwt, dw)
         else:
-            dq_t = tn(kw, dw) + dq_part[part, :]
+            dq_t = nn(kwt, dw) + dq_part[part, :]
             dq[here, :] = (dq_t.T * SCALE).astype(BF)
         dkw, dvw = nn(dw, qb), nn(ww, dob)
         if cut:
@@ -326,7 +367,8 @@
         rim_back[RIM:, :] = dv_rim[...].astype(BF)
 
 
-def row_backward_body(ids, picked, k, v, mine, other, dkg, dvg, dk, dv, sums):
+def row_backward_body(ids, own, sent, k, v, kt, mine, other, dkg, dvg, dk, dv, sums):
+    picked = ours(ids, own, sent)
     n = picked.shape[0] // 2
     step = 512
     query, d_out = picked[0:n, :], picked[n:, :]
@@ -340,7 +382,7 @@
         ds = (prob * (nt(vals, d_out) - delta)).astype(BF)
         dk[c : c + step, :] = nn(ds, query)
         dv[c : c + step, :] = nn(prob.astype(BF), d_out)
-        dq_t = dq_t + tn(keys, ds)
+        dq_t = dq_t + nn(kt[:, c : c + step], ds)
     sums[0:n, :] = (dq_t.T * SCALE).astype(BF)
     sums[n : 2 * n, :] = dkg[...].astype(BF)
     sums[2 * n :, :] = dvg[...].astype(BF)
@@ -421,7 +463,11 @@
     n_glob = global_pos.shape[0]
     seq_index = lax.axis_index("seq")
     group = seq_index // heads
-    ids = jnp.stack([seq_index % heads, group, lax.axis_index("head")]).astype(jnp.int32)
+    last = 1
+    while 2 * last < n_groups:
+        last *= 2
+    ids = jnp.stack([seq_index % heads, group, lax.axis_index("head"), jnp.int32(last)])
+    ids = ids.astype(jnp.int32)
     pos_col = global_pos.reshape(n_glob, 1)
     pos_row = global_pos.reshape(1, n_glob)
 
@@ -435,16 +481,18 @@
 
     def from_first(x):
         d = 1
-        while d < n_groups:
+        while True:
             route = [
                 (g * heads + j, (g + d) * heads + j)
                 for g in range(d)
                 for j in range(heads)
                 if g + d < n_groups
             ]
-            x = jnp.where((group >= d) & (group < 2 * d), lax.ppermute(x, "seq", route), x)
+            sent = lax.ppermute(x, "seq", route)
+            if 2 * d >= n_groups:
+                return x, sent
+            x = jnp.where((group >= d) & (group < 2 * d), sent, x)
             d *= 2
-        return x
 
     def to_next_group(x, step):
         route = [(s, s + step * heads) for s in range(n_seq) if 0 <= s + step * heads < n_seq]
@@ -493,7 +541,10 @@
             ((2 * RIM, HEAD_DIM), BF),
         ],
     )
-    kv_glob = from_first(picked)
+    kv_own, kv_sent = from_first(picked)
+    kv_glob = jnp.where(group >= last, kv_sent, kv_own)
+    kt, vt = local_call("turn", turn_body, ids, (k, v), [((HEAD_DIM, total), BF)] * 2)
+    rim_out, qo[2] = lax.optimization_barrier((rim_out, qo[2]))
     rim = to_next_group(rim_out, 1)
     q, d_attn, bias, qo_pick = local_call(
         "join_qo",
@@ -510,14 +561,14 @@
     )
     qo_glob = from_first(qo_pick)
     n_steps = total // QROWS
-    base = (q, d_attn, k, v, kv_glob)
+    base = (q, k, vt, bias, key_bias)
+    stat_rows = ((n_steps, QROWS), F32)
     forward_types = [
-        head_rows,
-        ((n_steps * (N_KEYS + n_glob), QROWS), BF),
-        ((n_steps, QROWS), F32),
+        ((n_steps * N_KEYS, QROWS), BF),
+        ((n_steps * HEAD_DIM, QROWS), F32),
+        stat_rows,
+        stat_rows,
     ]
-    backward_types = [head_rows, head_sums, head_sums, glob_sums, glob_sums]
-    rim_type = [((2 * RIM, HEAD_DIM), BF)]
 
     def window(name, body, args, state, outs, scratch=(), after=()):
         at = 1 + len(args)
@@ -536,21 +587,36 @@
     seen = window(
         "forward_inner",
         functools.partial(window_forward_body, range(2, n_steps), False),
-        base + (bias, key_bias),
+        base,
         (),
         forward_types,
     )
-    attn, weights, delta = window(
+    win_weights, *seen = window(
         "forward_rim",
         functools.partial(window_forward_body, range(0, 2), True),
-        base + (bias, key_bias, rim),
+        base + (rim,),
         seen,
         forward_types,
     )
-    backward = (q, d_attn, k, v, weights, delta)
+    attn, glob_weights, d_win, d_glob, delta_win, delta_glob = local_call(
+        "glob_forward",
+        glob_forward_body,
+        ids,
+        (q, d_attn, kv_glob, *seen),
+        [
+            head_rows,
+            ((n_steps * n_glob, QROWS), BF),
+            head_rows,
+            head_rows,
+            stat_rows,
+            stat_rows,
+        ],
+        mib=20,
+    )
+    backward = (q, d_win, kt, v, win_weights, delta_win)
     dq_rim, *state, rim_sum = window(
         "backward_rim",
-        functools.partial(window_backward_body, range(0, 2), n_glob, True),
+        functools.partial(window_backward_body, range(0, 2), True),
         backward + (rim,),
         (),
         [((2 * HEAD_DIM, QROWS), F32), head_sums, head_sums, ((2 * RIM, HEAD_DIM), BF)],
@@ -562,7 +628,7 @@
         "row_forward",
         row_forward_body,
         ids,
-        (qo_glob, k, v),
+        (*qo_glob, k, v, vt),
         [packed_rows],
         [pltpu.VMEM((total, n_glob), F32)],
         after=(rim_sum,),
@@ -576,7 +642,7 @@
         "glob_backward",
         glob_backward_body,
         ids,
-        (q, d_attn, kv_glob, weights, delta),
+        (q, d_glob, kv_glob, glob_weights, delta_glob),
         [((n_steps * HEAD_DIM, QROWS), F32), glob_sums, glob_sums],
         after=(mine,),
     )
@@ -584,7 +650,7 @@
         "row_backward",
         row_backward_body,
         ids,
-        (qo_glob, k, v, mine, other, dkg, dvg),
+        (*qo_glob, k, v, kt, mine, other, dkg, dvg),
         [head_sums, head_sums, ((3 * n_glob, HEAD_DIM), BF)],
     )
     attn_parts = swap_in_group(
@@ -600,7 +666,7 @@
     )
     dk, dv, dq = window(
         "backward_inner",
-        functools.partial(window_backward_body, range(2, n_steps), n_glob, False),
+        functools.partial(window_backward_body, range(2, n_steps), False),
         backward + (dq_part, dq_rim),
         state,
         [head_sums, head_sums, head_rows],

time: 103 us -> 101 us (0.981)
  Pallas kernels: 30 us -> 32.6 us
  waiting for transfers between devices: 23.4 us -> 20.8 us
  starting transfers between devices: 37.4 us -> 35.5 us
    ppermute x1, waiting for transfers between devices: 0.01 us -> 3.15 us  [with_group(): return lax.ppermute(x, 'seq', [(s, s ^ d * heads) for s in range(n_seq)])]
    ppermute x1, waiting for transfers between devices: 3.07 us -> 0.01 us  [to_lower(): return lax.ppermute(x, 'seq', route)]
    pallas_call x15 -> x17, Pallas kernels: 30 us -> 32.6 us  [local_call(): pl.pallas_call(kernel, name=name, out_shape=tuple((jax.ShapeDtypeStruct(s...]
    ppermute x1, starting transfers between devices: 1.84 us -> 0.07 us  [with_group(): return lax.ppermute(x, 'seq', [(s, s ^ d * heads) for s in range(n_seq)])]
    ppermute x12, waiting for transfers between devices: 19.1 us -> 17.6 us  [swap_in_group(): lax.ppermute(piece, 'seq', [(s, s ^ i) for s in range(n_seq)])]
    ppermute x2, waiting for transfers between devices: 1.23 us -> 0.01 us  [to_next_group(): return lax.ppermute(x, 'seq', route)]
  transfers between devices with their start and end apart: 20 -> 20, of which waited for: 7 -> 7; matrix products, arithmetic and copies ran while one was open for 1% -> 1% of each run, Pallas kernels for 21% -> 28%
where the time goes in v2:
time: 101 us
  starting transfers between devices  35.5 us (35%)
  Pallas kernels  32.6 us (32%)
  waiting for transfers between devices  20.8 us (21%)
  local copies, waits for them, and re-layouts  9.52 us (9%)
  other arithmetic  1.37 us (1%)
    pallas_call x17, Pallas kernels, local_call(): pl.pallas_call(kernel, name=name, out_shape=tuple((jax.ShapeDtypeStruct(s...  32.6 us
    ppermute x12, starting transfers between devices, swap_in_group(): lax.ppermute(piece, 'seq', [(s, s ^ i) for s in range(n_seq)])  18.5 us
    ppermute x12, waiting for transfers between devices, swap_in_group(): lax.ppermute(piece, 'seq', [(s, s ^ i) for s in range(n_seq)])  17.6 us
    ppermute x2, starting transfers between devices, from_first(): sent = lax.ppermute(x, 'seq', route)  10.3 us
    unnamed x22, local copies, waits for them, and re-layouts  9.32 us
    ppermute x2, starting transfers between devices, to_next_group(): return lax.ppermute(x, 'seq', route)  3.73 us
    ppermute x1, waiting for transfers between devices, with_group(): return lax.ppermute(x, 'seq', [(s, s ^ d * heads) for s in range(n_seq)])  3.15 us
  transfers between devices with their start and end apart: 20, of which 7 were waited for; matrix products, arithmetic and copies ran while one was open for 1% of the time, Pallas kernels for 28%

profile of v2, /device:TPU:0, one launch (start us, length us, event | category | flops | bytes accessed | tf_op | source)
XLA Modules:
  0.0 100.8 jit_solution(17412062473285938782)
XLA Ops:
  3.6 3.0 %collective-permute-start.1 = (bf16[1024,128]{1,0:T(8,128)(2,1)S(1)}, bf16[1024,128]{1,0:T(8,128)(2,1)S(1)}, u32[]{:S(2)}, u32[]{:S(2)}) collective-permute-start(bf16[1024,128]{1,0:T(8,128)(2,1)S(1)} %get-tuple-element.68), channel_id=1, source_target_pairs={{0,4},{4,0},{8,12},{12,8},{16,20},{20,16},{24,28},{28,24},{1,5},{5... | collective-permute-start | bytes 786440 | tf_op jit(solution)/shard_map/ppermute | solution.py:476
  6.7 1.6 %collective-permute-start.2 = (bf16[1024,128]{1,0:T(8,128)(2,1)S(1)}, bf16[1024,128]{1,0:T(8,128)(2,1)S(1)}, u32[]{:S(2)}, u32[]{:S(2)}) collective-permute-start(bf16[1024,128]{1,0:T(8,128)(2,1)S(1)} %get-tuple-element.69), channel_id=1, source_target_pairs={{0,8},{4,12},{8,0},{12,4},{16,24},{20,28},{24,16},{28,20},{1,9},{5... | collective-permute-start | bytes 786440 | tf_op jit(solution)/shard_map/ppermute | solution.py:476
  8.3 1.6 %copy-done = bf16[512,2048]{1,0:T(8,128)(2,1)S(1)} copy-done((bf16[512,2048]{1,0:T(8,128)(2,1)S(1)}, bf16[512,2048]{1,0:T(8,128)(2,1)}, u32[]{:S(2)}) %copy-start) | copy-done | bytes 2097176
  9.9 1.6 %copy-done.2 = bf16[512,2048]{1,0:T(8,128)(2,1)S(1)} copy-done((bf16[512,2048]{1,0:T(8,128)(2,1)S(1)}, bf16[512,2048]{1,0:T(8,128)(2,1)}, u32[]{:S(2)}) %copy-start.2) | copy-done | bytes 2097176
  13.2 2.8 %pack_qo.1 = (bf16[1040,128]{1,0:T(8,128)(2,1)S(1)}, bf16[1040,128]{1,0:T(8,128)(2,1)}, bf16[1040,128]{1,0:T(8,128)(2,1)}, bf16[1040,128]{1,0:T(8,128)(2,1)}) custom-call(s32[4]{0:T(128)S(1)} %pad_add_fusion.refs_0_, bf16[512,512]{1,0:T(8,128)(2,1)S(1)} %copy-done.3, bf16[512,2048]{1,0:T(8,128)(2,1)S(1)} %copy-done.2, bf16[512,2048]{1,0:T(8,128)(2,1)S(1)} %copy-done, ...), custom_call_target="tpu_custom_call" | custom-call | flops 1000 | bytes 1000 | tf_op jit(solution)/shard_map/pack_qo/pallas_call | solution.py:44
  15.9 2.0 %collective-permute-start.4 = (bf16[1040,128]{1,0:T(8,128)(2,1)}, bf16[1040,128]{1,0:T(8,128)(2,1)S(1)}, u32[]{:S(2)}, u32[]{:S(2)}) collective-permute-start(bf16[1040,128]{1,0:T(8,128)(2,1)} %get-tuple-element.72), channel_id=1, source_target_pairs={{0,8},{4,12},{8,0},{12,4},{16,24},{20,28},{24,16},{28,20},{1,9},{5... | collective-permute-start | bytes 798728 | tf_op jit(solution)/shard_map/ppermute | solution.py:476
  23.9 4.7 %collective-permute-start.6 = (bf16[512,128]{1,0:T(8,128)(2,1)S(1)}, bf16[512,128]{1,0:T(8,128)(2,1)S(1)}, u32[]{:S(2)}, u32[]{:S(2)}) collective-permute-start(bf16[512,128]{1,0:T(8,128)(2,1)S(1)} %get-tuple-element.75.refs_7_), channel_id=1, source_target_pairs={{0,16},{4,20},{8,24},{12,28},{1,17},{5,21},{9,25},{13,29},{2,18},{... | collective-permute-start | bytes 393224 | tf_op jit(solution)/shard_map/ppermute | solution.py:491
  29.5 2.3 %collective-permute-start.7 = (bf16[768,128]{1,0:T(8,128)(2,1)}, bf16[768,128]{1,0:T(8,128)(2,1)S(1)}, u32[]{:S(2)}, u32[]{:S(2)}) collective-permute-start(bf16[768,128]{1,0:T(8,128)(2,1)} %copy-done.10), channel_id=1, source_target_pairs={{0,16},{4,20},{8,24},{12,28},{1,17},{5,21},{9,25},{13,29},{2,18},{... | collective-permute-start | bytes 589832 | tf_op jit(solution)/shard_map/ppermute | solution.py:499
  33.1 5.6 %collective-permute-start.8 = (bf16[512,128]{1,0:T(8,128)(2,1)S(1)}, bf16[512,128]{1,0:T(8,128)(2,1)S(1)}, u32[]{:S(2)}, u32[]{:S(2)}) collective-permute-start(bf16[512,128]{1,0:T(8,128)(2,1)S(1)} %get-tuple-element.92.refs_1_), channel_id=1, source_target_pairs={{0,16},{4,20},{8,24},{12,28},{1,17},{5,21},{9,25},{13,29},{2,18},{... | collective-permute-start | bytes 393224 | tf_op jit(solution)/shard_map/ppermute | solution.py:491
  38.7 3.7 %forward_inner.1 = (bf16[5120,256]{1,0:T(8,128)(2,1)S(1)}, f32[1024,256]{1,0:T(8,128)S(1)}, f32[8,256]{1,0:T(8,128)S(1)}, f32[8,256]{1,0:T(8,128)S(1)}) custom-call(s32[4]{0:T(128)S(1)} %pad_add_fusion.refs_0_, bf16[2048,128]{1,0:T(8,128)(2,1)S(1)} %get-tuple-element.76.refs_1_, bf16[2048,128]{1,0:T(8,128)(2,1)S(1)} %get-tuple-element.78.refs_1_.refs_2_.refs_3_, ...), custom_call_target="tpu_custom_call" | custom-call | flops 1000 | bytes 1000 | tf_op jit(solution)/shard_map/forward_inner/pallas_call | solution.py:44
  42.4 1.7 %forward_rim.1 = (bf16[5120,256]{1,0:T(8,128)(2,1)S(1)}, f32[1024,256]{1,0:T(8,128)S(1)}, f32[8,256]{1,0:T(8,128)S(1)}, f32[8,256]{1,0:T(8,128)S(1)}) custom-call(s32[4]{0:T(128)S(1)} %pad_add_fusion.refs_0_, bf16[2048,128]{1,0:T(8,128)(2,1)S(1)} %get-tuple-element.76.refs_1_, ...), custom_call_target="tpu_custom_call", output_to_operand_aliasing={{0}: (7, {}), {1}: (8, {}), {2}: (9, {}), {3}: (10, {})} | custom-call | flops 1000 | bytes 1000 | tf_op jit(solution)/shard_map/forward_rim/pallas_call | solution.py:44
  44.1 3.1 %glob_forward.1 = (bf16[2048,128]{1,0:T(8,128)(2,1)S(1)}, bf16[2048,256]{1,0:T(8,128)(2,1)S(1)}, bf16[2048,128]{1,0:T(8,128)(2,1)S(1)}, bf16[2048,128]{1,0:T(8,1...) custom-call(s32[4]{0:T(128)S(1)} %pad_add_fusion.refs_0_, bf16[2048,128]{1,0:T(8,128)(2,1)S(1)} %get-tuple-element.76.refs_1_, ...), custom_call_target="tpu_custom_call" | custom-call | flops 1000 | bytes 1000 | tf_op jit(solution)/shard_map/glob_forward/pallas_call | solution.py:44
  47.2 1.8 %backward_rim.1 = (f32[256,256]{1,0:T(8,128)S(1)}, f32[2048,128]{1,0:T(8,128)S(1)}, f32[2048,128]{1,0:T(8,128)S(1)}, bf16[768,128]{1,0:T(8,128)(2,1)S(1)}) custom-call(s32[4]{0:T(128)S(1)} %pad_add_fusion.refs_0_, bf16[2048,128]{1,0:T(8,128)(2,1)S(1)} %get-tuple-element.76.refs_1_, bf16[2048,128]{1,0:T(8,128)(2,1)S(1)} %get-tuple-element.93.refs_2_, ...), custom_call_target="tpu_custom_call" | custom-call | flops 1000 | bytes 1000 | tf_op jit(solution)/shard_map/backward_rim/pallas_call | solution.py:44
  49.0 1.8 %row_forward.1.refs_6_.refs_3_ = bf16[144,256]{1,0:T(8,128)(2,1)S(1)} custom-call(s32[4]{0:T(128)S(1)} %pad_add_fusion.refs_0_, bf16[512,128]{1,0:T(8,128)(2,1)S(1)} %get-tuple-element.92.refs_1_, bf16[512,128]{1,0:T(8,128)(2,1)S(1)} %collective-permute-done.8.refs_2_, bf16[2048,128]{1,0:T(8,128)(2,1)S(1)} %get-tuple-element.78.refs_1_.refs_2_.refs_3_, ...), custom_call_target="tpu_custom_call" | custom-call | flops 1000 | bytes 1000 | tf_op jit(solution)/shard_map/row_forward/pallas_call | solution.py:44
  52.4 2.2 %glob_backward.1 = (f32[1024,256]{1,0:T(8,128)S(1)}, f32[256,128]{1,0:T(8,128)S(1)}, f32[256,128]{1,0:T(8,128)S(1)}) custom-call(s32[4]{0:T(128)S(1)} %pad_add_fusion.refs_0_, bf16[2048,128]{1,0:T(8,128)(2,1)S(1)} %get-tuple-element.76.refs_1_, bf16[2048,128]{1,0:T(8,128)(2,1)S(1)} %get-tuple-element.98.refs_2_, ...), custom_call_target="tpu_custom_call" | custom-call | flops 1000 | bytes 1000 | tf_op jit(solution)/shard_map/glob_backward/pallas_call | solution.py:44
  54.6 3.1 %collective-permute-done.9.refs_7_.refs_4_ = bf16[144,256]{1,0:T(8,128)(2,1)S(1)} collective-permute-done((bf16[144,256]{1,0:T(8,128)(2,1)S(1)}, bf16[144,256]{1,0:T(8,128)(2,1)S(1)}, u32[]{:S(2)}, u32[]{:S(2)}) %collective-permute-start.9) | collective-permute-done | bytes 73760 | tf_op jit(solution)/shard_map/ppermute | solution.py:502
  57.8 2.2 %row_backward.1 = (f32[2048,128]{1,0:T(8,128)S(1)}, f32[2048,128]{1,0:T(8,128)S(1)}, bf16[768,128]{1,0:T(8,128)(2,1)S(1)}) custom-call(s32[4]{0:T(128)S(1)} %pad_add_fusion.refs_0_, bf16[512,128]{1,0:T(8,128)(2,1)S(1)} %get-tuple-element.92.refs_1_, bf16[512,128]{1,0:T(8,128)(2,1)S(1)} %collective-permute-done.8.refs_2_, ...), custom_call_target="tpu_custom_call" | custom-call | flops 1000 | bytes 1000 | tf_op jit(solution)/shard_map/row_backward/pallas_call | solution.py:44
  62.3 6.3 %collective-permute-start.11 = (bf16[512,128]{1,0:T(8,128)(2,1)S(1)}, bf16[512,128]{1,0:T(8,128)(2,1)S(1)}, u32[]{:S(2)}, u32[]{:S(2)}) collective-permute-start(bf16[512,128]{1,0:T(8,128)(2,1)S(1)} %get-tuple-element.106), channel_id=1, source_target_pairs={{0,8},{4,12},{8,0},{12,4},{16,24},{20,28},{24,16},{28,20},{1,9},{5... | collective-permute-start | bytes 393224 | tf_op jit(solution)/shard_map/ppermute | solution.py:476
  69.0 3.7 %backward_inner.1 = (f32[2048,128]{1,0:T(8,128)S(1)}, f32[2048,128]{1,0:T(8,128)S(1)}, bf16[2048,128]{1,0:T(8,128)(2,1)S(1)}) custom-call(s32[4]{0:T(128)S(1)} %pad_add_fusion.refs_0_, bf16[2048,128]{1,0:T(8,128)(2,1)S(1)} %get-tuple-element.76.refs_1_, ...), custom_call_target="tpu_custom_call", output_to_operand_aliasing={{0}: (9, {}), {1}: (10, {})} | custom-call | flops 1000 | bytes 1000 | tf_op jit(solution)/shard_map/backward_inner/pallas_call | solution.py:44
  74.5 1.9 %project.1 = (bf16[2,512,512]{2,1,0:T(8,128)(2,1)S(1)}, bf16[2,512,512]{2,1,0:T(8,128)(2,1)S(1)}) custom-call(s32[4]{0:T(128)S(1)} %pad_add_fusion.refs_0_, bf16[512,2048]{1,0:T(8,128)(2,1)S(1)} %copy-done.1, bf16[512,128]{1,0:T(8,128)(2,1)S(1)} %get-tuple-element.104.refs_11_.refs_2_, bf16[512,128]{1,0:T(8,128)(2,1)S(1)} %collective-permute-done.10.refs_3_, ...), custom_call_target="tpu_custom_call" | custom-call | flops 1000 | bytes 1000 | tf_op jit(solution)/shard_map/project/pallas_call | solution.py:44
  82.0 6.0 %collective-permute-done.17.refs_2_ = bf16[1536,128]{1,0:T(8,128)(2,1)S(1)} collective-permute-done((bf16[1536,128]{1,0:T(8,128)(2,1)S(1)}, bf16[1536,128]{1,0:T(8,128)(2,1)S(1)}, u32[]{:S(2)}, u32[]{:S(2)}) %collective-permute-start.17) | collective-permute-done | bytes 393248 | tf_op jit(solution)/shard_map/ppermute | solution.py:476
  88.0 1.9 %collective-permute-done.18.refs_3_ = bf16[1536,128]{1,0:T(8,128)(2,1)S(1)} collective-permute-done((bf16[1536,128]{1,0:T(8,128)(2,1)S(1)}, bf16[1536,128]{1,0:T(8,128)(2,1)S(1)}, u32[]{:S(2)}, u32[]{:S(2)}) %collective-permute-start.18) | collective-permute-done | bytes 393248 | tf_op jit(solution)/shard_map/ppermute | solution.py:476
  89.9 7.9 %collective-permute-done.19.refs_4_ = bf16[1536,128]{1,0:T(8,128)(2,1)S(1)} collective-permute-done((bf16[1536,128]{1,0:T(8,128)(2,1)S(1)}, bf16[1536,128]{1,0:T(8,128)(2,1)S(1)}, u32[]{:S(2)}, u32[]{:S(2)}) %collective-permute-start.19) | collective-permute-done | bytes 393248 | tf_op jit(solution)/shard_map/ppermute | solution.py:476
  97.8 1.9 %join_grads.1 = (bf16[512,512]{1,0:T(8,128)(2,1)}, bf16[512,512]{1,0:T(8,128)(2,1)}, bf16[512,512]{1,0:T(8,128)(2,1)}) custom-call(s32[4]{0:T(128)S(1)} %pad_add_fusion.refs_0_, bf16[1536,128]{1,0:T(8,128)(2,1)S(1)} %get-tuple-element.117.refs_6_.refs_1_, bf16[1536,128]{1,0:T(8,128)(2,1)S(1)} %collective-permute-done.17.refs_2_, ...), custom_call_target="tpu_custom_call" | custom-call | flops 13800000512 | bytes 1000 | tf_op jit(solution)/shard_map/join_grads/pallas_call | solution.py:44
  (61 shorter events, 25.4 us)
Async XLA Ops:
  3.6 15.8 %collective-permute-start.1 = (bf16[1024,128]{1,0:T(8,128)(2,1)S(1)}, bf16[1024,128]{1,0:T(8,128)(2,1)S(1)}, u32[]{:S(2)}, u32[]{:S(2)}) collective-permute-start(bf16[1024,128]{1,0:T(8,128)(2,1)S(1)} %get-tuple-element.68), channel_id=1, source_target_pairs={{0,4},{4,0},{8,12},{12,8},{16,20},{20,16},{24,28},{28,24},{1,5},{5... | collective-permute-start | bytes 786440 | tf_op jit(solution)/shard_map/ppermute | solution.py:476
  6.7 12.9 %collective-permute-start.2 = (bf16[1024,128]{1,0:T(8,128)(2,1)S(1)}, bf16[1024,128]{1,0:T(8,128)(2,1)S(1)}, u32[]{:S(2)}, u32[]{:S(2)}) collective-permute-start(bf16[1024,128]{1,0:T(8,128)(2,1)S(1)} %get-tuple-element.69), channel_id=1, source_target_pairs={{0,8},{4,12},{8,0},{12,4},{16,24},{20,28},{24,16},{28,20},{1,9},{5... | collective-permute-start | bytes 786440 | tf_op jit(solution)/shard_map/ppermute | solution.py:476
  8.3 12.4 %collective-permute-start.3 = (bf16[1024,128]{1,0:T(8,128)(2,1)S(1)}, bf16[1024,128]{1,0:T(8,128)(2,1)S(1)}, u32[]{:S(2)}, u32[]{:S(2)}) collective-permute-start(bf16[1024,128]{1,0:T(8,128)(2,1)S(1)} %get-tuple-element.70), channel_id=1, source_target_pairs={{0,12},{4,8},{8,4},{12,0},{16,28},{20,24},{24,20},{28,16},{1,13},{... | collective-permute-start | bytes 786440 | tf_op jit(solution)/shard_map/ppermute | solution.py:476
  8.3 1.6 %copy-start = (bf16[512,2048]{1,0:T(8,128)(2,1)S(1)}, bf16[512,2048]{1,0:T(8,128)(2,1)}, u32[]{:S(2)}) copy-start(bf16[512,2048]{1,0:T(8,128)(2,1)} %refs_1_.5) | copy-start | bytes 6291460
  9.9 1.6 %copy-start.2 = (bf16[512,2048]{1,0:T(8,128)(2,1)S(1)}, bf16[512,2048]{1,0:T(8,128)(2,1)}, u32[]{:S(2)}) copy-start(bf16[512,2048]{1,0:T(8,128)(2,1)} %refs_2_.3) | copy-start | bytes 6291460
  13.2 6.3 %copy-start.8 = (s32[256]{0:T(256)S(1)}, s32[256]{0:T(256)}, u32[]{:S(2)}) copy-start(s32[256]{0:T(256)} %param.12) | copy-start | bytes 3076
  15.9 13.5 %collective-permute-start.4 = (bf16[1040,128]{1,0:T(8,128)(2,1)}, bf16[1040,128]{1,0:T(8,128)(2,1)S(1)}, u32[]{:S(2)}, u32[]{:S(2)}) collective-permute-start(bf16[1040,128]{1,0:T(8,128)(2,1)} %get-tuple-element.72), channel_id=1, source_target_pairs={{0,8},{4,12},{8,0},{12,4},{16,24},{20,28},{24,16},{28,20},{1,9},{5... | collective-permute-start | bytes 798728 | tf_op jit(solution)/shard_map/ppermute | solution.py:476
  17.9 13.8 %collective-permute-start = (bf16[1040,128]{1,0:T(8,128)(2,1)}, bf16[1040,128]{1,0:T(8,128)(2,1)S(1)}, u32[]{:S(2)}, u32[]{:S(2)}) collective-permute-start(bf16[1040,128]{1,0:T(8,128)(2,1)} %get-tuple-element.67), channel_id=1, source_target_pairs={{0,4},{4,0},{8,12},{12,8},{16,20},{20,16},{24,28},{28,24},{1,5},{5... | collective-permute-start | bytes 798728 | tf_op jit(solution)/shard_map/ppermute | solution.py:476
  19.4 12.7 %collective-permute-start.5 = (bf16[1040,128]{1,0:T(8,128)(2,1)}, bf16[1040,128]{1,0:T(8,128)(2,1)S(1)}, u32[]{:S(2)}, u32[]{:S(2)}) collective-permute-start(bf16[1040,128]{1,0:T(8,128)(2,1)} %get-tuple-element.74), channel_id=1, source_target_pairs={{0,12},{4,8},{8,4},{12,0},{16,28},{20,24},{24,20},{28,16},{1,13},{... | collective-permute-start | bytes 798728 | tf_op jit(solution)/shard_map/ppermute | solution.py:476
  23.9 18.5 %collective-permute-start.6 = (bf16[512,128]{1,0:T(8,128)(2,1)S(1)}, bf16[512,128]{1,0:T(8,128)(2,1)S(1)}, u32[]{:S(2)}, u32[]{:S(2)}) collective-permute-start(bf16[512,128]{1,0:T(8,128)(2,1)S(1)} %get-tuple-element.75.refs_7_), channel_id=1, source_target_pairs={{0,16},{4,20},{8,24},{12,28},{1,17},{5,21},{9,25},{13,29},{2,18},{... | collective-permute-start | bytes 393224 | tf_op jit(solution)/shard_map/ppermute | solution.py:491
  29.5 13.0 %collective-permute-start.7 = (bf16[768,128]{1,0:T(8,128)(2,1)}, bf16[768,128]{1,0:T(8,128)(2,1)S(1)}, u32[]{:S(2)}, u32[]{:S(2)}) collective-permute-start(bf16[768,128]{1,0:T(8,128)(2,1)} %copy-done.10), channel_id=1, source_target_pairs={{0,16},{4,20},{8,24},{12,28},{1,17},{5,21},{9,25},{13,29},{2,18},{... | collective-permute-start | bytes 589832 | tf_op jit(solution)/shard_map/ppermute | solution.py:499
  33.1 15.9 %collective-permute-start.8 = (bf16[512,128]{1,0:T(8,128)(2,1)S(1)}, bf16[512,128]{1,0:T(8,128)(2,1)S(1)}, u32[]{:S(2)}, u32[]{:S(2)}) collective-permute-start(bf16[512,128]{1,0:T(8,128)(2,1)S(1)} %get-tuple-element.92.refs_1_), channel_id=1, source_target_pairs={{0,16},{4,20},{8,24},{12,28},{1,17},{5,21},{9,25},{13,29},{2,18},{... | collective-permute-start | bytes 393224 | tf_op jit(solution)/shard_map/ppermute | solution.py:491
  50.8 6.9 %collective-permute-start.9 = (bf16[144,256]{1,0:T(8,128)(2,1)S(1)}, bf16[144,256]{1,0:T(8,128)(2,1)S(1)}, u32[]{:S(2)}, u32[]{:S(2)}) collective-permute-start(bf16[144,256]{1,0:T(8,128)(2,1)S(1)} %row_forward.1.refs_6_.refs_3_), channel_id=1, source_target_pairs={{0,16},{4,20},{8,24},{12,28},{16,0},{20,4},{24,8},{28,12},{1,17},{... | collective-permute-start | bytes 221192 | tf_op jit(solution)/shard_map/ppermute | solution.py:502
  50.9 21.8 %collective-permute-start.13 = (bf16[768,128]{1,0:T(8,128)(2,1)S(1)}, bf16[768,128]{1,0:T(8,128)(2,1)S(1)}, u32[]{:S(2)}, u32[]{:S(2)}) collective-permute-start(bf16[768,128]{1,0:T(8,128)(2,1)S(1)} %get-tuple-element.97.refs_6_), channel_id=1, source_target_pairs={{16,0},{20,4},{24,8},{28,12},{17,1},{21,5},{25,9},{29,13},{18,2},{... | collective-permute-start | bytes 589832 | tf_op jit(solution)/shard_map/ppermute | solution.py:499
  60.0 12.8 %collective-permute-start.14 = (bf16[768,128]{1,0:T(8,128)(2,1)S(1)}, bf16[768,128]{1,0:T(8,128)(2,1)S(1)}, u32[]{:S(2)}, u32[]{:S(2)}) collective-permute-start(bf16[768,128]{1,0:T(8,128)(2,1)S(1)} %get-tuple-element.103.refs_5_.refs_8_), channel_id=1, source_target_pairs={{16,0},{20,4},{24,8},{28,12},{17,1},{21,5},{25,9},{29,13},{18,2},{... | collective-permute-start | bytes 589832 | tf_op jit(solution)/shard_map/ppermute | solution.py:682
  62.2 12.0 %collective-permute-start.10 = (bf16[512,128]{1,0:T(8,128)(2,1)S(1)}, bf16[512,128]{1,0:T(8,128)(2,1)S(1)}, u32[]{:S(2)}, u32[]{:S(2)}) collective-permute-start(bf16[512,128]{1,0:T(8,128)(2,1)S(1)} %get-tuple-element.105), channel_id=1, source_target_pairs={{0,4},{4,0},{8,12},{12,8},{16,20},{20,16},{24,28},{28,24},{1,5},{5... | collective-permute-start | bytes 393224 | tf_op jit(solution)/shard_map/ppermute | solution.py:476
  62.3 11.9 %collective-permute-start.11 = (bf16[512,128]{1,0:T(8,128)(2,1)S(1)}, bf16[512,128]{1,0:T(8,128)(2,1)S(1)}, u32[]{:S(2)}, u32[]{:S(2)}) collective-permute-start(bf16[512,128]{1,0:T(8,128)(2,1)S(1)} %get-tuple-element.106), channel_id=1, source_target_pairs={{0,8},{4,12},{8,0},{12,4},{16,24},{20,28},{24,16},{28,20},{1,9},{5... | collective-permute-start | bytes 393224 | tf_op jit(solution)/shard_map/ppermute | solution.py:476
  68.6 5.9 %collective-permute-start.12 = (bf16[512,128]{1,0:T(8,128)(2,1)S(1)}, bf16[512,128]{1,0:T(8,128)(2,1)S(1)}, u32[]{:S(2)}, u32[]{:S(2)}) collective-permute-start(bf16[512,128]{1,0:T(8,128)(2,1)S(1)} %get-tuple-element.107), channel_id=1, source_target_pairs={{0,12},{4,8},{8,4},{12,0},{16,28},{20,24},{24,20},{28,16},{1,13},{... | collective-permute-start | bytes 393224 | tf_op jit(solution)/shard_map/ppermute | solution.py:476
  72.7 1.8 %copy-start.1 = (bf16[512,2048]{1,0:T(8,128)(2,1)S(1)}, bf16[512,2048]{1,0:T(8,128)(2,1)}, u32[]{:S(2)}) copy-start(bf16[512,2048]{1,0:T(8,128)(2,1)} %refs_1_.5) | copy-start | bytes 6291460
  76.4 3.6 %collective-permute-start.15 = (bf16[2,512,512]{2,1,0:T(8,128)(2,1)S(1)}, bf16[2,512,512]{2,1,0:T(8,128)(2,1)S(1)}, u32[]{:S(2)}, u32[]{:S(2)}) collective-permute-start(bf16[2,512,512]{2,1,0:T(8,128)(2,1)S(1)} %get-tuple-element.119), channel_id=1, source_target_pairs={{0,1},{1,0},{2,3},{3,2},{4,5},{5,4},{6,7},{7,6},{8,9},{9,8},{10,11... | collective-permute-start | bytes 3145736 | tf_op jit(solution)/shard_map/ppermute | solution.py:714
  76.5 11.5 %collective-permute-start.17 = (bf16[1536,128]{1,0:T(8,128)(2,1)S(1)}, bf16[1536,128]{1,0:T(8,128)(2,1)S(1)}, u32[]{:S(2)}, u32[]{:S(2)}) collective-permute-start(bf16[1536,128]{1,0:T(8,128)(2,1)S(1)} %get-tuple-element.120), channel_id=1, source_target_pairs={{0,4},{4,0},{8,12},{12,8},{16,20},{20,16},{24,28},{28,24},{1,5},{5... | collective-permute-start | bytes 1179656 | tf_op jit(solution)/shard_map/ppermute | solution.py:476
  78.0 12.0 %collective-permute-start.18 = (bf16[1536,128]{1,0:T(8,128)(2,1)S(1)}, bf16[1536,128]{1,0:T(8,128)(2,1)S(1)}, u32[]{:S(2)}, u32[]{:S(2)}) collective-permute-start(bf16[1536,128]{1,0:T(8,128)(2,1)S(1)} %get-tuple-element.121), channel_id=1, source_target_pairs={{0,8},{4,12},{8,0},{12,4},{16,24},{20,28},{24,16},{28,20},{1,9},{5... | collective-permute-start | bytes 1179656 | tf_op jit(solution)/shard_map/ppermute | solution.py:476
  79.5 18.3 %collective-permute-start.19 = (bf16[1536,128]{1,0:T(8,128)(2,1)S(1)}, bf16[1536,128]{1,0:T(8,128)(2,1)S(1)}, u32[]{:S(2)}, u32[]{:S(2)}) collective-permute-start(bf16[1536,128]{1,0:T(8,128)(2,1)S(1)} %get-tuple-element.122), channel_id=1, source_target_pairs={{0,12},{4,8},{8,4},{12,0},{16,28},{20,24},{24,20},{28,16},{1,13},{... | collective-permute-start | bytes 1179656 | tf_op jit(solution)/shard_map/ppermute | solution.py:476
  80.4 19.4 %collective-permute-start.16 = (bf16[512,512]{1,0:T(8,128)(2,1)S(1)}, bf16[512,512]{1,0:T(8,128)(2,1)S(1)}, u32[]{:S(2)}, u32[]{:S(2)}) collective-permute-start(bf16[512,512]{1,0:T(8,128)(2,1)S(1)} %fusion.2), channel_id=1, source_target_pairs={{0,2},{1,3},{2,0},{3,1},{4,6},{5,7},{6,4},{7,5},{8,10},{9,11},{10,... | collective-permute-start | bytes 1572872 | tf_op jit(solution)/shard_map/ppermute | solution.py:716
  (7 other events, 6.1 us)

commit v3 on v2

--- a/solution.py
+++ b/solution.py
@@ -57,6 +57,10 @@
             flops=1000 + int(us * 1.15e9), bytes_accessed=1000, transcendentals=0
         ),
     )(ids, *arrays, *[array for array, _ in far], *after)
+
+
+def in_hbm(x):
+    return pltpu.with_memory_space_constraint(x, pltpu.HBM)
 
 
 def pack_kv_body(ids, k, v, *refs):
@@ -508,7 +512,7 @@
         (),
         [((2 * tok, HEAD_DIM), BF)] * heads,
         [pltpu.SemaphoreType.DMA((2 * heads,))],
-        far=((keys, pltpu.HBM), (values, pltpu.HBM)),
+        far=((in_hbm(keys), pltpu.HBM), (in_hbm(values), pltpu.HBM)),
         mib=PACK_MIB,
         out_space=pltpu.VMEM,
     )

time: 101 us -> 100 us (0.990)
  local copies, waits for them, and re-layouts: 9.52 us -> 7.44 us
  Pallas kernels: 32.6 us -> 33.7 us
    unnamed x22 -> x18, local copies, waits for them, and re-layouts: 9.32 us -> 7.24 us
    pallas_call x17, Pallas kernels: 32.6 us -> 33.7 us  [local_call(): pl.pallas_call(kernel, name=name, out_shape=tuple((jax.ShapeDtypeStruct(s...]
where the time goes in v3:
time: 100 us; the launch traced here: 99.8 us
  starting transfers between devices  35.5 us (36%)
  Pallas kernels  33.7 us (34%)
  waiting for transfers between devices  20.8 us (21%)
  local copies, waits for them, and re-layouts  7.44 us (7%)
  other arithmetic  1.37 us (1%)
    pallas_call x17, Pallas kernels, local_call(): pl.pallas_call(kernel, name=name, out_shape=tuple((jax.ShapeDtypeStruct(s...  33.7 us
    ppermute x12, starting transfers between devices, swap_in_group(): lax.ppermute(piece, 'seq', [(s, s ^ i) for s in range(n_seq)])  18.5 us
    ppermute x12, waiting for transfers between devices, swap_in_group(): lax.ppermute(piece, 'seq', [(s, s ^ i) for s in range(n_seq)])  17.6 us
    ppermute x2, starting transfers between devices, from_first(): sent = lax.ppermute(x, 'seq', route)  10.3 us
    unnamed x18, local copies, waits for them, and re-layouts  7.24 us
    ppermute x2, starting transfers between devices, to_next_group(): return lax.ppermute(x, 'seq', route)  3.73 us
    ppermute x1, waiting for transfers between devices, with_group(): return lax.ppermute(x, 'seq', [(s, s ^ d * heads) for s in range(n_seq)])  3.15 us
  transfers between devices with their start and end apart: 20, of which 7 were waited for; matrix products, arithmetic and copies ran while one was open for 1% of the time, Pallas kernels for 28%

profile of v3, /device:TPU:0, one launch (start us, length us, event | category | flops | bytes accessed | tf_op | source)
XLA Modules:
  0.0 99.8 jit_solution(4047391203992963730)
XLA Ops:
  0.7 1.9 %pack_kv.1 = (bf16[1024,128]{1,0:T(8,128)(2,1)S(1)}, bf16[1024,128]{1,0:T(8,128)(2,1)S(1)}, bf16[1024,128]{1,0:T(8,128)(2,1)S(1)}, bf16[1024,128]{1,0:T(8,128)(2,1)S(1)}) custom-call(s32[4]{0:T(128)S(1)} %pad_add_fusion.refs_0_, bf16[512,512]{1,0:T(8,128)(2,1)} %refs_1_.3, bf16[512,512]{1,0:T(8,128)(2,1)} %refs_2_.2), custom_call_target="tpu_custom_call" | custom-call | flops 1000 | bytes 1000 | tf_op jit(solution)/shard_map/pack_kv/pallas_call | solution.py:44
  2.7 3.0 %collective-permute-start.1 = (bf16[1024,128]{1,0:T(8,128)(2,1)S(1)}, bf16[1024,128]{1,0:T(8,128)(2,1)S(1)}, u32[]{:S(2)}, u32[]{:S(2)}) collective-permute-start(bf16[1024,128]{1,0:T(8,128)(2,1)S(1)} %get-tuple-element.68), channel_id=1, source_target_pairs={{0,4},{4,0},{8,12},{12,8},{16,20},{20,16},{24,28},{28,24},{1,5},{5... | collective-permute-start | bytes 786440 | tf_op jit(solution)/shard_map/ppermute | solution.py:480
  7.3 1.6 %copy-done = bf16[512,2048]{1,0:T(8,128)(2,1)S(1)} copy-done((bf16[512,2048]{1,0:T(8,128)(2,1)S(1)}, bf16[512,2048]{1,0:T(8,128)(2,1)}, u32[]{:S(2)}) %copy-start) | copy-done | bytes 2097176
  8.9 1.6 %copy-done.2 = bf16[512,2048]{1,0:T(8,128)(2,1)S(1)} copy-done((bf16[512,2048]{1,0:T(8,128)(2,1)S(1)}, bf16[512,2048]{1,0:T(8,128)(2,1)}, u32[]{:S(2)}) %copy-start.2) | copy-done | bytes 2097176
  12.2 2.8 %pack_qo.1 = (bf16[1040,128]{1,0:T(8,128)(2,1)S(1)}, bf16[1040,128]{1,0:T(8,128)(2,1)}, bf16[1040,128]{1,0:T(8,128)(2,1)}, bf16[1040,128]{1,0:T(8,128)(2,1)}) custom-call(s32[4]{0:T(128)S(1)} %pad_add_fusion.refs_0_, bf16[512,512]{1,0:T(8,128)(2,1)S(1)} %copy-done.3, bf16[512,2048]{1,0:T(8,128)(2,1)S(1)} %copy-done.2, bf16[512,2048]{1,0:T(8,128)(2,1)S(1)} %copy-done, ...), custom_call_target="tpu_custom_call" | custom-call | flops 1000 | bytes 1000 | tf_op jit(solution)/shard_map/pack_qo/pallas_call | solution.py:44
  15.0 2.0 %collective-permute-start.4 = (bf16[1040,128]{1,0:T(8,128)(2,1)}, bf16[1040,128]{1,0:T(8,128)(2,1)S(1)}, u32[]{:S(2)}, u32[]{:S(2)}) collective-permute-start(bf16[1040,128]{1,0:T(8,128)(2,1)} %get-tuple-element.72), channel_id=1, source_target_pairs={{0,8},{4,12},{8,0},{12,4},{16,24},{20,28},{24,16},{28,20},{1,9},{5... | collective-permute-start | bytes 798728 | tf_op jit(solution)/shard_map/ppermute | solution.py:480
  22.9 4.7 %collective-permute-start.6 = (bf16[512,128]{1,0:T(8,128)(2,1)S(1)}, bf16[512,128]{1,0:T(8,128)(2,1)S(1)}, u32[]{:S(2)}, u32[]{:S(2)}) collective-permute-start(bf16[512,128]{1,0:T(8,128)(2,1)S(1)} %get-tuple-element.75.refs_7_), channel_id=1, source_target_pairs={{0,16},{4,20},{8,24},{12,28},{1,17},{5,21},{9,25},{13,29},{2,18},{... | collective-permute-start | bytes 393224 | tf_op jit(solution)/shard_map/ppermute | solution.py:495
  28.5 2.3 %collective-permute-start.7 = (bf16[768,128]{1,0:T(8,128)(2,1)}, bf16[768,128]{1,0:T(8,128)(2,1)S(1)}, u32[]{:S(2)}, u32[]{:S(2)}) collective-permute-start(bf16[768,128]{1,0:T(8,128)(2,1)} %copy-done.8), channel_id=1, source_target_pairs={{0,16},{4,20},{8,24},{12,28},{1,17},{5,21},{9,25},{13,29},{2,18},{... | collective-permute-start | bytes 589832 | tf_op jit(solution)/shard_map/ppermute | solution.py:503
  32.1 5.6 %collective-permute-start.8 = (bf16[512,128]{1,0:T(8,128)(2,1)S(1)}, bf16[512,128]{1,0:T(8,128)(2,1)S(1)}, u32[]{:S(2)}, u32[]{:S(2)}) collective-permute-start(bf16[512,128]{1,0:T(8,128)(2,1)S(1)} %get-tuple-element.92.refs_1_), channel_id=1, source_target_pairs={{0,16},{4,20},{8,24},{12,28},{1,17},{5,21},{9,25},{13,29},{2,18},{... | collective-permute-start | bytes 393224 | tf_op jit(solution)/shard_map/ppermute | solution.py:495
  37.7 3.7 %forward_inner.1 = (bf16[5120,256]{1,0:T(8,128)(2,1)S(1)}, f32[1024,256]{1,0:T(8,128)S(1)}, f32[8,256]{1,0:T(8,128)S(1)}, f32[8,256]{1,0:T(8,128)S(1)}) custom-call(s32[4]{0:T(128)S(1)} %pad_add_fusion.refs_0_, bf16[2048,128]{1,0:T(8,128)(2,1)S(1)} %get-tuple-element.76.refs_1_, bf16[2048,128]{1,0:T(8,128)(2,1)S(1)} %get-tuple-element.78.refs_1_.refs_2_.refs_3_, ...), custom_call_target="tpu_custom_call" | custom-call | flops 1000 | bytes 1000 | tf_op jit(solution)/shard_map/forward_inner/pallas_call | solution.py:44
  41.4 1.7 %forward_rim.1 = (bf16[5120,256]{1,0:T(8,128)(2,1)S(1)}, f32[1024,256]{1,0:T(8,128)S(1)}, f32[8,256]{1,0:T(8,128)S(1)}, f32[8,256]{1,0:T(8,128)S(1)}) custom-call(s32[4]{0:T(128)S(1)} %pad_add_fusion.refs_0_, bf16[2048,128]{1,0:T(8,128)(2,1)S(1)} %get-tuple-element.76.refs_1_, ...), custom_call_target="tpu_custom_call", output_to_operand_aliasing={{0}: (7, {}), {1}: (8, {}), {2}: (9, {}), {3}: (10, {})} | custom-call | flops 1000 | bytes 1000 | tf_op jit(solution)/shard_map/forward_rim/pallas_call | solution.py:44
  43.1 3.1 %glob_forward.1 = (bf16[2048,128]{1,0:T(8,128)(2,1)S(1)}, bf16[2048,256]{1,0:T(8,128)(2,1)S(1)}, bf16[2048,128]{1,0:T(8,128)(2,1)S(1)}, bf16[2048,128]{1,0:T(8,1...) custom-call(s32[4]{0:T(128)S(1)} %pad_add_fusion.refs_0_, bf16[2048,128]{1,0:T(8,128)(2,1)S(1)} %get-tuple-element.76.refs_1_, ...), custom_call_target="tpu_custom_call" | custom-call | flops 1000 | bytes 1000 | tf_op jit(solution)/shard_map/glob_forward/pallas_call | solution.py:44
  46.3 1.8 %backward_rim.1 = (f32[256,256]{1,0:T(8,128)S(1)}, f32[2048,128]{1,0:T(8,128)S(1)}, f32[2048,128]{1,0:T(8,128)S(1)}, bf16[768,128]{1,0:T(8,128)(2,1)S(1)}) custom-call(s32[4]{0:T(128)S(1)} %pad_add_fusion.refs_0_, bf16[2048,128]{1,0:T(8,128)(2,1)S(1)} %get-tuple-element.76.refs_1_, bf16[2048,128]{1,0:T(8,128)(2,1)S(1)} %get-tuple-element.93.refs_2_, ...), custom_call_target="tpu_custom_call" | custom-call | flops 1000 | bytes 1000 | tf_op jit(solution)/shard_map/backward_rim/pallas_call | solution.py:44
  48.1 1.8 %row_forward.1.refs_6_.refs_3_ = bf16[144,256]{1,0:T(8,128)(2,1)S(1)} custom-call(s32[4]{0:T(128)S(1)} %pad_add_fusion.refs_0_, bf16[512,128]{1,0:T(8,128)(2,1)S(1)} %get-tuple-element.92.refs_1_, bf16[512,128]{1,0:T(8,128)(2,1)S(1)} %collective-permute-done.8.refs_2_, bf16[2048,128]{1,0:T(8,128)(2,1)S(1)} %get-tuple-element.78.refs_1_.refs_2_.refs_3_, ...), custom_call_target="tpu_custom_call" | custom-call | flops 1000 | bytes 1000 | tf_op jit(solution)/shard_map/row_forward/pallas_call | solution.py:44
  51.4 2.2 %glob_backward.1 = (f32[1024,256]{1,0:T(8,128)S(1)}, f32[256,128]{1,0:T(8,128)S(1)}, f32[256,128]{1,0:T(8,128)S(1)}) custom-call(s32[4]{0:T(128)S(1)} %pad_add_fusion.refs_0_, bf16[2048,128]{1,0:T(8,128)(2,1)S(1)} %get-tuple-element.76.refs_1_, bf16[2048,128]{1,0:T(8,128)(2,1)S(1)} %get-tuple-element.98.refs_2_, ...), custom_call_target="tpu_custom_call" | custom-call | flops 1000 | bytes 1000 | tf_op jit(solution)/shard_map/glob_backward/pallas_call | solution.py:44
  53.6 3.2 %collective-permute-done.9.refs_7_.refs_4_ = bf16[144,256]{1,0:T(8,128)(2,1)S(1)} collective-permute-done((bf16[144,256]{1,0:T(8,128)(2,1)S(1)}, bf16[144,256]{1,0:T(8,128)(2,1)S(1)}, u32[]{:S(2)}, u32[]{:S(2)}) %collective-permute-start.9) | collective-permute-done | bytes 73760 | tf_op jit(solution)/shard_map/ppermute | solution.py:506
  56.8 2.2 %row_backward.1 = (f32[2048,128]{1,0:T(8,128)S(1)}, f32[2048,128]{1,0:T(8,128)S(1)}, bf16[768,128]{1,0:T(8,128)(2,1)S(1)}) custom-call(s32[4]{0:T(128)S(1)} %pad_add_fusion.refs_0_, bf16[512,128]{1,0:T(8,128)(2,1)S(1)} %get-tuple-element.92.refs_1_, bf16[512,128]{1,0:T(8,128)(2,1)S(1)} %collective-permute-done.8.refs_2_, ...), custom_call_target="tpu_custom_call" | custom-call | flops 1000 | bytes 1000 | tf_op jit(solution)/shard_map/row_backward/pallas_call | solution.py:44
  61.3 6.3 %collective-permute-start.11 = (bf16[512,128]{1,0:T(8,128)(2,1)S(1)}, bf16[512,128]{1,0:T(8,128)(2,1)S(1)}, u32[]{:S(2)}, u32[]{:S(2)}) collective-permute-start(bf16[512,128]{1,0:T(8,128)(2,1)S(1)} %get-tuple-element.106), channel_id=1, source_target_pairs={{0,8},{4,12},{8,0},{12,4},{16,24},{20,28},{24,16},{28,20},{1,9},{5... | collective-permute-start | bytes 393224 | tf_op jit(solution)/shard_map/ppermute | solution.py:480
  68.0 3.7 %backward_inner.1 = (f32[2048,128]{1,0:T(8,128)S(1)}, f32[2048,128]{1,0:T(8,128)S(1)}, bf16[2048,128]{1,0:T(8,128)(2,1)S(1)}) custom-call(s32[4]{0:T(128)S(1)} %pad_add_fusion.refs_0_, bf16[2048,128]{1,0:T(8,128)(2,1)S(1)} %get-tuple-element.76.refs_1_, ...), custom_call_target="tpu_custom_call", output_to_operand_aliasing={{0}: (9, {}), {1}: (10, {})} | custom-call | flops 1000 | bytes 1000 | tf_op jit(solution)/shard_map/backward_inner/pallas_call | solution.py:44
  73.5 1.9 %project.1 = (bf16[2,512,512]{2,1,0:T(8,128)(2,1)S(1)}, bf16[2,512,512]{2,1,0:T(8,128)(2,1)S(1)}) custom-call(s32[4]{0:T(128)S(1)} %pad_add_fusion.refs_0_, bf16[512,2048]{1,0:T(8,128)(2,1)S(1)} %copy-done.1, bf16[512,128]{1,0:T(8,128)(2,1)S(1)} %get-tuple-element.104.refs_11_.refs_2_, bf16[512,128]{1,0:T(8,128)(2,1)S(1)} %collective-permute-done.10.refs_3_, ...), custom_call_target="tpu_custom_call" | custom-call | flops 1000 | bytes 1000 | tf_op jit(solution)/shard_map/project/pallas_call | solution.py:44
  81.0 6.0 %collective-permute-done.17.refs_2_ = bf16[1536,128]{1,0:T(8,128)(2,1)S(1)} collective-permute-done((bf16[1536,128]{1,0:T(8,128)(2,1)S(1)}, bf16[1536,128]{1,0:T(8,128)(2,1)S(1)}, u32[]{:S(2)}, u32[]{:S(2)}) %collective-permute-start.17) | collective-permute-done | bytes 393248 | tf_op jit(solution)/shard_map/ppermute | solution.py:480
  87.0 2.0 %collective-permute-done.18.refs_3_ = bf16[1536,128]{1,0:T(8,128)(2,1)S(1)} collective-permute-done((bf16[1536,128]{1,0:T(8,128)(2,1)S(1)}, bf16[1536,128]{1,0:T(8,128)(2,1)S(1)}, u32[]{:S(2)}, u32[]{:S(2)}) %collective-permute-start.18) | collective-permute-done | bytes 393248 | tf_op jit(solution)/shard_map/ppermute | solution.py:480
  88.9 7.9 %collective-permute-done.19.refs_4_ = bf16[1536,128]{1,0:T(8,128)(2,1)S(1)} collective-permute-done((bf16[1536,128]{1,0:T(8,128)(2,1)S(1)}, bf16[1536,128]{1,0:T(8,128)(2,1)S(1)}, u32[]{:S(2)}, u32[]{:S(2)}) %collective-permute-start.19) | collective-permute-done | bytes 393248 | tf_op jit(solution)/shard_map/ppermute | solution.py:480
  96.9 1.9 %join_grads.1 = (bf16[512,512]{1,0:T(8,128)(2,1)}, bf16[512,512]{1,0:T(8,128)(2,1)}, bf16[512,512]{1,0:T(8,128)(2,1)}) custom-call(s32[4]{0:T(128)S(1)} %pad_add_fusion.refs_0_, bf16[1536,128]{1,0:T(8,128)(2,1)S(1)} %get-tuple-element.117.refs_6_.refs_1_, bf16[1536,128]{1,0:T(8,128)(2,1)S(1)} %collective-permute-done.17.refs_2_, ...), custom_call_target="tpu_custom_call" | custom-call | flops 13800000512 | bytes 1000 | tf_op jit(solution)/shard_map/join_grads/pallas_call | solution.py:44
  (57 shorter events, 24.1 us)
Async XLA Ops:
  2.7 15.8 %collective-permute-start.1 = (bf16[1024,128]{1,0:T(8,128)(2,1)S(1)}, bf16[1024,128]{1,0:T(8,128)(2,1)S(1)}, u32[]{:S(2)}, u32[]{:S(2)}) collective-permute-start(bf16[1024,128]{1,0:T(8,128)(2,1)S(1)} %get-tuple-element.68), channel_id=1, source_target_pairs={{0,4},{4,0},{8,12},{12,8},{16,20},{20,16},{24,28},{28,24},{1,5},{5... | collective-permute-start | bytes 786440 | tf_op jit(solution)/shard_map/ppermute | solution.py:480
  5.7 12.9 %collective-permute-start.2 = (bf16[1024,128]{1,0:T(8,128)(2,1)S(1)}, bf16[1024,128]{1,0:T(8,128)(2,1)S(1)}, u32[]{:S(2)}, u32[]{:S(2)}) collective-permute-start(bf16[1024,128]{1,0:T(8,128)(2,1)S(1)} %get-tuple-element.69), channel_id=1, source_target_pairs={{0,8},{4,12},{8,0},{12,4},{16,24},{20,28},{24,16},{28,20},{1,9},{5... | collective-permute-start | bytes 786440 | tf_op jit(solution)/shard_map/ppermute | solution.py:480
  7.3 12.4 %collective-permute-start.3 = (bf16[1024,128]{1,0:T(8,128)(2,1)S(1)}, bf16[1024,128]{1,0:T(8,128)(2,1)S(1)}, u32[]{:S(2)}, u32[]{:S(2)}) collective-permute-start(bf16[1024,128]{1,0:T(8,128)(2,1)S(1)} %get-tuple-element.70), channel_id=1, source_target_pairs={{0,12},{4,8},{8,4},{12,0},{16,28},{20,24},{24,20},{28,16},{1,13},{... | collective-permute-start | bytes 786440 | tf_op jit(solution)/shard_map/ppermute | solution.py:480
  7.3 1.6 %copy-start = (bf16[512,2048]{1,0:T(8,128)(2,1)S(1)}, bf16[512,2048]{1,0:T(8,128)(2,1)}, u32[]{:S(2)}) copy-start(bf16[512,2048]{1,0:T(8,128)(2,1)} %refs_1_.5) | copy-start | bytes 6291460
  8.9 1.6 %copy-start.2 = (bf16[512,2048]{1,0:T(8,128)(2,1)S(1)}, bf16[512,2048]{1,0:T(8,128)(2,1)}, u32[]{:S(2)}) copy-start(bf16[512,2048]{1,0:T(8,128)(2,1)} %refs_2_.3) | copy-start | bytes 6291460
  12.2 6.3 %copy-start.6 = (s32[256]{0:T(256)S(1)}, s32[256]{0:T(256)}, u32[]{:S(2)}) copy-start(s32[256]{0:T(256)} %param.12) | copy-start | bytes 3076
  15.0 13.5 %collective-permute-start.4 = (bf16[1040,128]{1,0:T(8,128)(2,1)}, bf16[1040,128]{1,0:T(8,128)(2,1)S(1)}, u32[]{:S(2)}, u32[]{:S(2)}) collective-permute-start(bf16[1040,128]{1,0:T(8,128)(2,1)} %get-tuple-element.72), channel_id=1, source_target_pairs={{0,8},{4,12},{8,0},{12,4},{16,24},{20,28},{24,16},{28,20},{1,9},{5... | collective-permute-start | bytes 798728 | tf_op jit(solution)/shard_map/ppermute | solution.py:480
  16.9 13.8 %collective-permute-start = (bf16[1040,128]{1,0:T(8,128)(2,1)}, bf16[1040,128]{1,0:T(8,128)(2,1)S(1)}, u32[]{:S(2)}, u32[]{:S(2)}) collective-permute-start(bf16[1040,128]{1,0:T(8,128)(2,1)} %get-tuple-element.67), channel_id=1, source_target_pairs={{0,4},{4,0},{8,12},{12,8},{16,20},{20,16},{24,28},{28,24},{1,5},{5... | collective-permute-start | bytes 798728 | tf_op jit(solution)/shard_map/ppermute | solution.py:480
  18.5 12.7 %collective-permute-start.5 = (bf16[1040,128]{1,0:T(8,128)(2,1)}, bf16[1040,128]{1,0:T(8,128)(2,1)S(1)}, u32[]{:S(2)}, u32[]{:S(2)}) collective-permute-start(bf16[1040,128]{1,0:T(8,128)(2,1)} %get-tuple-element.74), channel_id=1, source_target_pairs={{0,12},{4,8},{8,4},{12,0},{16,28},{20,24},{24,20},{28,16},{1,13},{... | collective-permute-start | bytes 798728 | tf_op jit(solution)/shard_map/ppermute | solution.py:480
  22.9 18.5 %collective-permute-start.6 = (bf16[512,128]{1,0:T(8,128)(2,1)S(1)}, bf16[512,128]{1,0:T(8,128)(2,1)S(1)}, u32[]{:S(2)}, u32[]{:S(2)}) collective-permute-start(bf16[512,128]{1,0:T(8,128)(2,1)S(1)} %get-tuple-element.75.refs_7_), channel_id=1, source_target_pairs={{0,16},{4,20},{8,24},{12,28},{1,17},{5,21},{9,25},{13,29},{2,18},{... | collective-permute-start | bytes 393224 | tf_op jit(solution)/shard_map/ppermute | solution.py:495
  28.5 13.0 %collective-permute-start.7 = (bf16[768,128]{1,0:T(8,128)(2,1)}, bf16[768,128]{1,0:T(8,128)(2,1)S(1)}, u32[]{:S(2)}, u32[]{:S(2)}) collective-permute-start(bf16[768,128]{1,0:T(8,128)(2,1)} %copy-done.8), channel_id=1, source_target_pairs={{0,16},{4,20},{8,24},{12,28},{1,17},{5,21},{9,25},{13,29},{2,18},{... | collective-permute-start | bytes 589832 | tf_op jit(solution)/shard_map/ppermute | solution.py:503
  32.1 15.9 %collective-permute-start.8 = (bf16[512,128]{1,0:T(8,128)(2,1)S(1)}, bf16[512,128]{1,0:T(8,128)(2,1)S(1)}, u32[]{:S(2)}, u32[]{:S(2)}) collective-permute-start(bf16[512,128]{1,0:T(8,128)(2,1)S(1)} %get-tuple-element.92.refs_1_), channel_id=1, source_target_pairs={{0,16},{4,20},{8,24},{12,28},{1,17},{5,21},{9,25},{13,29},{2,18},{... | collective-permute-start | bytes 393224 | tf_op jit(solution)/shard_map/ppermute | solution.py:495
  49.9 6.9 %collective-permute-start.9 = (bf16[144,256]{1,0:T(8,128)(2,1)S(1)}, bf16[144,256]{1,0:T(8,128)(2,1)S(1)}, u32[]{:S(2)}, u32[]{:S(2)}) collective-permute-start(bf16[144,256]{1,0:T(8,128)(2,1)S(1)} %row_forward.1.refs_6_.refs_3_), channel_id=1, source_target_pairs={{0,16},{4,20},{8,24},{12,28},{16,0},{20,4},{24,8},{28,12},{1,17},{... | collective-permute-start | bytes 221192 | tf_op jit(solution)/shard_map/ppermute | solution.py:506
  49.9 21.8 %collective-permute-start.13 = (bf16[768,128]{1,0:T(8,128)(2,1)S(1)}, bf16[768,128]{1,0:T(8,128)(2,1)S(1)}, u32[]{:S(2)}, u32[]{:S(2)}) collective-permute-start(bf16[768,128]{1,0:T(8,128)(2,1)S(1)} %get-tuple-element.97.refs_6_), channel_id=1, source_target_pairs={{16,0},{20,4},{24,8},{28,12},{17,1},{21,5},{25,9},{29,13},{18,2},{... | collective-permute-start | bytes 589832 | tf_op jit(solution)/shard_map/ppermute | solution.py:503
  59.0 12.8 %collective-permute-start.14 = (bf16[768,128]{1,0:T(8,128)(2,1)S(1)}, bf16[768,128]{1,0:T(8,128)(2,1)S(1)}, u32[]{:S(2)}, u32[]{:S(2)}) collective-permute-start(bf16[768,128]{1,0:T(8,128)(2,1)S(1)} %get-tuple-element.103.refs_5_.refs_8_), channel_id=1, source_target_pairs={{16,0},{20,4},{24,8},{28,12},{17,1},{21,5},{25,9},{29,13},{18,2},{... | collective-permute-start | bytes 589832 | tf_op jit(solution)/shard_map/ppermute | solution.py:686
  61.2 12.0 %collective-permute-start.10 = (bf16[512,128]{1,0:T(8,128)(2,1)S(1)}, bf16[512,128]{1,0:T(8,128)(2,1)S(1)}, u32[]{:S(2)}, u32[]{:S(2)}) collective-permute-start(bf16[512,128]{1,0:T(8,128)(2,1)S(1)} %get-tuple-element.105), channel_id=1, source_target_pairs={{0,4},{4,0},{8,12},{12,8},{16,20},{20,16},{24,28},{28,24},{1,5},{5... | collective-permute-start | bytes 393224 | tf_op jit(solution)/shard_map/ppermute | solution.py:480
  61.3 11.9 %collective-permute-start.11 = (bf16[512,128]{1,0:T(8,128)(2,1)S(1)}, bf16[512,128]{1,0:T(8,128)(2,1)S(1)}, u32[]{:S(2)}, u32[]{:S(2)}) collective-permute-start(bf16[512,128]{1,0:T(8,128)(2,1)S(1)} %get-tuple-element.106), channel_id=1, source_target_pairs={{0,8},{4,12},{8,0},{12,4},{16,24},{20,28},{24,16},{28,20},{1,9},{5... | collective-permute-start | bytes 393224 | tf_op jit(solution)/shard_map/ppermute | solution.py:480
  67.6 5.9 %collective-permute-start.12 = (bf16[512,128]{1,0:T(8,128)(2,1)S(1)}, bf16[512,128]{1,0:T(8,128)(2,1)S(1)}, u32[]{:S(2)}, u32[]{:S(2)}) collective-permute-start(bf16[512,128]{1,0:T(8,128)(2,1)S(1)} %get-tuple-element.107), channel_id=1, source_target_pairs={{0,12},{4,8},{8,4},{12,0},{16,28},{20,24},{24,20},{28,16},{1,13},{... | collective-permute-start | bytes 393224 | tf_op jit(solution)/shard_map/ppermute | solution.py:480
  71.8 1.8 %copy-start.1 = (bf16[512,2048]{1,0:T(8,128)(2,1)S(1)}, bf16[512,2048]{1,0:T(8,128)(2,1)}, u32[]{:S(2)}) copy-start(bf16[512,2048]{1,0:T(8,128)(2,1)} %refs_1_.5) | copy-start | bytes 6291460
  75.4 3.6 %collective-permute-start.15 = (bf16[2,512,512]{2,1,0:T(8,128)(2,1)S(1)}, bf16[2,512,512]{2,1,0:T(8,128)(2,1)S(1)}, u32[]{:S(2)}, u32[]{:S(2)}) collective-permute-start(bf16[2,512,512]{2,1,0:T(8,128)(2,1)S(1)} %get-tuple-element.119), channel_id=1, source_target_pairs={{0,1},{1,0},{2,3},{3,2},{4,5},{5,4},{6,7},{7,6},{8,9},{9,8},{10,11... | collective-permute-start | bytes 3145736 | tf_op jit(solution)/shard_map/ppermute | solution.py:718
  75.5 11.5 %collective-permute-start.17 = (bf16[1536,128]{1,0:T(8,128)(2,1)S(1)}, bf16[1536,128]{1,0:T(8,128)(2,1)S(1)}, u32[]{:S(2)}, u32[]{:S(2)}) collective-permute-start(bf16[1536,128]{1,0:T(8,128)(2,1)S(1)} %get-tuple-element.120), channel_id=1, source_target_pairs={{0,4},{4,0},{8,12},{12,8},{16,20},{20,16},{24,28},{28,24},{1,5},{5... | collective-permute-start | bytes 1179656 | tf_op jit(solution)/shard_map/ppermute | solution.py:480
  77.0 12.0 %collective-permute-start.18 = (bf16[1536,128]{1,0:T(8,128)(2,1)S(1)}, bf16[1536,128]{1,0:T(8,128)(2,1)S(1)}, u32[]{:S(2)}, u32[]{:S(2)}) collective-permute-start(bf16[1536,128]{1,0:T(8,128)(2,1)S(1)} %get-tuple-element.121), channel_id=1, source_target_pairs={{0,8},{4,12},{8,0},{12,4},{16,24},{20,28},{24,16},{28,20},{1,9},{5... | collective-permute-start | bytes 1179656 | tf_op jit(solution)/shard_map/ppermute | solution.py:480
  78.5 18.3 %collective-permute-start.19 = (bf16[1536,128]{1,0:T(8,128)(2,1)S(1)}, bf16[1536,128]{1,0:T(8,128)(2,1)S(1)}, u32[]{:S(2)}, u32[]{:S(2)}) collective-permute-start(bf16[1536,128]{1,0:T(8,128)(2,1)S(1)} %get-tuple-element.122), channel_id=1, source_target_pairs={{0,12},{4,8},{8,4},{12,0},{16,28},{20,24},{24,20},{28,16},{1,13},{... | collective-permute-start | bytes 1179656 | tf_op jit(solution)/shard_map/ppermute | solution.py:480
  79.4 19.4 %collective-permute-start.16 = (bf16[512,512]{1,0:T(8,128)(2,1)S(1)}, bf16[512,512]{1,0:T(8,128)(2,1)S(1)}, u32[]{:S(2)}, u32[]{:S(2)}) collective-permute-start(bf16[512,512]{1,0:T(8,128)(2,1)S(1)} %fusion.2), channel_id=1, source_target_pairs={{0,2},{1,3},{2,0},{3,1},{4,6},{5,7},{6,4},{7,5},{8,10},{9,11},{10,... | collective-permute-start | bytes 1572872 | tf_op jit(solution)/shard_map/ppermute | solution.py:720
  (5 other events, 4.1 us)

commit v4 on v3

--- a/solution.py
+++ b/solution.py
@@ -111,7 +111,7 @@
 
 
 def join_kv_body(ids, pos_col, pos_row, *refs):
-    pieces, (k, v, key_bias, picked, rim) = refs[:-5], refs[-5:]
+    pieces, (k, v, key_bias, picked) = refs[:-4], refs[-4:]
     tok = k.shape[0] // len(pieces)
     for i, piece in enumerate(pieces):
         slot = ids[0] ^ i
@@ -121,15 +121,15 @@
     n = pos_col.shape[0]
     picked[0:n, :] = nn(picks, k[0:tok, :]).astype(BF)
     picked[n:, :] = nn(picks, v[0:tok, :]).astype(BF)
+    hidden = jnp.logical_and(row_column(pos_row[...], tok), ids[1] == 0)
+    key_bias[...] = jnp.where(hidden, NEG, jnp.zeros(key_bias.shape, F32))
+
+
+def turn_body(ids, k, v, kt, vt, rim):
+    kt[...] = k[...].T
+    vt[...] = v[...].T
     rim[0:RIM, :] = k[k.shape[0] - RIM :, :]
     rim[RIM:, :] = v[k.shape[0] - RIM :, :]
-    hidden = jnp.logical_and(row_column(pos_row[...], tok), ids[1] == 0)
-    key_bias[...] = jnp.where(hidden, NEG, jnp.zeros(key_bias.shape, F32))
-
-
-def turn_body(ids, k, v, kt, vt):
-    kt[...] = k[...].T
-    vt[...] = v[...].T
 
 
 def join_qo_body(ids, pos_col, pos_row, *refs):
@@ -532,7 +532,7 @@
     head_rows = ((total, HEAD_DIM), BF)
     head_sums = ((total, HEAD_DIM), F32)
     glob_sums = ((n_glob, HEAD_DIM), F32)
-    k, v, key_bias, picked, rim_out = local_call(
+    k, v, key_bias, picked = local_call(
         "join_kv",
         join_kv_body,
         ids,
@@ -542,12 +542,18 @@
             head_rows,
             ((tok, HEAD_DIM), F32),
             ((2 * n_glob, HEAD_DIM), BF),
-            ((2 * RIM, HEAD_DIM), BF),
         ],
     )
     kv_own, kv_sent = from_first(picked)
     kv_glob = jnp.where(group >= last, kv_sent, kv_own)
-    kt, vt = local_call("turn", turn_body, ids, (k, v), [((HEAD_DIM, total), BF)] * 2)
+    kt, vt, rim_out = local_call(
+        "turn",
+        turn_body,
+        ids,
+        (k, v),
+        [((HEAD_DIM, total), BF)] * 2 + [((2 * RIM, HEAD_DIM), BF)],
+        after=(picked,),
+    )
     rim_out, qo[2] = lax.optimization_barrier((rim_out, qo[2]))
     rim = to_next_group(rim_out, 1)
     q, d_attn, bias, qo_pick = local_call(

time: 100 us -> 100 us (level)
    ppermute x2, starting transfers between devices: 3.73 us -> 4.86 us  [to_next_group(): return lax.ppermute(x, 'seq', route)]
    unnamed x18 -> x16, local copies, waits for them, and re-layouts: 7.24 us -> 6.56 us
  transfers between devices with their start and end apart: 20 -> 20, of which waited for: 7 -> 6; matrix products, arithmetic and copies ran while one was open for 1% -> 1% of each run, Pallas kernels for 28% -> 28%
where the time goes in v4:
time: 100 us; the launch traced here: 99.7 us
  starting transfers between devices  36.4 us (36%)
  Pallas kernels  33.7 us (34%)
  waiting for transfers between devices  20.5 us (20%)
  local copies, waits for them, and re-layouts  6.76 us (7%)
  other arithmetic  1.37 us (1%)
    pallas_call x17, Pallas kernels, local_call(): pl.pallas_call(kernel, name=name, out_shape=tuple((jax.ShapeDtypeStruct(s...  33.7 us
    ppermute x12, starting transfers between devices, swap_in_group(): lax.ppermute(piece, 'seq', [(s, s ^ i) for s in range(n_seq)])  18.2 us
    ppermute x12, waiting for transfers between devices, swap_in_group(): lax.ppermute(piece, 'seq', [(s, s ^ i) for s in range(n_seq)])  17.3 us
    ppermute x2, starting transfers between devices, from_first(): sent = lax.ppermute(x, 'seq', route)  10.3 us
    unnamed x16, local copies, waits for them, and re-layouts  6.56 us
    ppermute x2, starting transfers between devices, to_next_group(): return lax.ppermute(x, 'seq', route)  4.86 us
    ppermute x1, waiting for transfers between devices, with_group(): return lax.ppermute(x, 'seq', [(s, s ^ d * heads) for s in range(n_seq)])  3.13 us
  transfers between devices with their start and end apart: 20, of which 6 were waited for; matrix products, arithmetic and copies ran while one was open for 1% of the time, Pallas kernels for 28%

profile of v4, /device:TPU:0, one launch (start us, length us, event | category | flops | bytes accessed | tf_op | source)
XLA Modules:
  0.0 99.7 jit_solution(2214933712855122120)
XLA Ops:
  0.7 1.9 %pack_kv.1 = (bf16[1024,128]{1,0:T(8,128)(2,1)S(1)}, bf16[1024,128]{1,0:T(8,128)(2,1)S(1)}, bf16[1024,128]{1,0:T(8,128)(2,1)S(1)}, bf16[1024,128]{1,0:T(8,128)(2,1)S(1)}) custom-call(s32[4]{0:T(128)S(1)} %pad_add_fusion.refs_0_, bf16[512,512]{1,0:T(8,128)(2,1)} %refs_1_.3, bf16[512,512]{1,0:T(8,128)(2,1)} %refs_2_.2), custom_call_target="tpu_custom_call" | custom-call | flops 1000 | bytes 1000 | tf_op jit(solution)/shard_map/pack_kv/pallas_call | solution.py:44
  2.7 3.0 %collective-permute-start.1 = (bf16[1024,128]{1,0:T(8,128)(2,1)S(1)}, bf16[1024,128]{1,0:T(8,128)(2,1)S(1)}, u32[]{:S(2)}, u32[]{:S(2)}) collective-permute-start(bf16[1024,128]{1,0:T(8,128)(2,1)S(1)} %get-tuple-element.68), channel_id=1, source_target_pairs={{0,4},{4,0},{8,12},{12,8},{16,20},{20,16},{24,28},{28,24},{1,5},{5... | collective-permute-start | bytes 786440 | tf_op jit(solution)/shard_map/ppermute | solution.py:480
  7.3 1.6 %copy-done = bf16[512,2048]{1,0:T(8,128)(2,1)S(1)} copy-done((bf16[512,2048]{1,0:T(8,128)(2,1)S(1)}, bf16[512,2048]{1,0:T(8,128)(2,1)}, u32[]{:S(2)}) %copy-start) | copy-done | bytes 2097176
  8.9 1.6 %copy-done.2 = bf16[512,2048]{1,0:T(8,128)(2,1)S(1)} copy-done((bf16[512,2048]{1,0:T(8,128)(2,1)S(1)}, bf16[512,2048]{1,0:T(8,128)(2,1)}, u32[]{:S(2)}) %copy-start.2) | copy-done | bytes 2097176
  12.2 2.8 %pack_qo.1 = (bf16[1040,128]{1,0:T(8,128)(2,1)S(1)}, bf16[1040,128]{1,0:T(8,128)(2,1)}, bf16[1040,128]{1,0:T(8,128)(2,1)}, bf16[1040,128]{1,0:T(8,128)(2,1)}) custom-call(s32[4]{0:T(128)S(1)} %pad_add_fusion.refs_0_, bf16[512,512]{1,0:T(8,128)(2,1)S(1)} %copy-done.3, bf16[512,2048]{1,0:T(8,128)(2,1)S(1)} %copy-done.2, bf16[512,2048]{1,0:T(8,128)(2,1)S(1)} %copy-done, ...), custom_call_target="tpu_custom_call" | custom-call | flops 1000 | bytes 1000 | tf_op jit(solution)/shard_map/pack_qo/pallas_call | solution.py:44
  15.0 2.0 %collective-permute-start.4 = (bf16[1040,128]{1,0:T(8,128)(2,1)}, bf16[1040,128]{1,0:T(8,128)(2,1)S(1)}, u32[]{:S(2)}, u32[]{:S(2)}) collective-permute-start(bf16[1040,128]{1,0:T(8,128)(2,1)} %get-tuple-element.75), channel_id=1, source_target_pairs={{0,8},{4,12},{8,0},{12,4},{16,24},{20,28},{24,16},{28,20},{1,9},{5... | collective-permute-start | bytes 798728 | tf_op jit(solution)/shard_map/ppermute | solution.py:480
  22.2 4.7 %collective-permute-start.6 = (bf16[512,128]{1,0:T(8,128)(2,1)S(1)}, bf16[512,128]{1,0:T(8,128)(2,1)S(1)}, u32[]{:S(2)}, u32[]{:S(2)}) collective-permute-start(bf16[512,128]{1,0:T(8,128)(2,1)S(1)} %get-tuple-element.73.refs_3_.refs_7_), channel_id=1, source_target_pairs={{0,16},{4,20},{8,24},{12,28},{1,17},{5,21},{9,25},{13,29},{2,18},{... | collective-permute-start | bytes 393224 | tf_op jit(solution)/shard_map/ppermute | solution.py:495
  27.8 3.4 %collective-permute-start.7 = (bf16[768,128]{1,0:T(8,128)(2,1)S(1)}, bf16[768,128]{1,0:T(8,128)(2,1)S(1)}, u32[]{:S(2)}, u32[]{:S(2)}) collective-permute-start(bf16[768,128]{1,0:T(8,128)(2,1)S(1)} %get-tuple-element.83), channel_id=1, source_target_pairs={{0,16},{4,20},{8,24},{12,28},{1,17},{5,21},{9,25},{13,29},{2,18},{... | collective-permute-start | bytes 589832 | tf_op jit(solution)/shard_map/ppermute | solution.py:503
  32.2 5.6 %collective-permute-start.8 = (bf16[512,128]{1,0:T(8,128)(2,1)S(1)}, bf16[512,128]{1,0:T(8,128)(2,1)S(1)}, u32[]{:S(2)}, u32[]{:S(2)}) collective-permute-start(bf16[512,128]{1,0:T(8,128)(2,1)S(1)} %get-tuple-element.92.refs_1_), channel_id=1, source_target_pairs={{0,16},{4,20},{8,24},{12,28},{1,17},{5,21},{9,25},{13,29},{2,18},{... | collective-permute-start | bytes 393224 | tf_op jit(solution)/shard_map/ppermute | solution.py:495
  37.8 3.7 %forward_inner.1 = (bf16[5120,256]{1,0:T(8,128)(2,1)S(1)}, f32[1024,256]{1,0:T(8,128)S(1)}, f32[8,256]{1,0:T(8,128)S(1)}, f32[8,256]{1,0:T(8,128)S(1)}) custom-call(s32[4]{0:T(128)S(1)} %pad_add_fusion.refs_0_, bf16[2048,128]{1,0:T(8,128)(2,1)S(1)} %get-tuple-element.78.refs_1_, bf16[2048,128]{1,0:T(8,128)(2,1)S(1)} %get-tuple-element.71.refs_1_.refs_2_.refs_3_, ...), custom_call_target="tpu_custom_call" | custom-call | flops 1000 | bytes 1000 | tf_op jit(solution)/shard_map/forward_inner/pallas_call | solution.py:44
  41.6 1.7 %forward_rim.1 = (bf16[5120,256]{1,0:T(8,128)(2,1)S(1)}, f32[1024,256]{1,0:T(8,128)S(1)}, f32[8,256]{1,0:T(8,128)S(1)}, f32[8,256]{1,0:T(8,128)S(1)}) custom-call(s32[4]{0:T(128)S(1)} %pad_add_fusion.refs_0_, bf16[2048,128]{1,0:T(8,128)(2,1)S(1)} %get-tuple-element.78.refs_1_, ...), custom_call_target="tpu_custom_call", output_to_operand_aliasing={{0}: (7, {}), {1}: (8, {}), {2}: (9, {}), {3}: (10, {})} | custom-call | flops 1000 | bytes 1000 | tf_op jit(solution)/shard_map/forward_rim/pallas_call | solution.py:44
  43.3 3.1 %glob_forward.1 = (bf16[2048,128]{1,0:T(8,128)(2,1)S(1)}, bf16[2048,256]{1,0:T(8,128)(2,1)S(1)}, bf16[2048,128]{1,0:T(8,128)(2,1)S(1)}, bf16[2048,128]{1,0:T(8,1...) custom-call(s32[4]{0:T(128)S(1)} %pad_add_fusion.refs_0_, bf16[2048,128]{1,0:T(8,128)(2,1)S(1)} %get-tuple-element.78.refs_1_, ...), custom_call_target="tpu_custom_call" | custom-call | flops 1000 | bytes 1000 | tf_op jit(solution)/shard_map/glob_forward/pallas_call | solution.py:44
  46.4 1.8 %backward_rim.1 = (f32[256,256]{1,0:T(8,128)S(1)}, f32[2048,128]{1,0:T(8,128)S(1)}, f32[2048,128]{1,0:T(8,128)S(1)}, bf16[768,128]{1,0:T(8,128)(2,1)S(1)}) custom-call(s32[4]{0:T(128)S(1)} %pad_add_fusion.refs_0_, bf16[2048,128]{1,0:T(8,128)(2,1)S(1)} %get-tuple-element.78.refs_1_, bf16[2048,128]{1,0:T(8,128)(2,1)S(1)} %get-tuple-element.93.refs_2_, ...), custom_call_target="tpu_custom_call" | custom-call | flops 1000 | bytes 1000 | tf_op jit(solution)/shard_map/backward_rim/pallas_call | solution.py:44
  48.2 1.8 %row_forward.1.refs_6_.refs_3_ = bf16[144,256]{1,0:T(8,128)(2,1)S(1)} custom-call(s32[4]{0:T(128)S(1)} %pad_add_fusion.refs_0_, bf16[512,128]{1,0:T(8,128)(2,1)S(1)} %get-tuple-element.92.refs_1_, bf16[512,128]{1,0:T(8,128)(2,1)S(1)} %collective-permute-done.8.refs_2_, bf16[2048,128]{1,0:T(8,128)(2,1)S(1)} %get-tuple-element.71.refs_1_.refs_2_.refs_3_, ...), custom_call_target="tpu_custom_call" | custom-call | flops 1000 | bytes 1000 | tf_op jit(solution)/shard_map/row_forward/pallas_call | solution.py:44
  51.5 2.2 %glob_backward.1 = (f32[1024,256]{1,0:T(8,128)S(1)}, f32[256,128]{1,0:T(8,128)S(1)}, f32[256,128]{1,0:T(8,128)S(1)}) custom-call(s32[4]{0:T(128)S(1)} %pad_add_fusion.refs_0_, bf16[2048,128]{1,0:T(8,128)(2,1)S(1)} %get-tuple-element.78.refs_1_, bf16[2048,128]{1,0:T(8,128)(2,1)S(1)} %get-tuple-element.98.refs_2_, ...), custom_call_target="tpu_custom_call" | custom-call | flops 1000 | bytes 1000 | tf_op jit(solution)/shard_map/glob_backward/pallas_call | solution.py:44
  53.8 3.1 %collective-permute-done.9.refs_7_.refs_4_ = bf16[144,256]{1,0:T(8,128)(2,1)S(1)} collective-permute-done((bf16[144,256]{1,0:T(8,128)(2,1)S(1)}, bf16[144,256]{1,0:T(8,128)(2,1)S(1)}, u32[]{:S(2)}, u32[]{:S(2)}) %collective-permute-start.9) | collective-permute-done | bytes 73760 | tf_op jit(solution)/shard_map/ppermute | solution.py:506
  56.9 2.2 %row_backward.1 = (f32[2048,128]{1,0:T(8,128)S(1)}, f32[2048,128]{1,0:T(8,128)S(1)}, bf16[768,128]{1,0:T(8,128)(2,1)S(1)}) custom-call(s32[4]{0:T(128)S(1)} %pad_add_fusion.refs_0_, bf16[512,128]{1,0:T(8,128)(2,1)S(1)} %get-tuple-element.92.refs_1_, bf16[512,128]{1,0:T(8,128)(2,1)S(1)} %collective-permute-done.8.refs_2_, ...), custom_call_target="tpu_custom_call" | custom-call | flops 1000 | bytes 1000 | tf_op jit(solution)/shard_map/row_backward/pallas_call | solution.py:44
  61.4 5.9 %collective-permute-start.11 = (bf16[512,128]{1,0:T(8,128)(2,1)S(1)}, bf16[512,128]{1,0:T(8,128)(2,1)S(1)}, u32[]{:S(2)}, u32[]{:S(2)}) collective-permute-start(bf16[512,128]{1,0:T(8,128)(2,1)S(1)} %get-tuple-element.106), channel_id=1, source_target_pairs={{0,8},{4,12},{8,0},{12,4},{16,24},{20,28},{24,16},{28,20},{1,9},{5... | collective-permute-start | bytes 393224 | tf_op jit(solution)/shard_map/ppermute | solution.py:480
  67.9 3.7 %backward_inner.1 = (f32[2048,128]{1,0:T(8,128)S(1)}, f32[2048,128]{1,0:T(8,128)S(1)}, bf16[2048,128]{1,0:T(8,128)(2,1)S(1)}) custom-call(s32[4]{0:T(128)S(1)} %pad_add_fusion.refs_0_, bf16[2048,128]{1,0:T(8,128)(2,1)S(1)} %get-tuple-element.78.refs_1_, ...), custom_call_target="tpu_custom_call", output_to_operand_aliasing={{0}: (9, {}), {1}: (10, {})} | custom-call | flops 1000 | bytes 1000 | tf_op jit(solution)/shard_map/backward_inner/pallas_call | solution.py:44
  73.7 1.9 %project.1 = (bf16[2,512,512]{2,1,0:T(8,128)(2,1)S(1)}, bf16[2,512,512]{2,1,0:T(8,128)(2,1)S(1)}) custom-call(s32[4]{0:T(128)S(1)} %pad_add_fusion.refs_0_, bf16[512,2048]{1,0:T(8,128)(2,1)S(1)} %copy-done.1, bf16[512,128]{1,0:T(8,128)(2,1)S(1)} %get-tuple-element.104.refs_11_.refs_2_, bf16[512,128]{1,0:T(8,128)(2,1)S(1)} %collective-permute-done.10.refs_3_, ...), custom_call_target="tpu_custom_call" | custom-call | flops 1000 | bytes 1000 | tf_op jit(solution)/shard_map/project/pallas_call | solution.py:44
  81.2 6.0 %collective-permute-done.17.refs_2_ = bf16[1536,128]{1,0:T(8,128)(2,1)S(1)} collective-permute-done((bf16[1536,128]{1,0:T(8,128)(2,1)S(1)}, bf16[1536,128]{1,0:T(8,128)(2,1)S(1)}, u32[]{:S(2)}, u32[]{:S(2)}) %collective-permute-start.17) | collective-permute-done | bytes 393248 | tf_op jit(solution)/shard_map/ppermute | solution.py:480
  87.2 1.7 %collective-permute-done.18.refs_3_ = bf16[1536,128]{1,0:T(8,128)(2,1)S(1)} collective-permute-done((bf16[1536,128]{1,0:T(8,128)(2,1)S(1)}, bf16[1536,128]{1,0:T(8,128)(2,1)S(1)}, u32[]{:S(2)}, u32[]{:S(2)}) %collective-permute-start.18) | collective-permute-done | bytes 393248 | tf_op jit(solution)/shard_map/ppermute | solution.py:480
  88.9 7.9 %collective-permute-done.19.refs_4_ = bf16[1536,128]{1,0:T(8,128)(2,1)S(1)} collective-permute-done((bf16[1536,128]{1,0:T(8,128)(2,1)S(1)}, bf16[1536,128]{1,0:T(8,128)(2,1)S(1)}, u32[]{:S(2)}, u32[]{:S(2)}) %collective-permute-start.19) | collective-permute-done | bytes 393248 | tf_op jit(solution)/shard_map/ppermute | solution.py:480
  96.8 1.9 %join_grads.1 = (bf16[512,512]{1,0:T(8,128)(2,1)}, bf16[512,512]{1,0:T(8,128)(2,1)}, bf16[512,512]{1,0:T(8,128)(2,1)}) custom-call(s32[4]{0:T(128)S(1)} %pad_add_fusion.refs_0_, bf16[1536,128]{1,0:T(8,128)(2,1)S(1)} %get-tuple-element.117.refs_6_.refs_1_, bf16[1536,128]{1,0:T(8,128)(2,1)S(1)} %collective-permute-done.17.refs_2_, ...), custom_call_target="tpu_custom_call" | custom-call | flops 13800000512 | bytes 1000 | tf_op jit(solution)/shard_map/join_grads/pallas_call | solution.py:44
  (55 shorter events, 23.5 us)
Async XLA Ops:
  2.7 15.8 %collective-permute-start.1 = (bf16[1024,128]{1,0:T(8,128)(2,1)S(1)}, bf16[1024,128]{1,0:T(8,128)(2,1)S(1)}, u32[]{:S(2)}, u32[]{:S(2)}) collective-permute-start(bf16[1024,128]{1,0:T(8,128)(2,1)S(1)} %get-tuple-element.68), channel_id=1, source_target_pairs={{0,4},{4,0},{8,12},{12,8},{16,20},{20,16},{24,28},{28,24},{1,5},{5... | collective-permute-start | bytes 786440 | tf_op jit(solution)/shard_map/ppermute | solution.py:480
  5.7 12.9 %collective-permute-start.2 = (bf16[1024,128]{1,0:T(8,128)(2,1)S(1)}, bf16[1024,128]{1,0:T(8,128)(2,1)S(1)}, u32[]{:S(2)}, u32[]{:S(2)}) collective-permute-start(bf16[1024,128]{1,0:T(8,128)(2,1)S(1)} %get-tuple-element.69), channel_id=1, source_target_pairs={{0,8},{4,12},{8,0},{12,4},{16,24},{20,28},{24,16},{28,20},{1,9},{5... | collective-permute-start | bytes 786440 | tf_op jit(solution)/shard_map/ppermute | solution.py:480
  7.3 12.4 %collective-permute-start.3 = (bf16[1024,128]{1,0:T(8,128)(2,1)S(1)}, bf16[1024,128]{1,0:T(8,128)(2,1)S(1)}, u32[]{:S(2)}, u32[]{:S(2)}) collective-permute-start(bf16[1024,128]{1,0:T(8,128)(2,1)S(1)} %get-tuple-element.70), channel_id=1, source_target_pairs={{0,12},{4,8},{8,4},{12,0},{16,28},{20,24},{24,20},{28,16},{1,13},{... | collective-permute-start | bytes 786440 | tf_op jit(solution)/shard_map/ppermute | solution.py:480
  7.3 1.6 %copy-start = (bf16[512,2048]{1,0:T(8,128)(2,1)S(1)}, bf16[512,2048]{1,0:T(8,128)(2,1)}, u32[]{:S(2)}) copy-start(bf16[512,2048]{1,0:T(8,128)(2,1)} %refs_1_.5) | copy-start | bytes 6291460
  8.9 1.6 %copy-start.2 = (bf16[512,2048]{1,0:T(8,128)(2,1)S(1)}, bf16[512,2048]{1,0:T(8,128)(2,1)}, u32[]{:S(2)}) copy-start(bf16[512,2048]{1,0:T(8,128)(2,1)} %refs_2_.3) | copy-start | bytes 6291460
  12.2 6.3 %copy-start.6 = (s32[256]{0:T(256)S(1)}, s32[256]{0:T(256)}, u32[]{:S(2)}) copy-start(s32[256]{0:T(256)} %param.12) | copy-start | bytes 3076
  15.0 12.8 %collective-permute-start.4 = (bf16[1040,128]{1,0:T(8,128)(2,1)}, bf16[1040,128]{1,0:T(8,128)(2,1)S(1)}, u32[]{:S(2)}, u32[]{:S(2)}) collective-permute-start(bf16[1040,128]{1,0:T(8,128)(2,1)} %get-tuple-element.75), channel_id=1, source_target_pairs={{0,8},{4,12},{8,0},{12,4},{16,24},{20,28},{24,16},{28,20},{1,9},{5... | collective-permute-start | bytes 798728 | tf_op jit(solution)/shard_map/ppermute | solution.py:480
  16.9 14.3 %collective-permute-start = (bf16[1040,128]{1,0:T(8,128)(2,1)}, bf16[1040,128]{1,0:T(8,128)(2,1)S(1)}, u32[]{:S(2)}, u32[]{:S(2)}) collective-permute-start(bf16[1040,128]{1,0:T(8,128)(2,1)} %get-tuple-element.67), channel_id=1, source_target_pairs={{0,4},{4,0},{8,12},{12,8},{16,20},{20,16},{24,28},{28,24},{1,5},{5... | collective-permute-start | bytes 798728 | tf_op jit(solution)/shard_map/ppermute | solution.py:480
  18.5 12.8 %collective-permute-start.5 = (bf16[1040,128]{1,0:T(8,128)(2,1)}, bf16[1040,128]{1,0:T(8,128)(2,1)S(1)}, u32[]{:S(2)}, u32[]{:S(2)}) collective-permute-start(bf16[1040,128]{1,0:T(8,128)(2,1)} %get-tuple-element.77), channel_id=1, source_target_pairs={{0,12},{4,8},{8,4},{12,0},{16,28},{20,24},{24,20},{28,16},{1,13},{... | collective-permute-start | bytes 798728 | tf_op jit(solution)/shard_map/ppermute | solution.py:480
  22.2 19.3 %collective-permute-start.6 = (bf16[512,128]{1,0:T(8,128)(2,1)S(1)}, bf16[512,128]{1,0:T(8,128)(2,1)S(1)}, u32[]{:S(2)}, u32[]{:S(2)}) collective-permute-start(bf16[512,128]{1,0:T(8,128)(2,1)S(1)} %get-tuple-element.73.refs_3_.refs_7_), channel_id=1, source_target_pairs={{0,16},{4,20},{8,24},{12,28},{1,17},{5,21},{9,25},{13,29},{2,18},{... | collective-permute-start | bytes 393224 | tf_op jit(solution)/shard_map/ppermute | solution.py:495
  27.8 13.7 %collective-permute-start.7 = (bf16[768,128]{1,0:T(8,128)(2,1)S(1)}, bf16[768,128]{1,0:T(8,128)(2,1)S(1)}, u32[]{:S(2)}, u32[]{:S(2)}) collective-permute-start(bf16[768,128]{1,0:T(8,128)(2,1)S(1)} %get-tuple-element.83), channel_id=1, source_target_pairs={{0,16},{4,20},{8,24},{12,28},{1,17},{5,21},{9,25},{13,29},{2,18},{... | collective-permute-start | bytes 589832 | tf_op jit(solution)/shard_map/ppermute | solution.py:503
  32.2 16.0 %collective-permute-start.8 = (bf16[512,128]{1,0:T(8,128)(2,1)S(1)}, bf16[512,128]{1,0:T(8,128)(2,1)S(1)}, u32[]{:S(2)}, u32[]{:S(2)}) collective-permute-start(bf16[512,128]{1,0:T(8,128)(2,1)S(1)} %get-tuple-element.92.refs_1_), channel_id=1, source_target_pairs={{0,16},{4,20},{8,24},{12,28},{1,17},{5,21},{9,25},{13,29},{2,18},{... | collective-permute-start | bytes 393224 | tf_op jit(solution)/shard_map/ppermute | solution.py:495
  50.0 6.9 %collective-permute-start.9 = (bf16[144,256]{1,0:T(8,128)(2,1)S(1)}, bf16[144,256]{1,0:T(8,128)(2,1)S(1)}, u32[]{:S(2)}, u32[]{:S(2)}) collective-permute-start(bf16[144,256]{1,0:T(8,128)(2,1)S(1)} %row_forward.1.refs_6_.refs_3_), channel_id=1, source_target_pairs={{0,16},{4,20},{8,24},{12,28},{16,0},{20,4},{24,8},{28,12},{1,17},{... | collective-permute-start | bytes 221192 | tf_op jit(solution)/shard_map/ppermute | solution.py:506
  50.1 21.5 %collective-permute-start.13 = (bf16[768,128]{1,0:T(8,128)(2,1)S(1)}, bf16[768,128]{1,0:T(8,128)(2,1)S(1)}, u32[]{:S(2)}, u32[]{:S(2)}) collective-permute-start(bf16[768,128]{1,0:T(8,128)(2,1)S(1)} %get-tuple-element.97.refs_6_), channel_id=1, source_target_pairs={{16,0},{20,4},{24,8},{28,12},{17,1},{21,5},{25,9},{29,13},{18,2},{... | collective-permute-start | bytes 589832 | tf_op jit(solution)/shard_map/ppermute | solution.py:503
  59.1 12.5 %collective-permute-start.14 = (bf16[768,128]{1,0:T(8,128)(2,1)S(1)}, bf16[768,128]{1,0:T(8,128)(2,1)S(1)}, u32[]{:S(2)}, u32[]{:S(2)}) collective-permute-start(bf16[768,128]{1,0:T(8,128)(2,1)S(1)} %get-tuple-element.103.refs_5_.refs_8_), channel_id=1, source_target_pairs={{16,0},{20,4},{24,8},{28,12},{17,1},{21,5},{25,9},{29,13},{18,2},{... | collective-permute-start | bytes 589832 | tf_op jit(solution)/shard_map/ppermute | solution.py:692
  61.3 11.7 %collective-permute-start.10 = (bf16[512,128]{1,0:T(8,128)(2,1)S(1)}, bf16[512,128]{1,0:T(8,128)(2,1)S(1)}, u32[]{:S(2)}, u32[]{:S(2)}) collective-permute-start(bf16[512,128]{1,0:T(8,128)(2,1)S(1)} %get-tuple-element.105), channel_id=1, source_target_pairs={{0,4},{4,0},{8,12},{12,8},{16,20},{20,16},{24,28},{28,24},{1,5},{5... | collective-permute-start | bytes 393224 | tf_op jit(solution)/shard_map/ppermute | solution.py:480
  61.4 11.6 %collective-permute-start.11 = (bf16[512,128]{1,0:T(8,128)(2,1)S(1)}, bf16[512,128]{1,0:T(8,128)(2,1)S(1)}, u32[]{:S(2)}, u32[]{:S(2)}) collective-permute-start(bf16[512,128]{1,0:T(8,128)(2,1)S(1)} %get-tuple-element.106), channel_id=1, source_target_pairs={{0,8},{4,12},{8,0},{12,4},{16,24},{20,28},{24,16},{28,20},{1,9},{5... | collective-permute-start | bytes 393224 | tf_op jit(solution)/shard_map/ppermute | solution.py:480
  67.3 6.4 %collective-permute-start.12 = (bf16[512,128]{1,0:T(8,128)(2,1)S(1)}, bf16[512,128]{1,0:T(8,128)(2,1)S(1)}, u32[]{:S(2)}, u32[]{:S(2)}) collective-permute-start(bf16[512,128]{1,0:T(8,128)(2,1)S(1)} %get-tuple-element.107), channel_id=1, source_target_pairs={{0,12},{4,8},{8,4},{12,0},{16,28},{20,24},{24,20},{28,16},{1,13},{... | collective-permute-start | bytes 393224 | tf_op jit(solution)/shard_map/ppermute | solution.py:480
  71.6 2.1 %copy-start.1 = (bf16[512,2048]{1,0:T(8,128)(2,1)S(1)}, bf16[512,2048]{1,0:T(8,128)(2,1)}, u32[]{:S(2)}) copy-start(bf16[512,2048]{1,0:T(8,128)(2,1)} %refs_1_.5) | copy-start | bytes 6291460
  75.6 3.6 %collective-permute-start.15 = (bf16[2,512,512]{2,1,0:T(8,128)(2,1)S(1)}, bf16[2,512,512]{2,1,0:T(8,128)(2,1)S(1)}, u32[]{:S(2)}, u32[]{:S(2)}) collective-permute-start(bf16[2,512,512]{2,1,0:T(8,128)(2,1)S(1)} %get-tuple-element.119), channel_id=1, source_target_pairs={{0,1},{1,0},{2,3},{3,2},{4,5},{5,4},{6,7},{7,6},{8,9},{9,8},{10,11... | collective-permute-start | bytes 3145736 | tf_op jit(solution)/shard_map/ppermute | solution.py:724
  75.6 11.5 %collective-permute-start.17 = (bf16[1536,128]{1,0:T(8,128)(2,1)S(1)}, bf16[1536,128]{1,0:T(8,128)(2,1)S(1)}, u32[]{:S(2)}, u32[]{:S(2)}) collective-permute-start(bf16[1536,128]{1,0:T(8,128)(2,1)S(1)} %get-tuple-element.120), channel_id=1, source_target_pairs={{0,4},{4,0},{8,12},{12,8},{16,20},{20,16},{24,28},{28,24},{1,5},{5... | collective-permute-start | bytes 1179656 | tf_op jit(solution)/shard_map/ppermute | solution.py:480
  76.9 12.0 %collective-permute-start.18 = (bf16[1536,128]{1,0:T(8,128)(2,1)S(1)}, bf16[1536,128]{1,0:T(8,128)(2,1)S(1)}, u32[]{:S(2)}, u32[]{:S(2)}) collective-permute-start(bf16[1536,128]{1,0:T(8,128)(2,1)S(1)} %get-tuple-element.121), channel_id=1, source_target_pairs={{0,8},{4,12},{8,0},{12,4},{16,24},{20,28},{24,16},{28,20},{1,9},{5... | collective-permute-start | bytes 1179656 | tf_op jit(solution)/shard_map/ppermute | solution.py:480
  78.3 18.5 %collective-permute-start.19 = (bf16[1536,128]{1,0:T(8,128)(2,1)S(1)}, bf16[1536,128]{1,0:T(8,128)(2,1)S(1)}, u32[]{:S(2)}, u32[]{:S(2)}) collective-permute-start(bf16[1536,128]{1,0:T(8,128)(2,1)S(1)} %get-tuple-element.122), channel_id=1, source_target_pairs={{0,12},{4,8},{8,4},{12,0},{16,28},{20,24},{24,20},{28,16},{1,13},{... | collective-permute-start | bytes 1179656 | tf_op jit(solution)/shard_map/ppermute | solution.py:480
  79.6 19.1 %collective-permute-start.16 = (bf16[512,512]{1,0:T(8,128)(2,1)S(1)}, bf16[512,512]{1,0:T(8,128)(2,1)S(1)}, u32[]{:S(2)}, u32[]{:S(2)}) collective-permute-start(bf16[512,512]{1,0:T(8,128)(2,1)S(1)} %fusion.2), channel_id=1, source_target_pairs={{0,2},{1,3},{2,0},{3,1},{4,6},{5,7},{6,4},{7,5},{8,10},{9,11},{10,... | collective-permute-start | bytes 1572872 | tf_op jit(solution)/shard_map/ppermute | solution.py:726
  (4 other events, 3.4 us)

commit v5 on v4

--- a/solution.py
+++ b/solution.py
@@ -522,7 +522,7 @@
             "pack_qo",
             pack_qo_body,
             ids,
-            (queries, out_grad, out_weight),
+            (in_hbm(queries), in_hbm(out_grad), in_hbm(out_weight)),
             [((2 * tok + block_mask.size, HEAD_DIM), BF)] * heads,
             [pltpu.VMEM((tok, cols), BF)],
             far=((block_mask, pltpu.SMEM),),

time: 100 us -> 100 us (level)
  local copies, waits for them, and re-layouts: 6.76 us -> 2.54 us
  waiting for transfers between devices: 20.5 us -> 23.2 us
  Pallas kernels: 33.7 us -> 35.6 us
    unnamed x16 -> x10, local copies, waits for them, and re-layouts: 6.56 us -> 2.34 us
    ppermute x12, waiting for transfers between devices: 17.3 us -> 20 us  [swap_in_group(): lax.ppermute(piece, 'seq', [(s, s ^ i) for s in range(n_seq)])]
    pallas_call x17, Pallas kernels: 33.7 us -> 35.6 us  [local_call(): pl.pallas_call(kernel, name=name, out_shape=tuple((jax.ShapeDtypeStruct(s...]
  transfers between devices with their start and end apart: 20 -> 20, of which waited for: 6 -> 6; matrix products, arithmetic and copies ran while one was open for 1% -> 1% of each run, Pallas kernels for 28% -> 30%
where the time goes in v5:
time: 100 us; the launch traced here: 99.7 us
  starting transfers between devices  36.1 us (36%)
  Pallas kernels  35.6 us (36%)
  waiting for transfers between devices  23.2 us (23%)
  local copies, waits for them, and re-layouts  2.54 us (3%)
  other arithmetic  1.37 us (1%)
    pallas_call x17, Pallas kernels, local_call(): pl.pallas_call(kernel, name=name, out_shape=tuple((jax.ShapeDtypeStruct(s...  35.6 us
    ppermute x12, waiting for transfers between devices, swap_in_group(): lax.ppermute(piece, 'seq', [(s, s ^ i) for s in range(n_seq)])  20 us
    ppermute x12, starting transfers between devices, swap_in_group(): lax.ppermute(piece, 'seq', [(s, s ^ i) for s in range(n_seq)])  18.3 us
    ppermute x2, starting transfers between devices, from_first(): sent = lax.ppermute(x, 'seq', route)  10.5 us
    ppermute x2, starting transfers between devices, to_next_group(): return lax.ppermute(x, 'seq', route)  4.27 us
    ppermute x1, waiting for transfers between devices, with_group(): return lax.ppermute(x, 'seq', [(s, s ^ d * heads) for s in range(n_seq)])  3.13 us
    unnamed x10, local copies, waits for them, and re-layouts  2.34 us
  transfers between devices with their start and end apart: 20, of which 6 were waited for; matrix products, arithmetic and copies ran while one was open for 1% of the time, Pallas kernels for 30%

profile of v5, /device:TPU:0, one launch (start us, length us, event | category | flops | bytes accessed | tf_op | source)
XLA Modules:
  0.0 99.7 jit_solution(13450108708104598727)
XLA Ops:
  0.7 1.9 %pack_kv.1 = (bf16[1024,128]{1,0:T(8,128)(2,1)S(1)}, bf16[1024,128]{1,0:T(8,128)(2,1)S(1)}, bf16[1024,128]{1,0:T(8,128)(2,1)S(1)}, bf16[1024,128]{1,0:T(8,128)(2,1)S(1)}) custom-call(s32[4]{0:T(128)S(1)} %pad_add_fusion.refs_0_, bf16[512,512]{1,0:T(8,128)(2,1)} %refs_1_.3, bf16[512,512]{1,0:T(8,128)(2,1)} %refs_2_.2), custom_call_target="tpu_custom_call" | custom-call | flops 1000 | bytes 1000 | tf_op jit(solution)/shard_map/pack_kv/pallas_call | solution.py:44
  2.7 3.0 %collective-permute-start.1 = (bf16[1024,128]{1,0:T(8,128)(2,1)S(1)}, bf16[1024,128]{1,0:T(8,128)(2,1)S(1)}, u32[]{:S(2)}, u32[]{:S(2)}) collective-permute-start(bf16[1024,128]{1,0:T(8,128)(2,1)S(1)} %get-tuple-element.68), channel_id=1, source_target_pairs={{0,4},{4,0},{8,12},{12,8},{16,20},{20,16},{24,28},{28,24},{1,5},{5... | collective-permute-start | bytes 786440 | tf_op jit(solution)/shard_map/ppermute | solution.py:480
  8.0 4.6 %pack_qo.1 = (bf16[1040,128]{1,0:T(8,128)(2,1)S(1)}, bf16[1040,128]{1,0:T(8,128)(2,1)}, bf16[1040,128]{1,0:T(8,128)(2,1)}, bf16[1040,128]{1,0:T(8,128)(2,1)}) custom-call(s32[4]{0:T(128)S(1)} %pad_add_fusion.refs_0_, bf16[512,512]{1,0:T(8,128)(2,1)} %refs_1_.4, bf16[512,2048]{1,0:T(8,128)(2,1)} %refs_2_.3, bf16[512,2048]{1,0:T(8,128)(2,1)} %refs_1_.5, ...), custom_call_target="tpu_custom_call" | custom-call | flops 1000 | bytes 1000 | tf_op jit(solution)/shard_map/pack_qo/pallas_call | solution.py:44
  12.6 2.0 %collective-permute-start.4 = (bf16[1040,128]{1,0:T(8,128)(2,1)}, bf16[1040,128]{1,0:T(8,128)(2,1)S(1)}, u32[]{:S(2)}, u32[]{:S(2)}) collective-permute-start(bf16[1040,128]{1,0:T(8,128)(2,1)} %get-tuple-element.75), channel_id=1, source_target_pairs={{0,8},{4,12},{8,0},{12,4},{16,24},{20,28},{24,16},{28,20},{1,9},{5... | collective-permute-start | bytes 798728 | tf_op jit(solution)/shard_map/ppermute | solution.py:480
  16.2 3.8 %collective-permute-done.3.refs_6_ = bf16[1024,128]{1,0:T(8,128)(2,1)S(1)} collective-permute-done((bf16[1024,128]{1,0:T(8,128)(2,1)S(1)}, bf16[1024,128]{1,0:T(8,128)(2,1)S(1)}, u32[]{:S(2)}, u32[]{:S(2)}) %collective-permute-start.3) | collective-permute-done | bytes 262176 | tf_op jit(solution)/shard_map/ppermute | solution.py:480
  22.6 5.0 %collective-permute-start.6 = (bf16[512,128]{1,0:T(8,128)(2,1)S(1)}, bf16[512,128]{1,0:T(8,128)(2,1)S(1)}, u32[]{:S(2)}, u32[]{:S(2)}) collective-permute-start(bf16[512,128]{1,0:T(8,128)(2,1)S(1)} %get-tuple-element.73.refs_3_.refs_7_), channel_id=1, source_target_pairs={{0,16},{4,20},{8,24},{12,28},{1,17},{5,21},{9,25},{13,29},{2,18},{... | collective-permute-start | bytes 393224 | tf_op jit(solution)/shard_map/ppermute | solution.py:495
  28.5 2.8 %collective-permute-start.7 = (bf16[768,128]{1,0:T(8,128)(2,1)S(1)}, bf16[768,128]{1,0:T(8,128)(2,1)S(1)}, u32[]{:S(2)}, u32[]{:S(2)}) collective-permute-start(bf16[768,128]{1,0:T(8,128)(2,1)S(1)} %get-tuple-element.83), channel_id=1, source_target_pairs={{0,16},{4,20},{8,24},{12,28},{1,17},{5,21},{9,25},{13,29},{2,18},{... | collective-permute-start | bytes 589832 | tf_op jit(solution)/shard_map/ppermute | solution.py:503
  32.3 5.6 %collective-permute-start.8 = (bf16[512,128]{1,0:T(8,128)(2,1)S(1)}, bf16[512,128]{1,0:T(8,128)(2,1)S(1)}, u32[]{:S(2)}, u32[]{:S(2)}) collective-permute-start(bf16[512,128]{1,0:T(8,128)(2,1)S(1)} %get-tuple-element.92.refs_1_), channel_id=1, source_target_pairs={{0,16},{4,20},{8,24},{12,28},{1,17},{5,21},{9,25},{13,29},{2,18},{... | collective-permute-start | bytes 393224 | tf_op jit(solution)/shard_map/ppermute | solution.py:495
  37.9 3.7 %forward_inner.1 = (bf16[5120,256]{1,0:T(8,128)(2,1)S(1)}, f32[1024,256]{1,0:T(8,128)S(1)}, f32[8,256]{1,0:T(8,128)S(1)}, f32[8,256]{1,0:T(8,128)S(1)}) custom-call(s32[4]{0:T(128)S(1)} %pad_add_fusion.refs_0_, bf16[2048,128]{1,0:T(8,128)(2,1)S(1)} %get-tuple-element.78.refs_1_, bf16[2048,128]{1,0:T(8,128)(2,1)S(1)} %get-tuple-element.71.refs_1_.refs_2_.refs_3_, ...), custom_call_target="tpu_custom_call" | custom-call | flops 1000 | bytes 1000 | tf_op jit(solution)/shard_map/forward_inner/pallas_call | solution.py:44
  41.6 1.7 %forward_rim.1 = (bf16[5120,256]{1,0:T(8,128)(2,1)S(1)}, f32[1024,256]{1,0:T(8,128)S(1)}, f32[8,256]{1,0:T(8,128)S(1)}, f32[8,256]{1,0:T(8,128)S(1)}) custom-call(s32[4]{0:T(128)S(1)} %pad_add_fusion.refs_0_, bf16[2048,128]{1,0:T(8,128)(2,1)S(1)} %get-tuple-element.78.refs_1_, ...), custom_call_target="tpu_custom_call", output_to_operand_aliasing={{0}: (7, {}), {1}: (8, {}), {2}: (9, {}), {3}: (10, {})} | custom-call | flops 1000 | bytes 1000 | tf_op jit(solution)/shard_map/forward_rim/pallas_call | solution.py:44
  43.3 3.1 %glob_forward.1 = (bf16[2048,128]{1,0:T(8,128)(2,1)S(1)}, bf16[2048,256]{1,0:T(8,128)(2,1)S(1)}, bf16[2048,128]{1,0:T(8,128)(2,1)S(1)}, bf16[2048,128]{1,0:T(8,1...) custom-call(s32[4]{0:T(128)S(1)} %pad_add_fusion.refs_0_, bf16[2048,128]{1,0:T(8,128)(2,1)S(1)} %get-tuple-element.78.refs_1_, ...), custom_call_target="tpu_custom_call" | custom-call | flops 1000 | bytes 1000 | tf_op jit(solution)/shard_map/glob_forward/pallas_call | solution.py:44
  46.4 1.8 %backward_rim.1 = (f32[256,256]{1,0:T(8,128)S(1)}, f32[2048,128]{1,0:T(8,128)S(1)}, f32[2048,128]{1,0:T(8,128)S(1)}, bf16[768,128]{1,0:T(8,128)(2,1)S(1)}) custom-call(s32[4]{0:T(128)S(1)} %pad_add_fusion.refs_0_, bf16[2048,128]{1,0:T(8,128)(2,1)S(1)} %get-tuple-element.78.refs_1_, bf16[2048,128]{1,0:T(8,128)(2,1)S(1)} %get-tuple-element.93.refs_2_, ...), custom_call_target="tpu_custom_call" | custom-call | flops 1000 | bytes 1000 | tf_op jit(solution)/shard_map/backward_rim/pallas_call | solution.py:44
  48.2 1.8 %row_forward.1.refs_6_.refs_3_ = bf16[144,256]{1,0:T(8,128)(2,1)S(1)} custom-call(s32[4]{0:T(128)S(1)} %pad_add_fusion.refs_0_, bf16[512,128]{1,0:T(8,128)(2,1)S(1)} %get-tuple-element.92.refs_1_, bf16[512,128]{1,0:T(8,128)(2,1)S(1)} %collective-permute-done.8.refs_2_, bf16[2048,128]{1,0:T(8,128)(2,1)S(1)} %get-tuple-element.71.refs_1_.refs_2_.refs_3_, ...), custom_call_target="tpu_custom_call" | custom-call | flops 1000 | bytes 1000 | tf_op jit(solution)/shard_map/row_forward/pallas_call | solution.py:44
  51.6 2.2 %glob_backward.1 = (f32[1024,256]{1,0:T(8,128)S(1)}, f32[256,128]{1,0:T(8,128)S(1)}, f32[256,128]{1,0:T(8,128)S(1)}) custom-call(s32[4]{0:T(128)S(1)} %pad_add_fusion.refs_0_, bf16[2048,128]{1,0:T(8,128)(2,1)S(1)} %get-tuple-element.78.refs_1_, bf16[2048,128]{1,0:T(8,128)(2,1)S(1)} %get-tuple-element.98.refs_2_, ...), custom_call_target="tpu_custom_call" | custom-call | flops 1000 | bytes 1000 | tf_op jit(solution)/shard_map/glob_backward/pallas_call | solution.py:44
  53.8 3.1 %collective-permute-done.9.refs_7_.refs_4_ = bf16[144,256]{1,0:T(8,128)(2,1)S(1)} collective-permute-done((bf16[144,256]{1,0:T(8,128)(2,1)S(1)}, bf16[144,256]{1,0:T(8,128)(2,1)S(1)}, u32[]{:S(2)}, u32[]{:S(2)}) %collective-permute-start.9) | collective-permute-done | bytes 73760 | tf_op jit(solution)/shard_map/ppermute | solution.py:506
  56.9 2.2 %row_backward.1 = (f32[2048,128]{1,0:T(8,128)S(1)}, f32[2048,128]{1,0:T(8,128)S(1)}, bf16[768,128]{1,0:T(8,128)(2,1)S(1)}) custom-call(s32[4]{0:T(128)S(1)} %pad_add_fusion.refs_0_, bf16[512,128]{1,0:T(8,128)(2,1)S(1)} %get-tuple-element.92.refs_1_, bf16[512,128]{1,0:T(8,128)(2,1)S(1)} %collective-permute-done.8.refs_2_, ...), custom_call_target="tpu_custom_call" | custom-call | flops 1000 | bytes 1000 | tf_op jit(solution)/shard_map/row_backward/pallas_call | solution.py:44
  61.9 5.1 %collective-permute-start.11 = (bf16[512,128]{1,0:T(8,128)(2,1)S(1)}, bf16[512,128]{1,0:T(8,128)(2,1)S(1)}, u32[]{:S(2)}, u32[]{:S(2)}) collective-permute-start(bf16[512,128]{1,0:T(8,128)(2,1)S(1)} %get-tuple-element.106), channel_id=1, source_target_pairs={{0,8},{4,12},{8,0},{12,4},{16,24},{20,28},{24,16},{28,20},{1,9},{5... | collective-permute-start | bytes 393224 | tf_op jit(solution)/shard_map/ppermute | solution.py:480
  68.0 3.7 %backward_inner.1 = (f32[2048,128]{1,0:T(8,128)S(1)}, f32[2048,128]{1,0:T(8,128)S(1)}, bf16[2048,128]{1,0:T(8,128)(2,1)S(1)}) custom-call(s32[4]{0:T(128)S(1)} %pad_add_fusion.refs_0_, bf16[2048,128]{1,0:T(8,128)(2,1)S(1)} %get-tuple-element.78.refs_1_, ...), custom_call_target="tpu_custom_call", output_to_operand_aliasing={{0}: (9, {}), {1}: (10, {})} | custom-call | flops 1000 | bytes 1000 | tf_op jit(solution)/shard_map/backward_inner/pallas_call | solution.py:44
  73.4 1.9 %project.1 = (bf16[2,512,512]{2,1,0:T(8,128)(2,1)S(1)}, bf16[2,512,512]{2,1,0:T(8,128)(2,1)S(1)}) custom-call(s32[4]{0:T(128)S(1)} %pad_add_fusion.refs_0_, bf16[512,2048]{1,0:T(8,128)(2,1)S(1)} %copy-done, bf16[512,128]{1,0:T(8,128)(2,1)S(1)} %get-tuple-element.104.refs_11_.refs_2_, bf16[512,128]{1,0:T(8,128)(2,1)S(1)} %collective-permute-done.10.refs_3_, ...), custom_call_target="tpu_custom_call" | custom-call | flops 1000 | bytes 1000 | tf_op jit(solution)/shard_map/project/pallas_call | solution.py:44
  75.3 1.6 %collective-permute-start.17 = (bf16[1536,128]{1,0:T(8,128)(2,1)S(1)}, bf16[1536,128]{1,0:T(8,128)(2,1)S(1)}, u32[]{:S(2)}, u32[]{:S(2)}) collective-permute-start(bf16[1536,128]{1,0:T(8,128)(2,1)S(1)} %get-tuple-element.120), channel_id=1, source_target_pairs={{0,4},{4,0},{8,12},{12,8},{16,20},{20,16},{24,28},{28,24},{1,5},{5... | collective-permute-start | bytes 1179656 | tf_op jit(solution)/shard_map/ppermute | solution.py:480
  80.9 6.0 %collective-permute-done.17.refs_2_ = bf16[1536,128]{1,0:T(8,128)(2,1)S(1)} collective-permute-done((bf16[1536,128]{1,0:T(8,128)(2,1)S(1)}, bf16[1536,128]{1,0:T(8,128)(2,1)S(1)}, u32[]{:S(2)}, u32[]{:S(2)}) %collective-permute-start.17) | collective-permute-done | bytes 393248 | tf_op jit(solution)/shard_map/ppermute | solution.py:480
  86.9 2.0 %collective-permute-done.18.refs_3_ = bf16[1536,128]{1,0:T(8,128)(2,1)S(1)} collective-permute-done((bf16[1536,128]{1,0:T(8,128)(2,1)S(1)}, bf16[1536,128]{1,0:T(8,128)(2,1)S(1)}, u32[]{:S(2)}, u32[]{:S(2)}) %collective-permute-start.18) | collective-permute-done | bytes 393248 | tf_op jit(solution)/shard_map/ppermute | solution.py:480
  88.9 7.9 %collective-permute-done.19.refs_4_ = bf16[1536,128]{1,0:T(8,128)(2,1)S(1)} collective-permute-done((bf16[1536,128]{1,0:T(8,128)(2,1)S(1)}, bf16[1536,128]{1,0:T(8,128)(2,1)S(1)}, u32[]{:S(2)}, u32[]{:S(2)}) %collective-permute-start.19) | collective-permute-done | bytes 393248 | tf_op jit(solution)/shard_map/ppermute | solution.py:480
  96.8 1.9 %join_grads.1 = (bf16[512,512]{1,0:T(8,128)(2,1)}, bf16[512,512]{1,0:T(8,128)(2,1)}, bf16[512,512]{1,0:T(8,128)(2,1)}) custom-call(s32[4]{0:T(128)S(1)} %pad_add_fusion.refs_0_, bf16[1536,128]{1,0:T(8,128)(2,1)S(1)} %get-tuple-element.117.refs_6_.refs_1_, bf16[1536,128]{1,0:T(8,128)(2,1)S(1)} %collective-permute-done.17.refs_2_, ...), custom_call_target="tpu_custom_call" | custom-call | flops 13800000512 | bytes 1000 | tf_op jit(solution)/shard_map/join_grads/pallas_call | solution.py:44
  (49 shorter events, 20.3 us)
Async XLA Ops:
  2.7 13.4 %collective-permute-start.1 = (bf16[1024,128]{1,0:T(8,128)(2,1)S(1)}, bf16[1024,128]{1,0:T(8,128)(2,1)S(1)}, u32[]{:S(2)}, u32[]{:S(2)}) collective-permute-start(bf16[1024,128]{1,0:T(8,128)(2,1)S(1)} %get-tuple-element.68), channel_id=1, source_target_pairs={{0,4},{4,0},{8,12},{12,8},{16,20},{20,16},{24,28},{28,24},{1,5},{5... | collective-permute-start | bytes 786440 | tf_op jit(solution)/shard_map/ppermute | solution.py:480
  5.7 10.5 %collective-permute-start.2 = (bf16[1024,128]{1,0:T(8,128)(2,1)S(1)}, bf16[1024,128]{1,0:T(8,128)(2,1)S(1)}, u32[]{:S(2)}, u32[]{:S(2)}) collective-permute-start(bf16[1024,128]{1,0:T(8,128)(2,1)S(1)} %get-tuple-element.69), channel_id=1, source_target_pairs={{0,8},{4,12},{8,0},{12,4},{16,24},{20,28},{24,16},{28,20},{1,9},{5... | collective-permute-start | bytes 786440 | tf_op jit(solution)/shard_map/ppermute | solution.py:480
  7.3 12.8 %collective-permute-start.3 = (bf16[1024,128]{1,0:T(8,128)(2,1)S(1)}, bf16[1024,128]{1,0:T(8,128)(2,1)S(1)}, u32[]{:S(2)}, u32[]{:S(2)}) collective-permute-start(bf16[1024,128]{1,0:T(8,128)(2,1)S(1)} %get-tuple-element.70), channel_id=1, source_target_pairs={{0,12},{4,8},{8,4},{12,0},{16,28},{20,24},{24,20},{28,16},{1,13},{... | collective-permute-start | bytes 786440 | tf_op jit(solution)/shard_map/ppermute | solution.py:480
  8.0 8.1 %copy-start.3 = (s32[256]{0:T(256)S(1)}, s32[256]{0:T(256)}, u32[]{:S(2)}) copy-start(s32[256]{0:T(256)} %param.12) | copy-start | bytes 3076
  12.6 15.9 %collective-permute-start.4 = (bf16[1040,128]{1,0:T(8,128)(2,1)}, bf16[1040,128]{1,0:T(8,128)(2,1)S(1)}, u32[]{:S(2)}, u32[]{:S(2)}) collective-permute-start(bf16[1040,128]{1,0:T(8,128)(2,1)} %get-tuple-element.75), channel_id=1, source_target_pairs={{0,8},{4,12},{8,0},{12,4},{16,24},{20,28},{24,16},{28,20},{1,9},{5... | collective-permute-start | bytes 798728 | tf_op jit(solution)/shard_map/ppermute | solution.py:480
  14.5 16.7 %collective-permute-start = (bf16[1040,128]{1,0:T(8,128)(2,1)}, bf16[1040,128]{1,0:T(8,128)(2,1)S(1)}, u32[]{:S(2)}, u32[]{:S(2)}) collective-permute-start(bf16[1040,128]{1,0:T(8,128)(2,1)} %get-tuple-element.67), channel_id=1, source_target_pairs={{0,4},{4,0},{8,12},{12,8},{16,20},{20,16},{24,28},{28,24},{1,5},{5... | collective-permute-start | bytes 798728 | tf_op jit(solution)/shard_map/ppermute | solution.py:480
  16.1 15.2 %collective-permute-start.5 = (bf16[1040,128]{1,0:T(8,128)(2,1)}, bf16[1040,128]{1,0:T(8,128)(2,1)S(1)}, u32[]{:S(2)}, u32[]{:S(2)}) collective-permute-start(bf16[1040,128]{1,0:T(8,128)(2,1)} %get-tuple-element.77), channel_id=1, source_target_pairs={{0,12},{4,8},{8,4},{12,0},{16,28},{20,24},{24,20},{28,16},{1,13},{... | collective-permute-start | bytes 798728 | tf_op jit(solution)/shard_map/ppermute | solution.py:480
  20.0 0.7 copy-start.1
  20.7 0.9 copy-start.2
  22.6 18.9 %collective-permute-start.6 = (bf16[512,128]{1,0:T(8,128)(2,1)S(1)}, bf16[512,128]{1,0:T(8,128)(2,1)S(1)}, u32[]{:S(2)}, u32[]{:S(2)}) collective-permute-start(bf16[512,128]{1,0:T(8,128)(2,1)S(1)} %get-tuple-element.73.refs_3_.refs_7_), channel_id=1, source_target_pairs={{0,16},{4,20},{8,24},{12,28},{1,17},{5,21},{9,25},{13,29},{2,18},{... | collective-permute-start | bytes 393224 | tf_op jit(solution)/shard_map/ppermute | solution.py:495
  28.5 13.1 %collective-permute-start.7 = (bf16[768,128]{1,0:T(8,128)(2,1)S(1)}, bf16[768,128]{1,0:T(8,128)(2,1)S(1)}, u32[]{:S(2)}, u32[]{:S(2)}) collective-permute-start(bf16[768,128]{1,0:T(8,128)(2,1)S(1)} %get-tuple-element.83), channel_id=1, source_target_pairs={{0,16},{4,20},{8,24},{12,28},{1,17},{5,21},{9,25},{13,29},{2,18},{... | collective-permute-start | bytes 589832 | tf_op jit(solution)/shard_map/ppermute | solution.py:503
  32.3 15.9 %collective-permute-start.8 = (bf16[512,128]{1,0:T(8,128)(2,1)S(1)}, bf16[512,128]{1,0:T(8,128)(2,1)S(1)}, u32[]{:S(2)}, u32[]{:S(2)}) collective-permute-start(bf16[512,128]{1,0:T(8,128)(2,1)S(1)} %get-tuple-element.92.refs_1_), channel_id=1, source_target_pairs={{0,16},{4,20},{8,24},{12,28},{1,17},{5,21},{9,25},{13,29},{2,18},{... | collective-permute-start | bytes 393224 | tf_op jit(solution)/shard_map/ppermute | solution.py:495
  50.0 6.9 %collective-permute-start.9 = (bf16[144,256]{1,0:T(8,128)(2,1)S(1)}, bf16[144,256]{1,0:T(8,128)(2,1)S(1)}, u32[]{:S(2)}, u32[]{:S(2)}) collective-permute-start(bf16[144,256]{1,0:T(8,128)(2,1)S(1)} %row_forward.1.refs_6_.refs_3_), channel_id=1, source_target_pairs={{0,16},{4,20},{8,24},{12,28},{16,0},{20,4},{24,8},{28,12},{1,17},{... | collective-permute-start | bytes 221192 | tf_op jit(solution)/shard_map/ppermute | solution.py:506
  50.1 21.6 %collective-permute-start.13 = (bf16[768,128]{1,0:T(8,128)(2,1)S(1)}, bf16[768,128]{1,0:T(8,128)(2,1)S(1)}, u32[]{:S(2)}, u32[]{:S(2)}) collective-permute-start(bf16[768,128]{1,0:T(8,128)(2,1)S(1)} %get-tuple-element.97.refs_6_), channel_id=1, source_target_pairs={{16,0},{20,4},{24,8},{28,12},{17,1},{21,5},{25,9},{29,13},{18,2},{... | collective-permute-start | bytes 589832 | tf_op jit(solution)/shard_map/ppermute | solution.py:503
  59.1 12.6 %collective-permute-start.14 = (bf16[768,128]{1,0:T(8,128)(2,1)S(1)}, bf16[768,128]{1,0:T(8,128)(2,1)S(1)}, u32[]{:S(2)}, u32[]{:S(2)}) collective-permute-start(bf16[768,128]{1,0:T(8,128)(2,1)S(1)} %get-tuple-element.103.refs_5_.refs_8_), channel_id=1, source_target_pairs={{16,0},{20,4},{24,8},{28,12},{17,1},{21,5},{25,9},{29,13},{18,2},{... | collective-permute-start | bytes 589832 | tf_op jit(solution)/shard_map/ppermute | solution.py:692
  61.3 11.8 %collective-permute-start.10 = (bf16[512,128]{1,0:T(8,128)(2,1)S(1)}, bf16[512,128]{1,0:T(8,128)(2,1)S(1)}, u32[]{:S(2)}, u32[]{:S(2)}) collective-permute-start(bf16[512,128]{1,0:T(8,128)(2,1)S(1)} %get-tuple-element.105), channel_id=1, source_target_pairs={{0,4},{4,0},{8,12},{12,8},{16,20},{20,16},{24,28},{28,24},{1,5},{5... | collective-permute-start | bytes 393224 | tf_op jit(solution)/shard_map/ppermute | solution.py:480
  61.9 11.2 %collective-permute-start.11 = (bf16[512,128]{1,0:T(8,128)(2,1)S(1)}, bf16[512,128]{1,0:T(8,128)(2,1)S(1)}, u32[]{:S(2)}, u32[]{:S(2)}) collective-permute-start(bf16[512,128]{1,0:T(8,128)(2,1)S(1)} %get-tuple-element.106), channel_id=1, source_target_pairs={{0,8},{4,12},{8,0},{12,4},{16,24},{20,28},{24,16},{28,20},{1,9},{5... | collective-permute-start | bytes 393224 | tf_op jit(solution)/shard_map/ppermute | solution.py:480
  67.0 6.4 %collective-permute-start.12 = (bf16[512,128]{1,0:T(8,128)(2,1)S(1)}, bf16[512,128]{1,0:T(8,128)(2,1)S(1)}, u32[]{:S(2)}, u32[]{:S(2)}) collective-permute-start(bf16[512,128]{1,0:T(8,128)(2,1)S(1)} %get-tuple-element.107), channel_id=1, source_target_pairs={{0,12},{4,8},{8,4},{12,0},{16,28},{20,24},{24,20},{28,16},{1,13},{... | collective-permute-start | bytes 393224 | tf_op jit(solution)/shard_map/ppermute | solution.py:480
  71.7 1.7 %copy-start = (bf16[512,2048]{1,0:T(8,128)(2,1)S(1)}, bf16[512,2048]{1,0:T(8,128)(2,1)}, u32[]{:S(2)}) copy-start(bf16[512,2048]{1,0:T(8,128)(2,1)} %refs_1_.5) | copy-start | bytes 6291460
  75.3 3.7 %collective-permute-start.15 = (bf16[2,512,512]{2,1,0:T(8,128)(2,1)S(1)}, bf16[2,512,512]{2,1,0:T(8,128)(2,1)S(1)}, u32[]{:S(2)}, u32[]{:S(2)}) collective-permute-start(bf16[2,512,512]{2,1,0:T(8,128)(2,1)S(1)} %get-tuple-element.119), channel_id=1, source_target_pairs={{0,1},{1,0},{2,3},{3,2},{4,5},{5,4},{6,7},{7,6},{8,9},{9,8},{10,11... | collective-permute-start | bytes 3145736 | tf_op jit(solution)/shard_map/ppermute | solution.py:724
  75.3 11.5 %collective-permute-start.17 = (bf16[1536,128]{1,0:T(8,128)(2,1)S(1)}, bf16[1536,128]{1,0:T(8,128)(2,1)S(1)}, u32[]{:S(2)}, u32[]{:S(2)}) collective-permute-start(bf16[1536,128]{1,0:T(8,128)(2,1)S(1)} %get-tuple-element.120), channel_id=1, source_target_pairs={{0,4},{4,0},{8,12},{12,8},{16,20},{20,16},{24,28},{28,24},{1,5},{5... | collective-permute-start | bytes 1179656 | tf_op jit(solution)/shard_map/ppermute | solution.py:480
  76.9 12.0 %collective-permute-start.18 = (bf16[1536,128]{1,0:T(8,128)(2,1)S(1)}, bf16[1536,128]{1,0:T(8,128)(2,1)S(1)}, u32[]{:S(2)}, u32[]{:S(2)}) collective-permute-start(bf16[1536,128]{1,0:T(8,128)(2,1)S(1)} %get-tuple-element.121), channel_id=1, source_target_pairs={{0,8},{4,12},{8,0},{12,4},{16,24},{20,28},{24,16},{28,20},{1,9},{5... | collective-permute-start | bytes 1179656 | tf_op jit(solution)/shard_map/ppermute | solution.py:480
  78.0 18.8 %collective-permute-start.19 = (bf16[1536,128]{1,0:T(8,128)(2,1)S(1)}, bf16[1536,128]{1,0:T(8,128)(2,1)S(1)}, u32[]{:S(2)}, u32[]{:S(2)}) collective-permute-start(bf16[1536,128]{1,0:T(8,128)(2,1)S(1)} %get-tuple-element.122), channel_id=1, source_target_pairs={{0,12},{4,8},{8,4},{12,0},{16,28},{20,24},{24,20},{28,16},{1,13},{... | collective-permute-start | bytes 1179656 | tf_op jit(solution)/shard_map/ppermute | solution.py:480
  79.3 19.4 %collective-permute-start.16 = (bf16[512,512]{1,0:T(8,128)(2,1)S(1)}, bf16[512,512]{1,0:T(8,128)(2,1)S(1)}, u32[]{:S(2)}, u32[]{:S(2)}) collective-permute-start(bf16[512,512]{1,0:T(8,128)(2,1)S(1)} %fusion.2), channel_id=1, source_target_pairs={{0,2},{1,3},{2,0},{3,1},{4,6},{5,7},{6,4},{7,5},{8,10},{9,11},{10,... | collective-permute-start | bytes 1572872 | tf_op jit(solution)/shard_map/ppermute | solution.py:726
  (1 other events, 0.7 us)
